TPU v7x, 32 devices: a whole 2x2x4 slice. The times are simulated.
32 devices in a mesh: context: 8 (over z, y), tensor: 4 (over x, core).
Axes of the slice: x: 2, y: 2, z: 4, core: 2. Of those that a mesh axis runs over, the one named last changes fastest.
Arguments:
- layer_input: bfloat16 [4096, 1024], P('context', 'tensor'), may hold values from -6 to 6
- value_proj: bfloat16 [1024, 2048], P(None, 'tensor'), may hold values from -0.1875 to 0.1875
- conv_taps: float32 [4, 2048], P(None, 'tensor'), may hold values from -3 to 3
- conv_pre: bfloat16 [4096, 2048], P('context', 'tensor'), may hold values from -6 to 6
- state_in: bfloat16 [4096, 128], P('context'), may hold values from -6 to 6
- state_out: bfloat16 [4096, 128], P('context'), may hold values from -0.5 to 0.5
- step_size: float32 [32, 4096], P('tensor', 'context'), may hold values from 0 to 1
- log_decay: float32 [32, 4096], P('tensor', 'context'), may hold values from -2 to 0
- skip_gain: float32 [32], P('tensor'), may hold values from 0.5 to 2
- grad_out: bfloat16 [4096, 2048], P('context', 'tensor'), may hold values from -6 to 6
Outputs:
- grad_input: bfloat16 [4096, 1024], P('context', 'tensor')
- grad_value_proj: float32 [1024, 2048], P('context', 'tensor')
All inputs are finite; a program needn't handle non-finite values.
Results may differ from a plain program's by a relative error of at most 0.0059.
Values may be sent and summed in bfloat16 or wider, within the bound.
No kernel may reach another device: no remote copies, remote signals or barrier semaphores. Data moves between devices by JAX's collectives and lax.ppermute only.
A program may use at most 64 MiB of HBM per device.

v0:
```python
import math

import jax
import jax.numpy as jnp
from jax import lax
from jax.sharding import PartitionSpec as P

CONV = 4
BLOCK = 256


def prefix(part, axis, combine, identity):
    count = lax.axis_size(axis)
    place = lax.axis_index(axis)
    ahead = count - 1 - place
    gathered = jax.tree.map(lambda a: lax.all_gather(a, axis), part)
    state = jax.tree.map(lambda a, e: jnp.zeros_like(a) + jnp.asarray(e, a.dtype), part, identity)

    def one(hop, state):
        source = count - 1 - hop
        return combine(
            state, jax.tree.map(lambda a: lax.dynamic_index_in_dim(a, source, 0, False), gathered)
        )

    return lax.fori_loop(0, ahead, one, state)


def from_behind(value, axis, steps):
    count = lax.axis_size(axis)
    leading, last = (max(0, -steps), min(count, count - steps))
    return lax.ppermute(value, axis, [(source, source + steps) for source in range(leading, last)])


def silu_slope(values):
    sigmoid_value = jax.nn.sigmoid(values)
    return sigmoid_value * (1.0 + values * (1.0 - sigmoid_value))


def within_part(input_blk, output_blk, grad_blk, cumulative_blk):
    length = input_blk.shape[0]
    scores = lax.dot_general(
        input_blk, output_blk, (((1,), (1,)), ((), ())), preferred_element_type=jnp.float32
    )
    spread = cumulative_blk[:, None, :] - cumulative_blk[:, :, None]
    upper_mask = jnp.arange(length)[None, :] >= jnp.arange(length)[:, None]
    damping = jnp.where(upper_mask[None], jnp.exp(jnp.minimum(spread, 0.0)), 0.0)
    weights = (scores[None] * damping).astype(jnp.bfloat16)
    return jnp.einsum("hts,shp->thp", weights, grad_blk, preferred_element_type=jnp.float32)


def beyond_part(carried, input_blk, cumulative_blk):
    closing = cumulative_blk[:, -1:]
    beyond = jnp.einsum(
        "hpn,tn->thp", carried.astype(jnp.bfloat16), input_blk, preferred_element_type=jnp.float32
    )
    return beyond * jnp.exp(closing - cumulative_blk).T[:, :, None]


def carry_in(total_decay, local_state):

    def combine(earlier_part, later_part):
        return (
            later_part[0] + earlier_part[0],
            later_part[1] + jnp.exp(later_part[0])[:, None, None] * earlier_part[1],
        )

    identity = (jnp.zeros_like(total_decay), jnp.zeros_like(local_state))
    result = prefix((total_decay, local_state), "context", combine, identity)
    return result[1]


def local(
    layer_input,
    value_proj,
    conv_taps,
    conv_pre,
    state_in,
    state_out,
    step_size,
    log_decay,
    skip_gain,
    grad_out,
):
    gathered = lax.all_gather(layer_input, "tensor", axis=1, tiled=True)
    row_count, inner_width = grad_out.shape
    head_count = step_size.shape[0]
    head_width = inner_width // head_count
    state_width = state_in.shape[1]
    block_count = row_count // BLOCK
    input_blocks = state_in.reshape(block_count, BLOCK, state_width)
    output_blocks = state_out.reshape(block_count, BLOCK, state_width)
    grad_blocks = grad_out.reshape(block_count, BLOCK, head_count, head_width)
    step_blocks = step_size.reshape(head_count, block_count, BLOCK).transpose(1, 0, 2)
    running_total = jnp.cumsum(log_decay.reshape(head_count, block_count, BLOCK), axis=2).transpose(
        1, 0, 2
    )
    closings = running_total[:, :, -1]
    weighted = (
        grad_blocks.astype(jnp.float32) * jnp.exp(running_total).transpose(0, 2, 1)[:, :, :, None]
    ).astype(jnp.bfloat16)
    block_states = jnp.einsum(
        "kshp,ksn->khpn", weighted, output_blocks, preferred_element_type=jnp.float32
    )
    before = jnp.cumsum(closings, axis=0) - closings
    local_state = jnp.sum(jnp.exp(before)[:, :, None, None] * block_states, axis=0)
    incoming = carry_in(jnp.sum(closings, axis=0), local_state)

    def whole_increment(carried, pieces):
        input_blk, output_blk, grad_blk, step_blk, cumulative_blk, state_blk = pieces
        within = within_part(input_blk, output_blk, grad_blk, cumulative_blk)
        beyond = beyond_part(carried, input_blk, cumulative_blk)
        grad_block = step_blk.T[:, :, None] * (within + beyond) + skip_gain[
            None, :, None
        ] * grad_blk.astype(jnp.float32)
        carried = jnp.exp(cumulative_blk[:, -1])[:, None, None] * carried + state_blk
        return (carried, grad_block)

    block_inputs = (
        input_blocks,
        output_blocks,
        grad_blocks,
        step_blocks,
        running_total,
        block_states,
    )
    grad_x = lax.scan(whole_increment, incoming, block_inputs, reverse=True)[1].reshape(
        row_count, inner_width
    )
    grad_conv = (grad_x * silu_slope(conv_pre.astype(jnp.float32))).astype(jnp.bfloat16)
    subsequent = from_behind(grad_conv[: CONV - 1], "context", -1)
    extended = jnp.concatenate([grad_conv, subsequent], axis=0).astype(jnp.float32)
    summed = jnp.zeros((row_count, inner_width), jnp.float32)
    for offset in range(CONV):
        start_row = CONV - 1 - offset
        summed = summed + conv_taps[offset][None, :] * extended[start_row : start_row + row_count]
    grad_proj = summed.astype(jnp.bfloat16)
    context_count = lax.axis_size("context")
    scaling = 1.0 / math.sqrt(row_count * context_count)
    product = lax.dot_general(
        gathered, grad_proj, (((0,), (0,)), ((), ())), preferred_element_type=jnp.float32
    )
    grad_value_proj = lax.psum_scatter(
        product * scaling, "context", scatter_dimension=0, tiled=True
    )
    partial_input = lax.dot_general(
        grad_proj, value_proj, (((1,), (1,)), ((), ())), preferred_element_type=jnp.float32
    )
    grad_input = lax.psum_scatter(partial_input, "tensor", scatter_dimension=1, tiled=True).astype(
        jnp.bfloat16
    )
    return (grad_input, grad_value_proj)


def solution(mesh):
    return jax.shard_map(
        local,
        mesh=mesh,
        in_specs=(
            P("context", "tensor"),
            P(None, "tensor"),
            P(None, "tensor"),
            P("context", "tensor"),
            P("context", None),
            P("context", None),
            P("tensor", "context"),
            P("tensor", "context"),
            P("tensor"),
            P("context", "tensor"),
        ),
        out_specs=(P("context", "tensor"), P("context", "tensor")),
        check_vma=False,
    )
```

profile of v0, /device:TPU:0, one launch (start us, length us, event | category | flops | bytes accessed | tf_op | source)
XLA Modules:
  0.0 218.6 jit_solution(7906484307017823651)
XLA Ops:
  8.0 1.1 reduce-window.6
  9.8 1.3 copy.57
  11.6 1.9 multiply_reduce_fusion
  16.8 23.1 %all-reduce = f32[64]{0:T(128)S(1)} all-reduce(f32[64]{0:T(128)S(1)} %dynamic-update-slice), channel_id=3, replica_groups=mesh['context'=8,'tensor'=4] {'context'}, use_global_device_ids=true, to_apply=%add | all-reduce | flops 64 | bytes 512
  41.0 24.9 %all-gather.7.cloned.1.call-done = f32[64,64,128]{2,1,0:T(8,128)} async-done(((f32[8,64,128]{2,1,0:T(8,128)}), f32[64,64,128]{2,1,0:T(8,128)}) %all-gather.7.cloned.1.call-update) | async-done | bytes 2097168 | tf_op jit(solution)/shard_map/all_gather | solution.py:16
  65.9 7.8 %while.30 = (s32[]{:T(128)}, f32[8,64,128]{2,1,0:T(8,128)S(1)}, s32[]{:T(128)}, f32[8,8,64,128]{3,2,1,0:T(8,128)}, f32[8,8]{1,0:T(8,128)S(1)}, /*index=5*/s32[]{:T(128)}, s32[]{:T(128)}, s32[]{:T(128)}, s32[]{:T(128)}) while((s32[]{:T(128)}, f32[8,64,128]{2,1,0:T(8,128)S(1)}, s32[]{:T(128)}, f32[8,8,64,128]{3,2,1,0:T(8,128)}, ...), condition=%wide.region_6.7_spmd, body=%wide.region_5.6_spmd.sunk | while | flops 131078 | bytes 786683 | solution.py:25
  65.9 1.1 bitcast_add_fusion.4
  68.2 1.1 bitcast_add_fusion.4
  71.5 1.1 bitcast_add_fusion.4
  72.6 1.1 bitcast_add_fusion.4
  73.9 23.4 %while.31 = (s32[]{:T(128)}, f32[8,64,128]{2,1,0:T(8,128)S(1)}, f32[2,256,8,64]{1,0,3,2:T(2,128)S(1)}, f32[2,8,256]{2,1,0:T(8,128)S(1)}, f32[2,8,64,128]{3,2,1,0...) while((s32[]{:T(128)}, f32[8,64,128]{2,1,0:T(8,128)S(1)}, ...), condition=%wide.region_8.9_spmd, body=%wide.region_7.8_spmd.sunk | while | flops 121112576 | bytes 8325533 | solution.py:126
  76.4 1.4 fusion.63
  78.3 7.3 %dynamic_update_slice.11 = f32[2,256,8,64]{1,0,3,2:T(2,128)S(1)} dynamic-update-slice(f32[2,256,8,64]{1,0,3,2:T(2,128)S(1)} %get-tuple-element.496, f32[1,256,8,64]{1,0,3,2:T(1,128)S(1)} %copy.88, s32[]{:T(128)S(6)} %sub.113, s32[]{:T(128)} %constant.103.clone.1..sunk.1, s32[]{:T(128)} %constant.103.clone.1..sunk.1, s32[]{:T(128)} %constant.103.clone.1..sunk.1) | dynamic-update-slice | bytes 1048580 | tf_op jit(solution)/shard_map/while/body/jit(dynamic_update_index_in_dim)/dynamic_update_slice | solution.py:126
  88.1 1.4 fusion.63
  90.0 7.3 %dynamic_update_slice.11 = f32[2,256,8,64]{1,0,3,2:T(2,128)S(1)} dynamic-update-slice(f32[2,256,8,64]{1,0,3,2:T(2,128)S(1)} %get-tuple-element.496, f32[1,256,8,64]{1,0,3,2:T(1,128)S(1)} %copy.88, s32[]{:T(128)S(6)} %sub.113, s32[]{:T(128)} %constant.103.clone.1..sunk.1, s32[]{:T(128)} %constant.103.clone.1..sunk.1, s32[]{:T(128)} %constant.103.clone.1..sunk.1) | dynamic-update-slice | bytes 1048580 | tf_op jit(solution)/shard_map/while/body/jit(dynamic_update_index_in_dim)/dynamic_update_slice | solution.py:126
  98.8 1.3 collective-permute-start
  100.1 5.5 %collective-permute-done = bf16[3,512]{0,1:T(8,128)(2,1)S(1)} collective-permute-done((bf16[3,512]{0,1:T(8,128)(2,1)S(1)}, bf16[3,512]{0,1:T(8,128)(2,1)S(1)}, u32[]{:S(2)}, u32[]{:S(2)}) %collective-permute-start) | collective-permute-done | bytes 3104 | tf_op jit(solution)/shard_map/ppermute | solution.py:31
  105.8 1.3 fusion.32
  107.1 2.1 fusion.39
  109.3 3.2 %multiply_bitcast_fusion = f32[1024,512]{0,1:T(8,128)} fusion(bf16[512,512]{0,1:T(8,128)(2,1)S(1)} %fusion.32, bf16[512,1024]{1,0:T(8,128)(2,1)} %all-gather.5.cloned.1.call-done), kind=kOutput, calls=%fused_computation.35 | convolution fusion | flops 537395200 | bytes 3670016 | tf_op jit(solution)/shard_map/dot_general | solution.py:139
  112.5 25.5 %reduce-scatter.3.cloned.1.call-done = f32[512,256]{1,0:T(8,128)} async-done(((f32[512,1024]{1,0:T(8,128)}), f32[512,256]{1,0:T(8,128)}) %reduce-scatter.3.cloned.1.call-update) | async-done | bytes 524304 | tf_op jit(solution)/shard_map/reduce_scatter | solution.py:148
  138.0 1.8 convert_element_type.54
  139.8 70.5 %reduce-scatter.5.cloned.1.call-done = f32[128,512]{0,1:T(8,128)} async-done(((f32[1024,512]{0,1:T(8,128)}), f32[128,512]{0,1:T(8,128)}) %reduce-scatter.5.cloned.1.call-update) | async-done | bytes 262160 | tf_op jit(solution)/shard_map/reduce_scatter | solution.py:142
  210.3 1.8 copy.64
  (88 shorter events, 16.6 us)
Async XLA Ops:
  7.2 99.9 %copy-start = (bf16[1024,512]{1,0:T(8,128)(2,1)S(1)}, bf16[1024,512]{1,0:T(8,128)(2,1)}, u32[]{:S(2)}) copy-start(bf16[1024,512]{1,0:T(8,128)(2,1)} %param.15) | copy-start | bytes 3145732
  7.2 58.7 %all-gather.7.cloned.1.call-start = ((), (), s32[]{:S(2)}) async-start(), calls=%async_computation.5 | async-start | bytes 2359296 | tf_op jit(solution)/shard_map/all_gather | solution.py:16
  11.2 4.1 %copy-start.6 = (u32[32]{0:T(128)S(1)}, u32[32]{0:T(128)}, u32[]{:S(2)}) copy-start(u32[32]{0:T(128)} %constant.112) | copy-start | bytes 388
  11.2 28.8 %copy-start.3 = (bf16[512,512]{1,0:T(8,128)(2,1)S(1)}, bf16[512,512]{1,0:T(8,128)(2,1)}, u32[]{:S(2)}) copy-start(bf16[512,512]{1,0:T(8,128)(2,1)} %param.17) | copy-start | bytes 1572868
  13.6 95.7 %all-gather.5.cloned.1.call-start = ((), (), s32[]{:S(2)}) async-start(), calls=%async_computation.3 | async-start | bytes 1310720 | tf_op jit(solution)/shard_map/all_gather | solution.py:84
  14.3 123.7 %reduce-scatter.3.cloned.1.call-start = ((), (), s32[]{:S(2)}) async-start(), calls=%async_computation.2 | async-start | bytes 2621440 | tf_op jit(solution)/shard_map/reduce_scatter | solution.py:148
  65.9 8.1 %copy-start.1 = (bf16[512,128]{1,0:T(8,128)(2,1)S(1)}, bf16[512,128]{1,0:T(8,128)(2,1)}, u32[]{:S(2)}) copy-start(bf16[512,128]{1,0:T(8,128)(2,1)} %param.18) | copy-start | bytes 393220
  74.2 2.2 copy-start.4
  85.9 2.2 copy-start.4
  97.3 1.0 copy-start.2
  97.3 2.8 %copy-start.5 = (f32[4,512]{1,0:T(4,128)S(1)}, f32[4,512]{1,0:T(4,128)}, u32[]{:S(2)}) copy-start(f32[4,512]{1,0:T(4,128)} %param.16) | copy-start | bytes 24580
  98.8 6.9 %collective-permute-start = (bf16[3,512]{0,1:T(8,128)(2,1)S(1)}, bf16[3,512]{0,1:T(8,128)(2,1)S(1)}, u32[]{:S(2)}, u32[]{:S(2)}) collective-permute-start(bf16[3,512]{0,1:T(8,128)(2,1)S(1)} %slice.62), channel_id=1, source_target_pairs={{4,0},{8,4},{12,8},{16,12},{20,16},{24,20},{28,24},{5,1},{9,5},{13... | collective-permute-start | bytes 9224 | tf_op jit(solution)/shard_map/ppermute | solution.py:31
  109.2 101.1 %reduce-scatter.5.cloned.1.call-start = ((), (), s32[]{:S(2)}) async-start(), calls=%async_computation.4 | async-start | bytes 2359296 | tf_op jit(solution)/shard_map/reduce_scatter | solution.py:142
Sparse Core Ops, SparseCore 0:
  13.7 52.0 all-gather.6
  67.4 15.3 all-gather.4
  109.3 28.6 reduce-scatter.2
  141.8 68.3 reduce-scatter.4
where the time goes:
time: 219 us
  waiting for transfers between devices  127 us (58%)
  local copies, waits for them, and re-layouts  25.9 us (12%)
  blocking collectives  23.1 us (11%)
  between operations  14.6 us (7%)
  other arithmetic  13.3 us (6%)
  matrix products  12.6 us (6%)
    reduce_scatter x1, waiting for transfers between devices, local(): lax.psum_scatter(product * scaling, 'context', scatter_dimension=0, tiled...  70.5 us
    reduce_scatter x1, waiting for transfers between devices, local(): lax.psum_scatter(partial_input, 'tensor', scatter_dimension=1, tiled=True)  25.5 us
    all_gather x1, waiting for transfers between devices, prefix(): gathered = jax.tree.map(lambda a: lax.all_gather(a, axis), part)  24.9 us
    unnamed x1, blocking collectives  23.1 us
    dynamic_update_slice x4, local copies, waits for them, and re-layouts, local(): lax.scan(whole_increment, incoming, block_inputs, reverse=True)[1]  15.7 us
    add x7, other arithmetic, combine(): later_part[1] + jnp.exp(later_part[0])[:, None, None] * earlier_part[1]  7.46 us
    unnamed x19, local copies, waits for them, and re-layouts  5.97 us
    ppermute x1, waiting for transfers between devices, from_behind(): lax.ppermute(value, axis, [(source, source + steps) for source in range(l...  5.53 us
  transfers between devices with their start and end apart: 5, of which 4 were waited for; matrix products, arithmetic and copies ran while one was open for 20% of the time, Pallas kernels for 0%

commit v1 on v0

v1 whole, which is shorter than its diff:
```python
import functools
import math

import jax
import jax.numpy as jnp
from jax import lax
from jax.experimental import pallas as pl
from jax.experimental.pallas import tpu as pltpu
from jax.sharding import PartitionSpec as P

CONV = 4
BLOCK = 256
PAD = 16
ROW = 8
F32 = jnp.float32
BF16 = jnp.bfloat16
MIB = 1024 * 1024


def call(body, out_shapes, operands, scalars=0, hbm=0, idle=0, scratch=(), flops=0, moved=0, vmem=8):
    blocks = len(operands) - scalars - hbm - idle
    in_specs = [pl.BlockSpec(memory_space=pltpu.SMEM)] * scalars
    in_specs += [pl.BlockSpec(memory_space=pltpu.VMEM)] * blocks
    in_specs += [pl.BlockSpec(memory_space=pltpu.HBM)] * hbm
    in_specs += [pl.BlockSpec(memory_space=pl.ANY)] * idle
    kept = len(operands) - idle

    def run(*refs):
        body(*refs[:kept], *refs[len(operands) :])

    operands = list(operands)
    for index in range(scalars + blocks, scalars + blocks + hbm):
        operands[index] = pltpu.with_memory_space_constraint(operands[index], pltpu.HBM)
    return pl.pallas_call(
        run,
        out_shape=[jax.ShapeDtypeStruct(shape, kind) for shape, kind in out_shapes],
        in_specs=in_specs,
        out_specs=[pl.BlockSpec(memory_space=pltpu.VMEM)] * len(out_shapes),
        scratch_shapes=list(scratch),
        compiler_params=pltpu.CompilerParams(vmem_limit_bytes=vmem * MIB),
        cost_estimate=pl.CostEstimate(flops=flops, bytes_accessed=moved, transcendentals=0),
    )(*operands)


def radices(count, largest):
    found = []
    while count > 1:
        radix = next(r for r in range(min(largest, count), count + 1) if count % r == 0)
        found.append(radix)
        count //= radix
    return found


def partner(digit, radix, hop):
    if radix & (radix - 1) == 0:
        return digit ^ hop
    return (digit + hop) % radix


def origin(digit, radix, hop):
    if radix & (radix - 1) == 0:
        return digit ^ hop
    return (digit + radix - hop) % radix


def swap(value, axis, stride, radix, hop, back=False):
    count = lax.axis_size(axis)
    pairs = []
    for source in range(count):
        digit = source // stride % radix
        target = source + (partner(digit, radix, hop) - digit) * stride
        if not back or target < source:
            pairs.append((source, target))
    return lax.ppermute(value, axis, pairs)


def dot(a, b, contract):
    return lax.dot_general(a, b, ((contract[:1], contract[1:]), ((), ())), preferred_element_type=F32)


def spread_heads(heads, width):
    lane = lax.broadcasted_iota(jnp.int32, (heads, width), 1)
    head = lax.broadcasted_iota(jnp.int32, (heads, width), 0)
    return (lane // (width // heads) == head).astype(F32)


def spread_scalars(ref, heads, width):
    head = lax.broadcasted_iota(jnp.int32, (1, width), 1) // (width // heads)
    wide = jnp.zeros((1, width), F32)
    for index in range(heads):
        wide = jnp.where(head == index, ref[index], wide)
    return wide


def widen(per_head, spreader):
    high = per_head.astype(BF16).astype(F32)
    parts = jnp.concatenate([high, per_head - high], axis=0).astype(BF16)
    twice = jnp.concatenate([spreader, spreader], axis=0).astype(BF16)
    return dot(parts, twice, (0, 0))


def split(values):
    high = values.astype(BF16).astype(F32)
    middle = (values - high).astype(BF16).astype(F32)
    return high, middle, values - high - middle


def running(decay_blk):
    heads, length = decay_blk.shape
    row = lax.broadcasted_iota(jnp.int32, (length, length), 0)
    column = lax.broadcasted_iota(jnp.int32, (length, length), 1)
    parts = jnp.concatenate(split(decay_blk), axis=0).astype(BF16)
    sums = dot(parts, (row <= column).astype(F32).astype(BF16), (1, 0))
    return sums[:heads] + (sums[heads : 2 * heads] + sums[2 * heads :])


def pack_state(ref, state, decay_row):
    rows = state.shape[0]
    ref[:rows, :] = state.astype(BF16)
    high, middle, low = split(decay_row)
    place = lax.broadcasted_iota(jnp.int32, (PAD, decay_row.shape[1]), 0)
    packed = jnp.where(place == 0, high, jnp.where(place == 1, middle, jnp.where(place == 2, low, 0.0)))
    ref[rows:, :] = packed.astype(BF16)


def unpack_state(ref):
    rows = ref.shape[0] - PAD
    return ref[:rows, :].astype(F32), jnp.sum(ref[rows:, :].astype(F32), axis=0, keepdims=True)


def later_sum(digit, places, states, decays):
    total = None
    span = jnp.zeros_like(decays[0])
    for index, place in enumerate(places):
        between = jnp.zeros_like(decays[0])
        for other, other_place in enumerate(places):
            if other != index:
                inside = jnp.logical_and(other_place > digit, other_place < place)
                between = between + jnp.where(inside, decays[other], 0.0)
        weight = jnp.where(place > digit, jnp.exp(between), 0.0)
        total = weight * states[index] if total is None else total + weight * states[index]
        span = span + jnp.where(place > digit, decays[index], 0.0)
    return total, span


def state_body(heads, others, grad_hbm, output_hbm, decay_hbm, *refs):
    rest, refs = refs[:others], refs[others:]
    payload_ref, states_ref, grad_ref, output_ref, decay_ref = refs[:5]
    rest_out, sems = refs[5:-1], refs[-1]
    pairs = [(grad_hbm, grad_ref), (output_hbm, output_ref), (decay_hbm, decay_ref), *zip(rest, rest_out)]
    copies = [pltpu.make_async_copy(a, b, sems.at[index]) for index, (a, b) in enumerate(pairs)]
    firsts, later = copies[:3], copies[3:]
    for copy in firsts + later:
        copy.start()
    for copy in firsts:
        copy.wait()
    width = grad_ref.shape[1]
    count = grad_ref.shape[0] // BLOCK
    spreader = spread_heads(heads, width)
    states, spans = [], []
    for k in range(count):
        rows = slice(k * BLOCK, (k + 1) * BLOCK)
        cumulative = running(decay_ref[:, rows])
        spans.append(jnp.sum(spreader * cumulative[:, BLOCK - 1 :], axis=0, keepdims=True))
        weighted = (grad_ref[rows, :].astype(F32) * widen(jnp.exp(cumulative), spreader)).astype(BF16)
        states.append(dot(output_ref[rows, :], weighted, (0, 0)))
    total, span = states[-1], spans[-1]
    for k in reversed(range(count - 1)):
        total = states[k] + jnp.exp(spans[k]) * total
        span = span + spans[k]
    pack_state(payload_ref, total, span)
    for k in range(count):
        keep_state(states_ref.at[k], states[k], spans[k])
    for copy in later:
        copy.wait()


def keep_state(ref, state, span):
    rows = state.shape[0]
    ref[:rows, :] = state
    ref[rows:, :] = jnp.broadcast_to(span, (ROW, span.shape[1]))


def kept_state(ref):
    rows = ref.shape[0] - ROW
    return ref[:rows, :], ref[rows : rows + 1, :]


def merge_body(radix, stride, first, payload_ref, *refs):
    received = refs[: radix - 1]
    next_ref, held_out = refs[-2:]
    digit = lax.axis_index("context") // stride % radix
    pairs = [unpack_state(ref) for ref in (payload_ref, *received)]
    states, decays = [a for a, _ in pairs], [b for _, b in pairs]
    places = [origin(digit, radix, hop) for hop in range(radix)]
    whole, whole_span = later_sum(-1, places, states, decays)
    pack_state(next_ref, whole, whole_span)
    later, span = later_sum(digit, places[1:], states[1:], decays[1:])
    if not first:
        held, reach = kept_state(refs[radix - 1])
        later = held + jnp.exp(reach) * later
        span = reach + span
    keep_state(held_out, later, span)


def within_body(heads, skip_ref, *refs):
    input_ref, output_ref, grad_ref, step_ref, decay_ref, pre_ref, base_ref, coef_ref = refs
    for k in range(grad_ref.shape[0] // BLOCK):
        rows = slice(k * BLOCK, (k + 1) * BLOCK)
        within_block(
            heads,
            skip_ref,
            *(ref.at[rows, :] for ref in (input_ref, output_ref, grad_ref)),
            *(ref.at[:, rows] for ref in (step_ref, decay_ref)),
            *(ref.at[rows, :] for ref in (pre_ref, base_ref, coef_ref)),
        )


def within_block(heads, skip_ref, input_ref, output_ref, grad_ref, step_ref, decay_ref, pre_ref, base_ref, coef_ref):
    width = grad_ref.shape[1]
    head_width = width // heads
    group = max(1, 128 // head_width)
    half = BLOCK // 2
    spreader = spread_heads(heads, width)
    cumulative = running(decay_ref[...])
    across = cumulative.T
    scores = dot(input_ref[...], output_ref[...], (1, 1))
    step = step_ref[...]
    step_wide = widen(step, spreader)
    reach_wide = widen(step * jnp.exp(cumulative[:, BLOCK - 1 :] - cumulative), spreader)
    skip_wide = spread_scalars(skip_ref, heads, width)
    row = lax.broadcasted_iota(jnp.int32, (half, half), 0)
    column = lax.broadcasted_iota(jnp.int32, (half, half), 1)
    keep = column >= row
    lane = lax.broadcasted_iota(jnp.int32, (half, group * head_width), 1) // head_width

    def weigh(head, rows, columns, diagonal):
        spread = cumulative[head : head + 1, columns] - across[rows, head : head + 1]
        if diagonal:
            spread = jnp.where(keep, spread, -jnp.inf)
        return (scores[rows, columns] * jnp.exp(spread)).astype(BF16)

    first, second = slice(0, half), slice(half, BLOCK)
    for start in range(0, heads, group):
        channels = slice(start * head_width, (start + group) * head_width)
        grads = grad_ref[:, channels]
        upper = lower = None
        for member in range(group):
            head = start + member
            top = jnp.concatenate([weigh(head, first, first, True), weigh(head, first, second, False)], axis=1)
            one = dot(top, grads, (1, 0))
            two = dot(weigh(head, second, second, True), grads[half:, :], (1, 0))
            upper = one if upper is None else jnp.where(lane == member, one, upper)
            lower = two if lower is None else jnp.where(lane == member, two, lower)
        for rows, product in ((first, upper), (second, lower)):
            pre = pre_ref[rows, channels].astype(F32)
            gate = 1.0 / (1.0 + jnp.exp(-pre))
            slope = gate * (1.0 + pre * (1.0 - gate))
            direct = step_wide[rows, channels] * product + skip_wide[:, channels] * grads[rows, :].astype(F32)
            base_ref[rows, channels] = slope * direct
            coef_ref[rows, channels] = slope * reach_wide[rows, channels]


def turn_body(members, *refs):
    pieces, turned, ends_ref = refs[:members], refs[members : 2 * members], refs[-1]
    for hop in range(members):
        ends_ref[hop] = pieces[hop][pieces[hop].shape[0] - PAD :, :]
    for hop in range(members):
        turned[hop][...] = pieces[hop][...].T


def tail_body(radix, stride, first, members, chunk, *refs):
    received, refs = refs[: radix - 1], refs[radix - 1 :]
    if not first:
        held_ref, refs = refs[0], refs[1:]
    states_ref, base_ref, coef_ref, input_ref, taps_ref, ends_ref = refs[:6]
    layer_refs = refs[6 : 6 + members]
    keep_near, send_near, keep_far, send_far, grads_ref, conv_ref = refs[6 + members :]
    length, width = base_ref.shape
    place = lax.axis_index("context")
    digit = place // stride % radix
    pairs = [unpack_state(ref) for ref in received]
    places = [origin(digit, radix, hop) for hop in range(1, radix)]
    carry, _ = later_sum(digit, places, [a for a, _ in pairs], [b for _, b in pairs])
    if not first:
        held, reach = kept_state(held_ref)
        carry = held + jnp.exp(reach) * carry
    conv_ref[:PAD, :] = jnp.zeros((PAD, width), F32)
    conv_ref[PAD + length :, :] = jnp.zeros((PAD, width), F32)
    for k in reversed(range(length // BLOCK)):
        rows = slice(k * BLOCK, (k + 1) * BLOCK)
        product = dot(input_ref[rows, :], carry.astype(BF16), (1, 0))
        value = base_ref[rows, :] + coef_ref[rows, :] * product
        conv_ref[PAD + k * BLOCK : PAD + (k + 1) * BLOCK, :] = value.astype(BF16).astype(F32)
        if k:
            state, span = kept_state(states_ref.at[k])
            carry = state + jnp.exp(span) * carry
    total = None
    for offset in range(CONV):
        shift = CONV - 1 - offset
        term = taps_ref[offset : offset + 1, :] * conv_ref[shift : shift + PAD + length, :]
        total = term if total is None else total + term
    grads_ref[...] = total.astype(BF16)
    features = layer_refs[0].shape[0]
    per_piece = features // chunk
    me = lax.axis_index("tensor")
    half = width // 2

    def put(keep, send, same, index, value):
        @pl.when(same)
        def _():
            keep[index] = value

        @pl.when(jnp.logical_not(same))
        def _():
            send[index] = value.astype(BF16)

    for hop in range(members):
        source = origin(me, members, hop)
        product = dot(layer_refs[hop][...], grads_ref[PAD:, :], (1, 0)) + dot(ends_ref[hop], grads_ref[:PAD, :], (0, 0))
        for index in range(per_piece):
            number = source * per_piece + index
            rows = product[index * chunk : (index + 1) * chunk, :]
            put(keep_near, send_near, (number & 1) == (place & 1), number >> 1, rows[:, :half])
            put(keep_far, send_far, (number & 2) == (place & 2), (number & 1) + ((number >> 2) << 1), rows[:, half:])


def overlaps(index, high, sizes):
    start, found = 0, []
    for part, size in enumerate(sizes):
        first, last = max(start, index * high), min(start + size, (index + 1) * high)
        if first < last:
            found.append((part, slice(first - start, last - start), slice(first - index * high, last - index * high)))
        start += size
    return found


def share_body(members, sizes, grads_ref, proj_ref, *refs):
    keep_refs, send_refs = refs[: members // 2], refs[members // 2 :]
    high, features = keep_refs[0].shape
    for hop in range(members):
        goal = lax.axis_index("tensor") ^ hop
        block = proj_ref[pl.ds(pl.multiple_of(goal * features, features), features), :]
        share = dot(grads_ref[...], block, (1, 1))
        if hop % 2:
            for part, there, here in overlaps(hop // 2, high, sizes):
                send_refs[part][there, :] = share[here, :].astype(BF16)
        else:
            keep_refs[hop // 2][...] = share


def share_sum_body(count, sizes, *refs):
    keeps, arrivals, outs = refs[:count], refs[count : count + len(sizes)], refs[count + len(sizes) :]
    for index in range(count):
        out = outs[index // 2 + index % 2 * (count // 2)]
        for part, there, here in overlaps(index, out.shape[0], sizes):
            out[here, :] = (keeps[index][here, :] + arrivals[part][there, :].astype(F32)).astype(out.dtype)


def settle_body(share_ref, arrived_ref, head_ref, own_ref):
    head_ref[...] = share_ref[:PAD, :] + arrived_ref[:PAD, :].astype(F32)
    own_ref[...] = share_ref[PAD:, :] + arrived_ref[PAD:, :].astype(F32)


def end_body(scaling, keep_ref, got_ref, own_ref, ahead_ref, proj_out, input_out):
    proj_out[...] = (keep_ref[0] + got_ref[0].astype(F32)) * scaling
    rest = own_ref.shape[0] - PAD
    input_out[:rest, :] = own_ref[:rest, :].astype(BF16)
    input_out[rest:, :] = (own_ref[rest:, :] + ahead_ref[...]).astype(BF16)


def halve(bit, keep_ref, received_ref, keep_out, send_out):
    for index in range(keep_out.shape[0]):
        mine, other = 2 * index + bit, 2 * index + 1 - bit
        keep_out[index] = keep_ref[mine] + received_ref[mine].astype(F32)
        send_out[index] = (keep_ref[other] + received_ref[other].astype(F32)).astype(BF16)


def bit_of_place(shift):
    return (lax.axis_index("context") >> shift) & 1


def halve_body(shift, keep_ref, received_ref, keep_out, send_out):
    halve(bit_of_place(shift), keep_ref, received_ref, keep_out, send_out)


def halve_both_body(keep_near, got_near, keep_far, got_far, near_out, near_send, far_out, far_send):
    halve(bit_of_place(1), keep_near, got_near, near_out, near_send)
    halve(bit_of_place(0), keep_far, got_far, far_out, far_send)


def join_body(keep_near, got_near, keep_far, got_far, keep_out, send_out):
    bit = bit_of_place(2)
    half = keep_near.shape[2]
    halve(bit, keep_near, got_near, keep_out.at[:, :, :half], send_out.at[:, :, :half])
    halve(bit, keep_far, got_far, keep_out.at[:, :, half:], send_out.at[:, :, half:])


def local(
    layer_input,
    value_proj,
    conv_taps,
    conv_pre,
    state_in,
    state_out,
    step_size,
    log_decay,
    skip_gain,
    grad_out,
):
    length, width = grad_out.shape
    heads = step_size.shape[0]
    state_width = state_in.shape[1]
    count = length // BLOCK
    features = layer_input.shape[1]
    spans_of = lax.axis_size("context")
    members = lax.axis_size("tensor")

    layers = [layer_input]
    stride = members // 2
    while stride:
        layers += [swap(layer, "tensor", stride, 2, 1) for layer in layers]
        stride //= 2
    bits = members.bit_length() - 1
    layers = [layers[int(format(hop, f"0{bits}b")[::-1], 2)] for hop in range(members)]

    fetched = [grad_out, state_out, log_decay, state_in, step_size, conv_pre, conv_taps]
    payload, states, grad_here, output_here, decay_here, input_here, step_here, pre_here, taps_here = call(
        functools.partial(state_body, heads, len(fetched) - 3),
        [((state_width + PAD, width), BF16), ((count, state_width + ROW, width), F32)]
        + [(a.shape, a.dtype) for a in fetched],
        fetched,
        hbm=len(fetched),
        scratch=[pltpu.SemaphoreType.DMA((len(fetched),))],
        flops=2 * length * width * state_width,
        moved=2 * length * width,
        vmem=12,
    )

    base, coef = call(
        functools.partial(within_body, heads),
        [((length, width), F32), ((length, width), F32)],
        [skip_gain, input_here, output_here, grad_here, step_here, decay_here, pre_here],
        scalars=1,
        flops=64 * length * width * BLOCK * 8,
        moved=12 * length * width,
        vmem=16,
    )

    stages = radices(spans_of, 4)
    stride, held = 1, []
    for radix in stages:
        last = stride * radix == spans_of
        received = [swap(payload, "context", stride, radix, hop, last) for hop in range(1, radix)]
        if not last:
            payload, *held = call(
                functools.partial(merge_body, radix, stride, not held),
                [(payload.shape, BF16), ((state_width + ROW, width), F32)],
                [payload, *received, *held, base],
                idle=1,
            )
            stride *= radix

    *layers, ends = call(
        functools.partial(turn_body, members),
        [((features, length), BF16)] * members + [((members, PAD, features), BF16)],
        layers,
        moved=2 * members * features * length,
    )
    ends = lax.ppermute(ends, "context", [(i, i + 1) for i in range(spans_of - 1)])

    total_rows = members * features
    chunk = total_rows // spans_of
    scaling = 1.0 / math.sqrt(length * spans_of)
    split_shape = (spans_of // 2, chunk, width // 2)
    keep_near, send_near, keep_far, send_far, grads = call(
        functools.partial(tail_body, stages[-1], stride, not held, members, chunk),
        [(split_shape, F32), (split_shape, BF16), (split_shape, F32), (split_shape, BF16), ((PAD + length, width), BF16)],
        [*received, *held, states, base, coef, input_here, taps_here, ends, *layers],
        scratch=[pltpu.VMEM((length + 2 * PAD, width), F32)],
        flops=2 * length * width * total_rows,
        moved=16 * length * width,
        vmem=16,
    )

    got_near = swap(send_near, "context", 1, 2, 1)
    got_far = swap(send_far, "context", 2, 2, 1)

    quarter_shape = (spans_of // 4, chunk, width // 2)
    keep_near, send_near, keep_far, send_far = call(
        halve_both_body,
        [(quarter_shape, F32), (quarter_shape, BF16)] * 2,
        [keep_near, got_near, keep_far, got_far],
        moved=2 * total_rows * width,
        vmem=8,
    )
    got_near = swap(send_near, "context", 2, 2, 1)
    got_far = swap(send_far, "context", 1, 2, 1)
    half = members // 2
    high = PAD + length
    size = -(-half * high // (3 * PAD)) * PAD
    sizes = [min(size, half * high - start) for start in range(0, half * high, size)]
    shares = call(
        functools.partial(share_body, members, sizes),
        [((high, features), F32)] * half + [((size, features), BF16) for size in sizes],
        [grads, value_proj],
        flops=2 * length * width * total_rows,
        moved=8 * length * width,
        vmem=12,
    )
    stride = 1
    share, arrived = shares[:half], [swap(a, "tensor", stride, 2, 1) for a in shares[half:]]
    while half > 1:
        count, half = half, half // 2
        outs = call(
            functools.partial(share_sum_body, count, sizes),
            [((high, features), F32)] * half + [((high, features), BF16)] * half,
            [*share, *arrived],
            moved=4 * length * features,
        )
        stride *= 2
        sizes = [high] * half
        share, arrived = outs[:half], [swap(a, "tensor", stride, 2, 1) for a in outs[half:]]

    joined_shape = (spans_of // 8, chunk, width)
    keep, send = call(
        join_body,
        [(joined_shape, F32), (joined_shape, BF16)],
        [keep_near, got_near, keep_far, got_far],
        moved=total_rows * width,
        vmem=8,
    )
    got, shift = swap(send, "context", 4, 2, 1), 3
    while keep.shape[0] > 1:
        joined_shape = (keep.shape[0] // 2, chunk, width)
        keep, send = call(
            functools.partial(halve_body, shift),
            [(joined_shape, F32), (joined_shape, BF16)],
            [keep, got],
            moved=total_rows * width,
            vmem=8,
        )
        got = swap(send, "context", 1 << shift, 2, 1)
        shift += 1
    head, own = call(
        settle_body,
        [((PAD, features), F32), ((length, features), F32)],
        [*share, *arrived],
    )
    ahead = lax.ppermute(head, "context", [(i + 1, i) for i in range(spans_of - 1)])
    grad_value_proj, grad_input = call(
        functools.partial(end_body, scaling),
        [((chunk, width), F32), ((length, features), BF16)],
        [keep, got, own, ahead],
    )
    return (grad_input, grad_value_proj)


def solution(mesh):
    return jax.shard_map(
        local,
        mesh=mesh,
        in_specs=(
            P("context", "tensor"),
            P(None, "tensor"),
            P(None, "tensor"),
            P("context", "tensor"),
            P("context", None),
            P("context", None),
            P("tensor", "context"),
            P("tensor", "context"),
            P("tensor"),
            P("context", "tensor"),
        ),
        out_specs=(P("context", "tensor"), P("context", "tensor")),
        check_vma=False,
    )
```

time: 219 us -> 53.2 us (0.24)
  waiting for transfers between devices: 127 us -> 25.7 us
  local copies, waits for them, and re-layouts: 25.9 us -> 0.66 us
  blocking collectives: 23.1 us -> 0 us
  starting transfers between devices: 1.45 us -> 16.1 us
  between operations: 14.6 us -> 0.79 us
  other arithmetic: 13.3 us -> 0 us
  matrix products: 12.6 us -> 0 us
  Pallas kernels: 0 us -> 9.72 us
    reduce_scatter x2 -> x0, waiting for transfers between devices: 96 us -> none  [the longest x1 70.5 us: local(): lax.psum_scatter(product * scaling, 'context', scatter_dimension=0, tiled...]
    all_gather x2 -> x0, waiting for transfers between devices: 24.9 us -> none  [the longest x1 24.9 us: prefix(): gathered = jax.tree.map(lambda a: lax.all_gather(a, axis), part)]
    unnamed x1 -> x0, blocking collectives: 23.1 us -> none
    ppermute x1 -> x18, waiting for transfers between devices: 5.53 us -> 25.7 us  [the longest x16 21.3 us: swap(): return lax.ppermute(value, axis, pairs)]
    dynamic_update_slice x4 -> x0, local copies, waits for them, and re-layouts: 15.7 us -> none  [local(): lax.scan(whole_increment, incoming, block_inputs, reverse=True)[1]]
    ppermute x1 -> x18, starting transfers between devices: 1.29 us -> 16.1 us  [the longest x16 11.5 us: swap(): return lax.ppermute(value, axis, pairs)]
    dot_general x9 -> x0, matrix products: 12.6 us -> none  [the longest x1 3.23 us: local(): lax.dot_general(gathered, grad_proj, (((0,), (0,)), ((), ())), preferred_...]
    pallas_call x0 -> x11, Pallas kernels: none -> 9.72 us  [call(): pl.pallas_call(run, out_shape=[jax.ShapeDtypeStruct(shape, kind) for shap...]
  transfers between devices with their start and end apart: 5 -> 18, of which waited for: 4 -> 12; matrix products, arithmetic and copies ran while one was open for 20% -> 0% of each run, Pallas kernels for 0% -> 12%
where the time goes in v1:
time: 53.2 us; the launch traced here: 53 us
  waiting for transfers between devices  25.7 us (48%)
  starting transfers between devices  16.1 us (30%)
  Pallas kernels  9.72 us (18%)
  between operations  0.79 us (1%)
  local copies, waits for them, and re-layouts  0.66 us (1%)
    ppermute x16, waiting for transfers between devices, swap(): return lax.ppermute(value, axis, pairs)  21.3 us
    ppermute x16, starting transfers between devices, swap(): return lax.ppermute(value, axis, pairs)  11.5 us
    pallas_call x11, Pallas kernels, call(): pl.pallas_call(run, out_shape=[jax.ShapeDtypeStruct(shape, kind) for shap...  9.72 us
    ppermute x1, waiting for transfers between devices, local(): lax.ppermute(head, 'context', [(i + 1, i) for i in range(spans_of - 1)])  4.33 us
    ppermute x1, starting transfers between devices, local(): lax.ppermute(ends, 'context', [(i, i + 1) for i in range(spans_of - 1)])  3.32 us
    ppermute x1, starting transfers between devices, local(): lax.ppermute(head, 'context', [(i + 1, i) for i in range(spans_of - 1)])  1.29 us
  transfers between devices with their start and end apart: 18, of which 12 were waited for; matrix products, arithmetic and copies ran while one was open for 0% of the time, Pallas kernels for 12%

profile of v1, /device:TPU:0, one launch (start us, length us, event | category | flops | bytes accessed | tf_op | source)
XLA Modules:
  0.0 53.0 jit_solution(9457818256603180145)
XLA Ops:
  0.6 3.0 %collective-permute-start.5 = (bf16[512,256]{1,0:T(8,128)(2,1)}, bf16[512,256]{1,0:T(8,128)(2,1)S(1)}, u32[]{:S(2)}, u32[]{:S(2)}) collective-permute-start(bf16[512,256]{1,0:T(8,128)(2,1)} %refs_0_.5), channel_id=1, source_target_pairs={{0,2},{1,3},{2,0},{3,1},{4,6},{5,7},{6,4},{7,5},{8,10},{9,11},{10,... | collective-permute-start | bytes 786440 | tf_op jit(solution)/shard_map/ppermute | solution.py:74
  3.6 2.0 %shard_map.113 = (bf16[144,512]{1,0:T(8,128)(2,1)S(1)}, f32[2,136,512]{2,1,0:T(8,128)S(1)}, bf16[512,512]{1,0:T(8,128)(2,1)S(1)}, bf16[512,128]{1,0:T(8,128)(2,1...) custom-call(bf16[512,512]{1,0:T(8,128)(2,1)} %refs_0_.3, ...), custom_call_target="tpu_custom_call" | custom-call | flops 67108864 | bytes 524288 | tf_op jit(solution)/shard_map/pallas_call | solution.py:34
  5.6 2.6 %collective-permute-start.2 = (bf16[144,512]{1,0:T(8,128)(2,1)S(1)}, bf16[144,512]{1,0:T(8,128)(2,1)S(1)}, u32[]{:S(2)}, u32[]{:S(2)}) collective-permute-start(bf16[144,512]{1,0:T(8,128)(2,1)S(1)} %get-tuple-element.42.refs_0_), channel_id=1, source_target_pairs={{0,12},{4,8},{8,4},{12,0},{16,28},{20,24},{24,20},{28,16},{1,13},{... | collective-permute-start | bytes 442376 | tf_op jit(solution)/shard_map/ppermute | solution.py:74
  8.7 0.5 collective-permute-start
  9.2 1.0 %collective-permute-done.5.refs_2_ = bf16[512,256]{1,0:T(8,128)(2,1)S(1)} collective-permute-done((bf16[512,256]{1,0:T(8,128)(2,1)}, bf16[512,256]{1,0:T(8,128)(2,1)S(1)}, u32[]{:S(2)}, u32[]{:S(2)}) %collective-permute-start.5) | collective-permute-done | bytes 262176 | tf_op jit(solution)/shard_map/ppermute | solution.py:74
  10.2 0.7 %copy-done.2 = f32[8]{0:T(128)S(1)} copy-done((f32[8]{0:T(128)S(1)}, f32[8]{0:T(128)}, u32[]{:S(2)}) %copy-start.2) | copy-done | bytes 56
  10.8 2.7 %shard_map.114 = (f32[512,512]{1,0:T(8,128)S(1)}, f32[512,512]{1,0:T(8,128)S(1)}) custom-call(f32[8]{0:T(128)S(1)} %copy-done.2, bf16[512,128]{1,0:T(8,128)(2,1)S(1)} %get-tuple-element.43.refs_1_.refs_5_, bf16[512,128]{1,0:T(8,128)(2,1)S(1)} %get-tuple-element.44.refs_2_, bf16[512,512]{1,0:T(8,128)(2,1)S(1)} %get-tuple-element.45.refs_3_, ...), custom_call_target="tpu_custom_call" | custom-call | flops 34359738368 | bytes 3145728 | tf_op jit(solution)/shard_map/pallas_call | solution.py:34
  13.5 2.6 %collective-permute-done.1.refs_2_ = bf16[144,512]{1,0:T(8,128)(2,1)S(1)} collective-permute-done((bf16[144,512]{1,0:T(8,128)(2,1)S(1)}, bf16[144,512]{1,0:T(8,128)(2,1)S(1)}, u32[]{:S(2)}, u32[]{:S(2)}) %collective-permute-start.1) | collective-permute-done | bytes 147488 | tf_op jit(solution)/shard_map/ppermute | solution.py:74
  16.4 1.3 %collective-permute-start.3 = (bf16[144,512]{1,0:T(8,128)(2,1)S(1)}, bf16[144,512]{1,0:T(8,128)(2,1)S(1)}, u32[]{:S(2)}, u32[]{:S(2)}) collective-permute-start(bf16[144,512]{1,0:T(8,128)(2,1)S(1)} %get-tuple-element.50), channel_id=1, source_target_pairs={{16,0},{20,4},{24,8},{28,12},{17,1},{21,5},{25,9},{29,13},{18,2},{... | collective-permute-start | bytes 442376 | tf_op jit(solution)/shard_map/ppermute | solution.py:74
  18.0 3.3 %collective-permute-start.7 = (bf16[4,16,256]{2,1,0:T(8,128)(2,1)S(1)}, bf16[4,16,256]{2,1,0:T(8,128)(2,1)S(1)}, u32[]{:S(2)}, u32[]{:S(2)}) collective-permute-start(bf16[4,16,256]{2,1,0:T(8,128)(2,1)S(1)} %get-tuple-element.55), channel_id=1, source_target_pairs={{0,4},{4,8},{8,12},{12,16},{16,20},{20,24},{24,28},{1,5},{5,9},{9,... | collective-permute-start | bytes 98312 | tf_op jit(solution)/shard_map/ppermute | solution.py:470
  21.4 6.6 %collective-permute-done.3.refs_0_ = bf16[144,512]{1,0:T(8,128)(2,1)S(1)} collective-permute-done((bf16[144,512]{1,0:T(8,128)(2,1)S(1)}, bf16[144,512]{1,0:T(8,128)(2,1)S(1)}, u32[]{:S(2)}, u32[]{:S(2)}) %collective-permute-start.3) | collective-permute-done | bytes 147488 | tf_op jit(solution)/shard_map/ppermute | solution.py:74
  28.0 2.6 %shard_map.117 = (f32[4,128,256]{2,1,0:T(8,128)S(1)}, bf16[4,128,256]{2,1,0:T(8,128)(2,1)S(1)}, f32[4,128,256]{2,1,0:T(8,128)S(1)}, bf16[4,128,256]{2,1,0:T(8,128)(2,1)S(1)}, bf16[528,512]{1,0:T(8,128)(2,1)S(1)}) custom-call(bf16[144,512]{1,0:T(8,128)(2,1)S(1)} %collective-permute-done.3.refs_0_, f32[136,512]{1,0:T(8,128)S(1)} %get-tuple-element.51.refs_1_, ...), custom_call_target="tpu_custom_call" | custom-call | flops 536870912 | bytes 4194304 | tf_op jit(solution)/shard_map/pallas_call | solution.py:34
  30.6 1.6 %collective-permute-start.8 = (bf16[4,128,256]{2,1,0:T(8,128)(2,1)S(1)}, bf16[4,128,256]{2,1,0:T(8,128)(2,1)S(1)}, u32[]{:S(2)}, u32[]{:S(2)}) collective-permute-start(bf16[4,128,256]{2,1,0:T(8,128)(2,1)S(1)} %get-tuple-element.61), channel_id=1, source_target_pairs={{0,4},{4,0},{8,12},{12,8},{16,20},{20,16},{24,28},{28,24},{1,5},{5... | collective-permute-start | bytes 786440 | tf_op jit(solution)/shard_map/ppermute | solution.py:74
  32.2 0.8 %shard_map.120 = (f32[528,256]{1,0:T(8,128)S(1)}, f32[528,256]{1,0:T(8,128)S(1)}, bf16[352,256]{1,0:T(8,128)(2,1)S(1)}, bf16[352,256]{1,0:T(8,128)(2,1)S(1)}, bf16[352,256]{1,0:T(8,128)(2,1)S(1)}) custom-call(bf16[528,512]{1,0:T(8,128)(2,1)S(1)} %get-tuple-element.70.refs_0_, bf16[1024,512]{1,0:T(8,128)(2,1)S(1)} %copy-done.1), custom_call_target="tpu_custom_call" | custom-call | flops 536870912 | bytes 2097152 | tf_op jit(solution)/shard_map/pallas_call | solution.py:34
  33.1 0.5 collective-permute-start.14
  33.7 0.8 %collective-permute-done.13.refs_2_ = bf16[352,256]{1,0:T(8,128)(2,1)S(1)} collective-permute-done((bf16[352,256]{1,0:T(8,128)(2,1)S(1)}, bf16[352,256]{1,0:T(8,128)(2,1)S(1)}, u32[]{:S(2)}, u32[]{:S(2)}) %collective-permute-start.13) | collective-permute-done | bytes 180256 | tf_op jit(solution)/shard_map/ppermute | solution.py:74
  35.1 0.6 %collective-permute-start.16 = (bf16[528,256]{1,0:T(8,128)(2,1)S(1)}, bf16[528,256]{1,0:T(8,128)(2,1)S(1)}, u32[]{:S(2)}, u32[]{:S(2)}) collective-permute-start(bf16[528,256]{1,0:T(8,128)(2,1)S(1)} %get-tuple-element.77), channel_id=1, source_target_pairs={{0,2},{1,3},{2,0},{3,1},{4,6},{5,7},{6,4},{7,5},{8,10},{9,11},{10,... | collective-permute-start | bytes 811016 | tf_op jit(solution)/shard_map/ppermute | solution.py:74
  35.7 2.2 %collective-permute-done.8.refs_1_ = bf16[4,128,256]{2,1,0:T(8,128)(2,1)S(1)} collective-permute-done((bf16[4,128,256]{2,1,0:T(8,128)(2,1)S(1)}, bf16[4,128,256]{2,1,0:T(8,128)(2,1)S(1)}, u32[]{:S(2)}, u32[]{:S(2)}) %collective-permute-start.8) | collective-permute-done | bytes 262176 | tf_op jit(solution)/shard_map/ppermute | solution.py:74
  38.0 1.4 %collective-permute-done.9.refs_3_ = bf16[4,128,256]{2,1,0:T(8,128)(2,1)S(1)} collective-permute-done((bf16[4,128,256]{2,1,0:T(8,128)(2,1)S(1)}, bf16[4,128,256]{2,1,0:T(8,128)(2,1)S(1)}, u32[]{:S(2)}, u32[]{:S(2)}) %collective-permute-start.9) | collective-permute-done | bytes 262176 | tf_op jit(solution)/shard_map/ppermute | solution.py:74
  40.2 4.3 %collective-permute-done.10.refs_1_ = bf16[2,128,256]{2,1,0:T(8,128)(2,1)S(1)} collective-permute-done((bf16[2,128,256]{2,1,0:T(8,128)(2,1)S(1)}, bf16[2,128,256]{2,1,0:T(8,128)(2,1)S(1)}, u32[]{:S(2)}, u32[]{:S(2)}) %collective-permute-start.10) | collective-permute-done | bytes 131104 | tf_op jit(solution)/shard_map/ppermute | solution.py:74
  45.0 1.3 %collective-permute-start.17 = (f32[16,256]{1,0:T(8,128)S(1)}, f32[16,256]{1,0:T(8,128)S(1)}, u32[]{:S(2)}, u32[]{:S(2)}) collective-permute-start(f32[16,256]{1,0:T(8,128)S(1)} %get-tuple-element.79), channel_id=1, source_target_pairs={{4,0},{8,4},{12,8},{16,12},{20,16},{24,20},{28,24},{5,1},{9,5},{13... | collective-permute-start | bytes 49160 | tf_op jit(solution)/shard_map/ppermute | solution.py:550
  46.3 4.3 %collective-permute-done.17.refs_3_ = f32[16,256]{1,0:T(8,128)S(1)} collective-permute-done((f32[16,256]{1,0:T(8,128)S(1)}, f32[16,256]{1,0:T(8,128)S(1)}, u32[]{:S(2)}, u32[]{:S(2)}) %collective-permute-start.17) | collective-permute-done | bytes 16416 | tf_op jit(solution)/shard_map/ppermute | solution.py:550
  50.6 1.6 %collective-permute-done.12.refs_1_ = bf16[1,128,512]{2,1,0:T(8,128)(2,1)S(1)} collective-permute-done((bf16[1,128,512]{2,1,0:T(8,128)(2,1)S(1)}, bf16[1,128,512]{2,1,0:T(8,128)(2,1)S(1)}, u32[]{:S(2)}, u32[]{:S(2)}) %collective-permute-start.12) | collective-permute-done | bytes 131104 | tf_op jit(solution)/shard_map/ppermute | solution.py:74
  52.1 0.8 %shard_map.123 = (f32[128,512]{1,0:T(8,128)}, bf16[512,256]{1,0:T(8,128)(2,1)}) custom-call(f32[1,128,512]{2,1,0:T(8,128)S(1)} %get-tuple-element.68.refs_0_, bf16[1,128,512]{2,1,0:T(8,128)(2,1)S(1)} %collective-permute-done.12.refs_1_, f32[512,256]{1,0:T(8,128)S(1)} %get-tuple-element.78.refs_2_, f32[16,256]{1,0:T(8,128)S(1)} %collective-permute-done.17.refs_3_), custom_call_target="tpu_custom_call" | custom-call | tf_op jit(solution)/shard_map/pallas_call | solution.py:34
  (29 shorter events, 3.1 us)
Async XLA Ops:
  0.6 9.5 %collective-permute-start.5 = (bf16[512,256]{1,0:T(8,128)(2,1)}, bf16[512,256]{1,0:T(8,128)(2,1)S(1)}, u32[]{:S(2)}, u32[]{:S(2)}) collective-permute-start(bf16[512,256]{1,0:T(8,128)(2,1)} %refs_0_.5), channel_id=1, source_target_pairs={{0,2},{1,3},{2,0},{3,1},{4,6},{5,7},{6,4},{7,5},{8,10},{9,11},{10,... | collective-permute-start | bytes 786440 | tf_op jit(solution)/shard_map/ppermute | solution.py:74
  3.6 14.0 %collective-permute-start.4 = (bf16[512,256]{1,0:T(8,128)(2,1)}, bf16[512,256]{1,0:T(8,128)(2,1)S(1)}, u32[]{:S(2)}, u32[]{:S(2)}) collective-permute-start(bf16[512,256]{1,0:T(8,128)(2,1)} %refs_0_.5), channel_id=1, source_target_pairs={{0,1},{1,0},{2,3},{3,2},{4,5},{5,4},{6,7},{7,6},{8,9},{9,8},{10,11... | collective-permute-start | bytes 786440 | tf_op jit(solution)/shard_map/ppermute | solution.py:74
  5.6 7.8 %collective-permute-start.2 = (bf16[144,512]{1,0:T(8,128)(2,1)S(1)}, bf16[144,512]{1,0:T(8,128)(2,1)S(1)}, u32[]{:S(2)}, u32[]{:S(2)}) collective-permute-start(bf16[144,512]{1,0:T(8,128)(2,1)S(1)} %get-tuple-element.42.refs_0_), channel_id=1, source_target_pairs={{0,12},{4,8},{8,4},{12,0},{16,28},{20,24},{24,20},{28,16},{1,13},{... | collective-permute-start | bytes 442376 | tf_op jit(solution)/shard_map/ppermute | solution.py:74
  8.2 7.9 %collective-permute-start.1 = (bf16[144,512]{1,0:T(8,128)(2,1)S(1)}, bf16[144,512]{1,0:T(8,128)(2,1)S(1)}, u32[]{:S(2)}, u32[]{:S(2)}) collective-permute-start(bf16[144,512]{1,0:T(8,128)(2,1)S(1)} %get-tuple-element.42.refs_0_), channel_id=1, source_target_pairs={{0,8},{4,12},{8,0},{12,4},{16,24},{20,28},{24,16},{28,20},{1,9},{5... | collective-permute-start | bytes 442376 | tf_op jit(solution)/shard_map/ppermute | solution.py:74
  8.7 7.4 %collective-permute-start = (bf16[144,512]{1,0:T(8,128)(2,1)S(1)}, bf16[144,512]{1,0:T(8,128)(2,1)S(1)}, u32[]{:S(2)}, u32[]{:S(2)}) collective-permute-start(bf16[144,512]{1,0:T(8,128)(2,1)S(1)} %get-tuple-element.42.refs_0_), channel_id=1, source_target_pairs={{0,4},{4,0},{8,12},{12,8},{16,20},{20,16},{24,28},{28,24},{1,5},{5... | collective-permute-start | bytes 442376 | tf_op jit(solution)/shard_map/ppermute | solution.py:74
  10.2 7.5 %collective-permute-start.6 = (bf16[512,256]{1,0:T(8,128)(2,1)S(1)}, bf16[512,256]{1,0:T(8,128)(2,1)S(1)}, u32[]{:S(2)}, u32[]{:S(2)}) collective-permute-start(bf16[512,256]{1,0:T(8,128)(2,1)S(1)} %collective-permute-done.5.refs_2_), channel_id=1, source_target_pairs={{0,1},{1,0},{2,3},{3,2},{4,5},{5,4},{6,7},{7,6},{8,9},{9,8},{10,11... | collective-permute-start | bytes 786440 | tf_op jit(solution)/shard_map/ppermute | solution.py:74
  10.2 0.7 %copy-start.2 = (f32[8]{0:T(128)S(1)}, f32[8]{0:T(128)}, u32[]{:S(2)}) copy-start(f32[8]{0:T(128)} %refs_0_.4) | copy-start | bytes 100
  16.1 1.6 %copy-start = (bf16[512,256]{1,0:T(8,128)(2,1)S(1)}, bf16[512,256]{1,0:T(8,128)(2,1)}, u32[]{:S(2)}) copy-start(bf16[512,256]{1,0:T(8,128)(2,1)} %refs_0_.5) | copy-start | bytes 786436
  16.4 11.6 %collective-permute-start.3 = (bf16[144,512]{1,0:T(8,128)(2,1)S(1)}, bf16[144,512]{1,0:T(8,128)(2,1)S(1)}, u32[]{:S(2)}, u32[]{:S(2)}) collective-permute-start(bf16[144,512]{1,0:T(8,128)(2,1)S(1)} %get-tuple-element.50), channel_id=1, source_target_pairs={{16,0},{20,4},{24,8},{28,12},{17,1},{21,5},{25,9},{29,13},{18,2},{... | collective-permute-start | bytes 442376 | tf_op jit(solution)/shard_map/ppermute | solution.py:74
  18.0 10.0 %collective-permute-start.7 = (bf16[4,16,256]{2,1,0:T(8,128)(2,1)S(1)}, bf16[4,16,256]{2,1,0:T(8,128)(2,1)S(1)}, u32[]{:S(2)}, u32[]{:S(2)}) collective-permute-start(bf16[4,16,256]{2,1,0:T(8,128)(2,1)S(1)} %get-tuple-element.55), channel_id=1, source_target_pairs={{0,4},{4,8},{8,12},{12,16},{16,20},{20,24},{24,28},{1,5},{5,9},{9,... | collective-permute-start | bytes 98312 | tf_op jit(solution)/shard_map/ppermute | solution.py:470
  28.0 4.2 %copy-start.1 = (bf16[1024,512]{1,0:T(8,128)(2,1)S(1)}, bf16[1024,512]{1,0:T(8,128)(2,1)}, u32[]{:S(2)}) copy-start(bf16[1024,512]{1,0:T(8,128)(2,1)} %refs_1_.3) | copy-start | bytes 3145732
  30.6 7.3 %collective-permute-start.8 = (bf16[4,128,256]{2,1,0:T(8,128)(2,1)S(1)}, bf16[4,128,256]{2,1,0:T(8,128)(2,1)S(1)}, u32[]{:S(2)}, u32[]{:S(2)}) collective-permute-start(bf16[4,128,256]{2,1,0:T(8,128)(2,1)S(1)} %get-tuple-element.61), channel_id=1, source_target_pairs={{0,4},{4,0},{8,12},{12,8},{16,20},{20,16},{24,28},{28,24},{1,5},{5... | collective-permute-start | bytes 786440 | tf_op jit(solution)/shard_map/ppermute | solution.py:74
  32.2 7.1 %collective-permute-start.9 = (bf16[4,128,256]{2,1,0:T(8,128)(2,1)S(1)}, bf16[4,128,256]{2,1,0:T(8,128)(2,1)S(1)}, u32[]{:S(2)}, u32[]{:S(2)}) collective-permute-start(bf16[4,128,256]{2,1,0:T(8,128)(2,1)S(1)} %get-tuple-element.63), channel_id=1, source_target_pairs={{0,8},{4,12},{8,0},{12,4},{16,24},{20,28},{24,16},{28,20},{1,9},{5... | collective-permute-start | bytes 786440 | tf_op jit(solution)/shard_map/ppermute | solution.py:74
  33.0 1.5 %collective-permute-start.13 = (bf16[352,256]{1,0:T(8,128)(2,1)S(1)}, bf16[352,256]{1,0:T(8,128)(2,1)S(1)}, u32[]{:S(2)}, u32[]{:S(2)}) collective-permute-start(bf16[352,256]{1,0:T(8,128)(2,1)S(1)} %get-tuple-element.73), channel_id=1, source_target_pairs={{0,1},{1,0},{2,3},{3,2},{4,5},{5,4},{6,7},{7,6},{8,9},{9,8},{10,11... | collective-permute-start | bytes 540680 | tf_op jit(solution)/shard_map/ppermute | solution.py:74
  33.1 1.7 %collective-permute-start.14 = (bf16[352,256]{1,0:T(8,128)(2,1)S(1)}, bf16[352,256]{1,0:T(8,128)(2,1)S(1)}, u32[]{:S(2)}, u32[]{:S(2)}) collective-permute-start(bf16[352,256]{1,0:T(8,128)(2,1)S(1)} %get-tuple-element.74), channel_id=1, source_target_pairs={{0,1},{1,0},{2,3},{3,2},{4,5},{5,4},{6,7},{7,6},{8,9},{9,8},{10,11... | collective-permute-start | bytes 540680 | tf_op jit(solution)/shard_map/ppermute | solution.py:74
  33.6 1.4 %collective-permute-start.15 = (bf16[352,256]{1,0:T(8,128)(2,1)S(1)}, bf16[352,256]{1,0:T(8,128)(2,1)S(1)}, u32[]{:S(2)}, u32[]{:S(2)}) collective-permute-start(bf16[352,256]{1,0:T(8,128)(2,1)S(1)} %get-tuple-element.75), channel_id=1, source_target_pairs={{0,1},{1,0},{2,3},{3,2},{4,5},{5,4},{6,7},{7,6},{8,9},{9,8},{10,11... | collective-permute-start | bytes 540680 | tf_op jit(solution)/shard_map/ppermute | solution.py:74
  35.1 9.8 %collective-permute-start.16 = (bf16[528,256]{1,0:T(8,128)(2,1)S(1)}, bf16[528,256]{1,0:T(8,128)(2,1)S(1)}, u32[]{:S(2)}, u32[]{:S(2)}) collective-permute-start(bf16[528,256]{1,0:T(8,128)(2,1)S(1)} %get-tuple-element.77), channel_id=1, source_target_pairs={{0,2},{1,3},{2,0},{3,1},{4,6},{5,7},{6,4},{7,5},{8,10},{9,11},{10,... | collective-permute-start | bytes 811016 | tf_op jit(solution)/shard_map/ppermute | solution.py:74
  39.4 5.0 %collective-permute-start.10 = (bf16[2,128,256]{2,1,0:T(8,128)(2,1)S(1)}, bf16[2,128,256]{2,1,0:T(8,128)(2,1)S(1)}, u32[]{:S(2)}, u32[]{:S(2)}) collective-permute-start(bf16[2,128,256]{2,1,0:T(8,128)(2,1)S(1)} %get-tuple-element.65), channel_id=1, source_target_pairs={{0,8},{4,12},{8,0},{12,4},{16,24},{20,28},{24,16},{28,20},{1,9},{5... | collective-permute-start | bytes 393224 | tf_op jit(solution)/shard_map/ppermute | solution.py:74
  39.8 5.0 %collective-permute-start.11 = (bf16[2,128,256]{2,1,0:T(8,128)(2,1)S(1)}, bf16[2,128,256]{2,1,0:T(8,128)(2,1)S(1)}, u32[]{:S(2)}, u32[]{:S(2)}) collective-permute-start(bf16[2,128,256]{2,1,0:T(8,128)(2,1)S(1)} %get-tuple-element.67), channel_id=1, source_target_pairs={{0,4},{4,0},{8,12},{12,8},{16,20},{20,16},{24,28},{28,24},{1,5},{5... | collective-permute-start | bytes 393224 | tf_op jit(solution)/shard_map/ppermute | solution.py:74
  44.8 7.3 %collective-permute-start.12 = (bf16[1,128,512]{2,1,0:T(8,128)(2,1)S(1)}, bf16[1,128,512]{2,1,0:T(8,128)(2,1)S(1)}, u32[]{:S(2)}, u32[]{:S(2)}) collective-permute-start(bf16[1,128,512]{2,1,0:T(8,128)(2,1)S(1)} %get-tuple-element.69), channel_id=1, source_target_pairs={{0,16},{4,20},{8,24},{12,28},{16,0},{20,4},{24,8},{28,12},{1,17},{... | collective-permute-start | bytes 393224 | tf_op jit(solution)/shard_map/ppermute | solution.py:74
  45.0 5.6 %collective-permute-start.17 = (f32[16,256]{1,0:T(8,128)S(1)}, f32[16,256]{1,0:T(8,128)S(1)}, u32[]{:S(2)}, u32[]{:S(2)}) collective-permute-start(f32[16,256]{1,0:T(8,128)S(1)} %get-tuple-element.79), channel_id=1, source_target_pairs={{4,0},{8,4},{12,8},{16,12},{20,16},{24,20},{28,24},{5,1},{9,5},{13... | collective-permute-start | bytes 49160 | tf_op jit(solution)/shard_map/ppermute | solution.py:550

commit v2 on v1

--- a/solution.py
+++ b/solution.py
@@ -194,7 +194,10 @@
     states, decays = [a for a, _ in pairs], [b for _, b in pairs]
     places = [origin(digit, radix, hop) for hop in range(radix)]
     whole, whole_span = later_sum(-1, places, states, decays)
-    pack_state(next_ref, whole, whole_span)
+    if next_ref.shape[0] > whole.shape[0]:
+        pack_state(next_ref, whole, whole_span)
+    else:
+        next_ref[...] = whole.astype(BF16)
     later, span = later_sum(digit, places[1:], states[1:], decays[1:])
     if not first:
         held, reach = kept_state(refs[radix - 1])
@@ -279,9 +282,12 @@
     length, width = base_ref.shape
     place = lax.axis_index("context")
     digit = place // stride % radix
-    pairs = [unpack_state(ref) for ref in received]
-    places = [origin(digit, radix, hop) for hop in range(1, radix)]
-    carry, _ = later_sum(digit, places, [a for a, _ in pairs], [b for _, b in pairs])
+    if radix == 2:
+        carry = jnp.where(digit == 0, received[0][...].astype(F32), 0.0)
+    else:
+        pairs = [unpack_state(ref) for ref in received]
+        places = [origin(digit, radix, hop) for hop in range(1, radix)]
+        carry, _ = later_sum(digit, places, [a for a, _ in pairs], [b for _, b in pairs])
     if not first:
         held, reach = kept_state(held_ref)
         carry = held + jnp.exp(reach) * carry
@@ -306,23 +312,35 @@
     me = lax.axis_index("tensor")
     half = width // 2
 
-    def put(keep, send, same, index, value):
-        @pl.when(same)
-        def _():
-            keep[index] = value
-
-        @pl.when(jnp.logical_not(same))
-        def _():
-            send[index] = value.astype(BF16)
-
-    for hop in range(members):
-        source = origin(me, members, hop)
-        product = dot(layer_refs[hop][...], grads_ref[PAD:, :], (1, 0)) + dot(ends_ref[hop], grads_ref[:PAD, :], (0, 0))
-        for index in range(per_piece):
-            number = source * per_piece + index
-            rows = product[index * chunk : (index + 1) * chunk, :]
-            put(keep_near, send_near, (number & 1) == (place & 1), number >> 1, rows[:, :half])
-            put(keep_far, send_far, (number & 2) == (place & 2), (number & 1) + ((number >> 2) << 1), rows[:, half:])
+    def put(keep, send, bit, there, zero, one):
+        mine = bit == 0
+        keep[there] = jnp.where(mine, zero, one)
+        send[there] = jnp.where(mine, one, zero).astype(BF16)
+
+    near_bit, far_bit = place & 1, (place >> 1) & 1
+    for start in range(0, members, 2):
+        products = []
+        for hop in (start, start + 1):
+            ends = ends_ref[hop]
+            products.append(dot(layer_refs[hop][...], grads_ref[PAD:, :], (1, 0)) + dot(ends, grads_ref[:PAD, :], (0, 0)))
+        chunks = [[p[i * chunk : (i + 1) * chunk, :] for i in range(per_piece)] for p in products]
+        sources = [origin(me, members, hop) for hop in (start, start + 1)]
+        for source, parts in zip(sources, chunks):
+            for i in range(0, per_piece, 2):
+                zero, one = parts[i][:, :half], parts[i + 1][:, :half]
+                put(keep_near, send_near, near_bit, (source * per_piece + i) >> 1, zero, one)
+        if per_piece > 2:
+            for source, parts in zip(sources, chunks):
+                for i in range(per_piece):
+                    if not i & 2:
+                        number = source * per_piece + i
+                        zero, one = parts[i][:, half:], parts[i + 2][:, half:]
+                        put(keep_far, send_far, far_bit, (number & 1) + ((number >> 2) << 1), zero, one)
+        else:
+            swapped = (sources[0] & 1) ^ far_bit
+            for i in range(per_piece):
+                there = i + ((sources[0] >> 1) << 1)
+                put(keep_far, send_far, swapped, there, chunks[0][i][:, half:], chunks[1][i][:, half:])
 
 
 def overlaps(index, high, sizes):
@@ -362,11 +380,14 @@
     own_ref[...] = share_ref[PAD:, :] + arrived_ref[PAD:, :].astype(F32)
 
 
-def end_body(scaling, keep_ref, got_ref, own_ref, ahead_ref, proj_out, input_out):
-    proj_out[...] = (keep_ref[0] + got_ref[0].astype(F32)) * scaling
+def input_end_body(own_ref, ahead_ref, out_ref):
     rest = own_ref.shape[0] - PAD
-    input_out[:rest, :] = own_ref[:rest, :].astype(BF16)
-    input_out[rest:, :] = (own_ref[rest:, :] + ahead_ref[...]).astype(BF16)
+    out_ref[:rest, :] = own_ref[:rest, :].astype(BF16)
+    out_ref[rest:, :] = (own_ref[rest:, :] + ahead_ref[...]).astype(BF16)
+
+
+def proj_end_body(scaling, keep_ref, got_ref, out_ref):
+    out_ref[...] = (keep_ref[0] + got_ref[0].astype(F32)) * scaling
 
 
 def halve(bit, keep_ref, received_ref, keep_out, send_out):
@@ -453,9 +474,11 @@
         last = stride * radix == spans_of
         received = [swap(payload, "context", stride, radix, hop, last) for hop in range(1, radix)]
         if not last:
+            following = stages[stages.index(radix) + 1] if len(stages) == 2 else 4
+            rows = state_width if following == 2 else state_width + PAD
             payload, *held = call(
                 functools.partial(merge_body, radix, stride, not held),
-                [(payload.shape, BF16), ((state_width + ROW, width), F32)],
+                [((rows, width), BF16), ((state_width + ROW, width), F32)],
                 [payload, *received, *held, base],
                 idle=1,
             )
@@ -548,11 +571,8 @@
         [*share, *arrived],
     )
     ahead = lax.ppermute(head, "context", [(i + 1, i) for i in range(spans_of - 1)])
-    grad_value_proj, grad_input = call(
-        functools.partial(end_body, scaling),
-        [((chunk, width), F32), ((length, features), BF16)],
-        [keep, got, own, ahead],
-    )
+    (grad_input,) = call(input_end_body, [((length, features), BF16)], [own, ahead])
+    (grad_value_proj,) = call(functools.partial(proj_end_body, scaling), [((chunk, width), F32)], [keep, got])
     return (grad_input, grad_value_proj)
 
 

time: 53.2 us -> 51.8 us (0.974)
  waiting for transfers between devices: 25.7 us -> 23.6 us
  starting transfers between devices: 16.1 us -> 16.8 us
    ppermute x16, waiting for transfers between devices: 21.3 us -> 19.3 us  [swap(): return lax.ppermute(value, axis, pairs)]
    ppermute x16, starting transfers between devices: 11.5 us -> 12.2 us  [swap(): return lax.ppermute(value, axis, pairs)]
    pallas_call x11 -> x12, Pallas kernels: 9.72 us -> 9.68 us  [call(): pl.pallas_call(run, out_shape=[jax.ShapeDtypeStruct(shape, kind) for shap...]
  transfers between devices with their start and end apart: 18 -> 18, of which waited for: 12 -> 12; matrix products, arithmetic and copies ran while one was open for 0% -> 0% of each run, Pallas kernels for 12% -> 14%
where the time goes in v2:
time: 51.8 us; the launch traced here: 51.6 us
  waiting for transfers between devices  23.6 us (46%)
  starting transfers between devices  16.8 us (32%)
  Pallas kernels  9.68 us (19%)
  between operations  0.77 us (1%)
  local copies, waits for them, and re-layouts  0.66 us (1%)
    ppermute x16, waiting for transfers between devices, swap(): return lax.ppermute(value, axis, pairs)  19.3 us
    ppermute x16, starting transfers between devices, swap(): return lax.ppermute(value, axis, pairs)  12.2 us
    pallas_call x12, Pallas kernels, call(): pl.pallas_call(run, out_shape=[jax.ShapeDtypeStruct(shape, kind) for shap...  9.68 us
    ppermute x1, waiting for transfers between devices, local(): lax.ppermute(head, 'context', [(i + 1, i) for i in range(spans_of - 1)])  4.33 us
    ppermute x1, starting transfers between devices, local(): lax.ppermute(ends, 'context', [(i, i + 1) for i in range(spans_of - 1)])  3.32 us
    ppermute x1, starting transfers between devices, local(): lax.ppermute(head, 'context', [(i + 1, i) for i in range(spans_of - 1)])  1.29 us
  transfers between devices with their start and end apart: 18, of which 12 were waited for; matrix products, arithmetic and copies ran while one was open for 0% of the time, Pallas kernels for 14%

profile of v2, /device:TPU:0, one launch (start us, length us, event | category | flops | bytes accessed | tf_op | source)
XLA Modules:
  0.0 51.6 jit_solution(12107430384301412995)
XLA Ops:
  0.6 3.0 %collective-permute-start.5 = (bf16[512,256]{1,0:T(8,128)(2,1)}, bf16[512,256]{1,0:T(8,128)(2,1)S(1)}, u32[]{:S(2)}, u32[]{:S(2)}) collective-permute-start(bf16[512,256]{1,0:T(8,128)(2,1)} %refs_0_.5), channel_id=1, source_target_pairs={{0,2},{1,3},{2,0},{3,1},{4,6},{5,7},{6,4},{7,5},{8,10},{9,11},{10,... | collective-permute-start | bytes 786440 | tf_op jit(solution)/shard_map/ppermute | solution.py:74
  3.6 2.0 %shard_map.113 = (bf16[144,512]{1,0:T(8,128)(2,1)S(1)}, f32[2,136,512]{2,1,0:T(8,128)S(1)}, bf16[512,512]{1,0:T(8,128)(2,1)S(1)}, bf16[512,128]{1,0:T(8,128)(2,1...) custom-call(bf16[512,512]{1,0:T(8,128)(2,1)} %refs_0_.3, ...), custom_call_target="tpu_custom_call" | custom-call | flops 67108864 | bytes 524288 | tf_op jit(solution)/shard_map/pallas_call | solution.py:34
  5.6 2.6 %collective-permute-start.2 = (bf16[144,512]{1,0:T(8,128)(2,1)S(1)}, bf16[144,512]{1,0:T(8,128)(2,1)S(1)}, u32[]{:S(2)}, u32[]{:S(2)}) collective-permute-start(bf16[144,512]{1,0:T(8,128)(2,1)S(1)} %get-tuple-element.40.refs_0_), channel_id=1, source_target_pairs={{0,12},{4,8},{8,4},{12,0},{16,28},{20,24},{24,20},{28,16},{1,13},{... | collective-permute-start | bytes 442376 | tf_op jit(solution)/shard_map/ppermute | solution.py:74
  8.7 0.5 collective-permute-start
  9.2 1.0 %collective-permute-done.5.refs_2_ = bf16[512,256]{1,0:T(8,128)(2,1)S(1)} collective-permute-done((bf16[512,256]{1,0:T(8,128)(2,1)}, bf16[512,256]{1,0:T(8,128)(2,1)S(1)}, u32[]{:S(2)}, u32[]{:S(2)}) %collective-permute-start.5) | collective-permute-done | bytes 262176 | tf_op jit(solution)/shard_map/ppermute | solution.py:74
  10.2 0.7 %copy-done.2 = f32[8]{0:T(128)S(1)} copy-done((f32[8]{0:T(128)S(1)}, f32[8]{0:T(128)}, u32[]{:S(2)}) %copy-start.2) | copy-done | bytes 56
  10.8 2.7 %shard_map.114 = (f32[512,512]{1,0:T(8,128)S(1)}, f32[512,512]{1,0:T(8,128)S(1)}) custom-call(f32[8]{0:T(128)S(1)} %copy-done.2, bf16[512,128]{1,0:T(8,128)(2,1)S(1)} %get-tuple-element.41.refs_1_.refs_5_, bf16[512,128]{1,0:T(8,128)(2,1)S(1)} %get-tuple-element.42.refs_2_, bf16[512,512]{1,0:T(8,128)(2,1)S(1)} %get-tuple-element.43.refs_3_, ...), custom_call_target="tpu_custom_call" | custom-call | flops 34359738368 | bytes 3145728 | tf_op jit(solution)/shard_map/pallas_call | solution.py:34
  13.5 2.6 %collective-permute-done.1.refs_2_ = bf16[144,512]{1,0:T(8,128)(2,1)S(1)} collective-permute-done((bf16[144,512]{1,0:T(8,128)(2,1)S(1)}, bf16[144,512]{1,0:T(8,128)(2,1)S(1)}, u32[]{:S(2)}, u32[]{:S(2)}) %collective-permute-start.1) | collective-permute-done | bytes 147488 | tf_op jit(solution)/shard_map/ppermute | solution.py:74
  16.4 1.3 %collective-permute-start.3 = (bf16[128,512]{1,0:T(8,128)(2,1)S(1)}, bf16[128,512]{1,0:T(8,128)(2,1)S(1)}, u32[]{:S(2)}, u32[]{:S(2)}) collective-permute-start(bf16[128,512]{1,0:T(8,128)(2,1)S(1)} %get-tuple-element.48), channel_id=1, source_target_pairs={{16,0},{20,4},{24,8},{28,12},{17,1},{21,5},{25,9},{29,13},{18,2},{... | collective-permute-start | bytes 393224 | tf_op jit(solution)/shard_map/ppermute | solution.py:74
  18.0 3.3 %collective-permute-start.7 = (bf16[4,16,256]{2,1,0:T(8,128)(2,1)S(1)}, bf16[4,16,256]{2,1,0:T(8,128)(2,1)S(1)}, u32[]{:S(2)}, u32[]{:S(2)}) collective-permute-start(bf16[4,16,256]{2,1,0:T(8,128)(2,1)S(1)} %get-tuple-element.53), channel_id=1, source_target_pairs={{0,4},{4,8},{8,12},{12,16},{16,20},{20,24},{24,28},{1,5},{5,9},{9,... | collective-permute-start | bytes 98312 | tf_op jit(solution)/shard_map/ppermute | solution.py:493
  21.3 5.9 %collective-permute-done.3.refs_0_ = bf16[128,512]{1,0:T(8,128)(2,1)S(1)} collective-permute-done((bf16[128,512]{1,0:T(8,128)(2,1)S(1)}, bf16[128,512]{1,0:T(8,128)(2,1)S(1)}, u32[]{:S(2)}, u32[]{:S(2)}) %collective-permute-start.3) | collective-permute-done | bytes 131104 | tf_op jit(solution)/shard_map/ppermute | solution.py:74
  27.3 2.0 %shard_map.117 = (f32[4,128,256]{2,1,0:T(8,128)S(1)}, bf16[4,128,256]{2,1,0:T(8,128)(2,1)S(1)}, f32[4,128,256]{2,1,0:T(8,128)S(1)}, bf16[4,128,256]{2,1,0:T(8,128)(2,1)S(1)}, bf16[528,512]{1,0:T(8,128)(2,1)S(1)}) custom-call(bf16[128,512]{1,0:T(8,128)(2,1)S(1)} %collective-permute-done.3.refs_0_, f32[136,512]{1,0:T(8,128)S(1)} %get-tuple-element.49.refs_1_, ...), custom_call_target="tpu_custom_call" | custom-call | flops 536870912 | bytes 4194304 | tf_op jit(solution)/shard_map/pallas_call | solution.py:34
  29.3 1.6 %collective-permute-start.13 = (bf16[4,128,256]{2,1,0:T(8,128)(2,1)S(1)}, bf16[4,128,256]{2,1,0:T(8,128)(2,1)S(1)}, u32[]{:S(2)}, u32[]{:S(2)}) collective-permute-start(bf16[4,128,256]{2,1,0:T(8,128)(2,1)S(1)} %get-tuple-element.69), channel_id=1, source_target_pairs={{0,4},{4,0},{8,12},{12,8},{16,20},{20,16},{24,28},{28,24},{1,5},{5... | collective-permute-start | bytes 786440 | tf_op jit(solution)/shard_map/ppermute | solution.py:74
  30.8 0.8 %shard_map.118 = (f32[528,256]{1,0:T(8,128)S(1)}, f32[528,256]{1,0:T(8,128)S(1)}, bf16[352,256]{1,0:T(8,128)(2,1)S(1)}, bf16[352,256]{1,0:T(8,128)(2,1)S(1)}, bf16[352,256]{1,0:T(8,128)(2,1)S(1)}) custom-call(bf16[528,512]{1,0:T(8,128)(2,1)S(1)} %get-tuple-element.58.refs_0_, bf16[1024,512]{1,0:T(8,128)(2,1)S(1)} %copy-done.1), custom_call_target="tpu_custom_call" | custom-call | flops 536870912 | bytes 2097152 | tf_op jit(solution)/shard_map/pallas_call | solution.py:34
  32.3 0.8 %collective-permute-done.8.refs_2_ = bf16[352,256]{1,0:T(8,128)(2,1)S(1)} collective-permute-done((bf16[352,256]{1,0:T(8,128)(2,1)S(1)}, bf16[352,256]{1,0:T(8,128)(2,1)S(1)}, u32[]{:S(2)}, u32[]{:S(2)}) %collective-permute-start.8) | collective-permute-done | bytes 180256 | tf_op jit(solution)/shard_map/ppermute | solution.py:74
  33.7 0.6 %collective-permute-start.11 = (bf16[528,256]{1,0:T(8,128)(2,1)S(1)}, bf16[528,256]{1,0:T(8,128)(2,1)S(1)}, u32[]{:S(2)}, u32[]{:S(2)}) collective-permute-start(bf16[528,256]{1,0:T(8,128)(2,1)S(1)} %get-tuple-element.65), channel_id=1, source_target_pairs={{0,2},{1,3},{2,0},{3,1},{4,6},{5,7},{6,4},{7,5},{8,10},{9,11},{10,... | collective-permute-start | bytes 811016 | tf_op jit(solution)/shard_map/ppermute | solution.py:74
  34.3 2.3 %collective-permute-done.13.refs_1_ = bf16[4,128,256]{2,1,0:T(8,128)(2,1)S(1)} collective-permute-done((bf16[4,128,256]{2,1,0:T(8,128)(2,1)S(1)}, bf16[4,128,256]{2,1,0:T(8,128)(2,1)S(1)}, u32[]{:S(2)}, u32[]{:S(2)}) %collective-permute-start.13) | collective-permute-done | bytes 262176 | tf_op jit(solution)/shard_map/ppermute | solution.py:74
  36.6 1.3 %collective-permute-done.14.refs_3_ = bf16[4,128,256]{2,1,0:T(8,128)(2,1)S(1)} collective-permute-done((bf16[4,128,256]{2,1,0:T(8,128)(2,1)S(1)}, bf16[4,128,256]{2,1,0:T(8,128)(2,1)S(1)}, u32[]{:S(2)}, u32[]{:S(2)}) %collective-permute-start.14) | collective-permute-done | bytes 262176 | tf_op jit(solution)/shard_map/ppermute | solution.py:74
  38.8 4.3 %collective-permute-done.15.refs_1_ = bf16[2,128,256]{2,1,0:T(8,128)(2,1)S(1)} collective-permute-done((bf16[2,128,256]{2,1,0:T(8,128)(2,1)S(1)}, bf16[2,128,256]{2,1,0:T(8,128)(2,1)S(1)}, u32[]{:S(2)}, u32[]{:S(2)}) %collective-permute-start.15) | collective-permute-done | bytes 131104 | tf_op jit(solution)/shard_map/ppermute | solution.py:74
  43.4 0.8 %collective-permute-start.17 = (bf16[1,128,512]{2,1,0:T(8,128)(2,1)S(1)}, bf16[1,128,512]{2,1,0:T(8,128)(2,1)S(1)}, u32[]{:S(2)}, u32[]{:S(2)}) collective-permute-start(bf16[1,128,512]{2,1,0:T(8,128)(2,1)S(1)} %get-tuple-element.77), channel_id=1, source_target_pairs={{0,16},{4,20},{8,24},{12,28},{16,0},{20,4},{24,8},{28,12},{1,17},{... | collective-permute-start | bytes 393224 | tf_op jit(solution)/shard_map/ppermute | solution.py:74
  44.2 1.3 %collective-permute-start.12 = (f32[16,256]{1,0:T(8,128)S(1)}, f32[16,256]{1,0:T(8,128)S(1)}, u32[]{:S(2)}, u32[]{:S(2)}) collective-permute-start(f32[16,256]{1,0:T(8,128)S(1)} %get-tuple-element.67), channel_id=1, source_target_pairs={{4,0},{8,4},{12,8},{16,12},{20,16},{24,20},{28,24},{5,1},{9,5},{13... | collective-permute-start | bytes 49160 | tf_op jit(solution)/shard_map/ppermute | solution.py:573
  45.5 4.3 %collective-permute-done.12.refs_1_ = f32[16,256]{1,0:T(8,128)S(1)} collective-permute-done((f32[16,256]{1,0:T(8,128)S(1)}, f32[16,256]{1,0:T(8,128)S(1)}, u32[]{:S(2)}, u32[]{:S(2)}) %collective-permute-start.12) | collective-permute-done | bytes 16416 | tf_op jit(solution)/shard_map/ppermute | solution.py:573
  49.9 0.7 %shard_map.121 = bf16[512,256]{1,0:T(8,128)(2,1)} custom-call(f32[512,256]{1,0:T(8,128)S(1)} %get-tuple-element.66.refs_0_, f32[16,256]{1,0:T(8,128)S(1)} %collective-permute-done.12.refs_1_), custom_call_target="tpu_custom_call" | custom-call | tf_op jit(solution)/shard_map/pallas_call | solution.py:34
  50.9 0.7 %shard_map.124 = f32[128,512]{1,0:T(8,128)} custom-call(f32[1,128,512]{2,1,0:T(8,128)S(1)} %get-tuple-element.76.refs_0_, bf16[1,128,512]{2,1,0:T(8,128)(2,1)S(1)} %collective-permute-done.17.refs_1_), custom_call_target="tpu_custom_call" | custom-call | tf_op jit(solution)/shard_map/pallas_call | solution.py:34
  (30 shorter events, 3.8 us)
Async XLA Ops:
  0.6 9.5 %collective-permute-start.5 = (bf16[512,256]{1,0:T(8,128)(2,1)}, bf16[512,256]{1,0:T(8,128)(2,1)S(1)}, u32[]{:S(2)}, u32[]{:S(2)}) collective-permute-start(bf16[512,256]{1,0:T(8,128)(2,1)} %refs_0_.5), channel_id=1, source_target_pairs={{0,2},{1,3},{2,0},{3,1},{4,6},{5,7},{6,4},{7,5},{8,10},{9,11},{10,... | collective-permute-start | bytes 786440 | tf_op jit(solution)/shard_map/ppermute | solution.py:74
  3.6 14.0 %collective-permute-start.4 = (bf16[512,256]{1,0:T(8,128)(2,1)}, bf16[512,256]{1,0:T(8,128)(2,1)S(1)}, u32[]{:S(2)}, u32[]{:S(2)}) collective-permute-start(bf16[512,256]{1,0:T(8,128)(2,1)} %refs_0_.5), channel_id=1, source_target_pairs={{0,1},{1,0},{2,3},{3,2},{4,5},{5,4},{6,7},{7,6},{8,9},{9,8},{10,11... | collective-permute-start | bytes 786440 | tf_op jit(solution)/shard_map/ppermute | solution.py:74
  5.6 7.8 %collective-permute-start.2 = (bf16[144,512]{1,0:T(8,128)(2,1)S(1)}, bf16[144,512]{1,0:T(8,128)(2,1)S(1)}, u32[]{:S(2)}, u32[]{:S(2)}) collective-permute-start(bf16[144,512]{1,0:T(8,128)(2,1)S(1)} %get-tuple-element.40.refs_0_), channel_id=1, source_target_pairs={{0,12},{4,8},{8,4},{12,0},{16,28},{20,24},{24,20},{28,16},{1,13},{... | collective-permute-start | bytes 442376 | tf_op jit(solution)/shard_map/ppermute | solution.py:74
  8.2 7.9 %collective-permute-start.1 = (bf16[144,512]{1,0:T(8,128)(2,1)S(1)}, bf16[144,512]{1,0:T(8,128)(2,1)S(1)}, u32[]{:S(2)}, u32[]{:S(2)}) collective-permute-start(bf16[144,512]{1,0:T(8,128)(2,1)S(1)} %get-tuple-element.40.refs_0_), channel_id=1, source_target_pairs={{0,8},{4,12},{8,0},{12,4},{16,24},{20,28},{24,16},{28,20},{1,9},{5... | collective-permute-start | bytes 442376 | tf_op jit(solution)/shard_map/ppermute | solution.py:74
  8.7 7.4 %collective-permute-start = (bf16[144,512]{1,0:T(8,128)(2,1)S(1)}, bf16[144,512]{1,0:T(8,128)(2,1)S(1)}, u32[]{:S(2)}, u32[]{:S(2)}) collective-permute-start(bf16[144,512]{1,0:T(8,128)(2,1)S(1)} %get-tuple-element.40.refs_0_), channel_id=1, source_target_pairs={{0,4},{4,0},{8,12},{12,8},{16,20},{20,16},{24,28},{28,24},{1,5},{5... | collective-permute-start | bytes 442376 | tf_op jit(solution)/shard_map/ppermute | solution.py:74
  10.2 7.5 %collective-permute-start.6 = (bf16[512,256]{1,0:T(8,128)(2,1)S(1)}, bf16[512,256]{1,0:T(8,128)(2,1)S(1)}, u32[]{:S(2)}, u32[]{:S(2)}) collective-permute-start(bf16[512,256]{1,0:T(8,128)(2,1)S(1)} %collective-permute-done.5.refs_2_), channel_id=1, source_target_pairs={{0,1},{1,0},{2,3},{3,2},{4,5},{5,4},{6,7},{7,6},{8,9},{9,8},{10,11... | collective-permute-start | bytes 786440 | tf_op jit(solution)/shard_map/ppermute | solution.py:74
  10.2 0.7 %copy-start.2 = (f32[8]{0:T(128)S(1)}, f32[8]{0:T(128)}, u32[]{:S(2)}) copy-start(f32[8]{0:T(128)} %refs_0_.4) | copy-start | bytes 100
  16.1 1.6 %copy-start = (bf16[512,256]{1,0:T(8,128)(2,1)S(1)}, bf16[512,256]{1,0:T(8,128)(2,1)}, u32[]{:S(2)}) copy-start(bf16[512,256]{1,0:T(8,128)(2,1)} %refs_0_.5) | copy-start | bytes 786436
  16.4 10.9 %collective-permute-start.3 = (bf16[128,512]{1,0:T(8,128)(2,1)S(1)}, bf16[128,512]{1,0:T(8,128)(2,1)S(1)}, u32[]{:S(2)}, u32[]{:S(2)}) collective-permute-start(bf16[128,512]{1,0:T(8,128)(2,1)S(1)} %get-tuple-element.48), channel_id=1, source_target_pairs={{16,0},{20,4},{24,8},{28,12},{17,1},{21,5},{25,9},{29,13},{18,2},{... | collective-permute-start | bytes 393224 | tf_op jit(solution)/shard_map/ppermute | solution.py:74
  18.0 9.3 %collective-permute-start.7 = (bf16[4,16,256]{2,1,0:T(8,128)(2,1)S(1)}, bf16[4,16,256]{2,1,0:T(8,128)(2,1)S(1)}, u32[]{:S(2)}, u32[]{:S(2)}) collective-permute-start(bf16[4,16,256]{2,1,0:T(8,128)(2,1)S(1)} %get-tuple-element.53), channel_id=1, source_target_pairs={{0,4},{4,8},{8,12},{12,16},{16,20},{20,24},{24,28},{1,5},{5,9},{9,... | collective-permute-start | bytes 98312 | tf_op jit(solution)/shard_map/ppermute | solution.py:493
  27.3 3.6 %copy-start.1 = (bf16[1024,512]{1,0:T(8,128)(2,1)S(1)}, bf16[1024,512]{1,0:T(8,128)(2,1)}, u32[]{:S(2)}) copy-start(bf16[1024,512]{1,0:T(8,128)(2,1)} %refs_1_.3) | copy-start | bytes 3145732
  29.3 7.3 %collective-permute-start.13 = (bf16[4,128,256]{2,1,0:T(8,128)(2,1)S(1)}, bf16[4,128,256]{2,1,0:T(8,128)(2,1)S(1)}, u32[]{:S(2)}, u32[]{:S(2)}) collective-permute-start(bf16[4,128,256]{2,1,0:T(8,128)(2,1)S(1)} %get-tuple-element.69), channel_id=1, source_target_pairs={{0,4},{4,0},{8,12},{12,8},{16,20},{20,16},{24,28},{28,24},{1,5},{5... | collective-permute-start | bytes 786440 | tf_op jit(solution)/shard_map/ppermute | solution.py:74
  30.8 7.1 %collective-permute-start.14 = (bf16[4,128,256]{2,1,0:T(8,128)(2,1)S(1)}, bf16[4,128,256]{2,1,0:T(8,128)(2,1)S(1)}, u32[]{:S(2)}, u32[]{:S(2)}) collective-permute-start(bf16[4,128,256]{2,1,0:T(8,128)(2,1)S(1)} %get-tuple-element.71), channel_id=1, source_target_pairs={{0,8},{4,12},{8,0},{12,4},{16,24},{20,28},{24,16},{28,20},{1,9},{5... | collective-permute-start | bytes 786440 | tf_op jit(solution)/shard_map/ppermute | solution.py:74
  31.6 1.5 %collective-permute-start.8 = (bf16[352,256]{1,0:T(8,128)(2,1)S(1)}, bf16[352,256]{1,0:T(8,128)(2,1)S(1)}, u32[]{:S(2)}, u32[]{:S(2)}) collective-permute-start(bf16[352,256]{1,0:T(8,128)(2,1)S(1)} %get-tuple-element.61), channel_id=1, source_target_pairs={{0,1},{1,0},{2,3},{3,2},{4,5},{5,4},{6,7},{7,6},{8,9},{9,8},{10,11... | collective-permute-start | bytes 540680 | tf_op jit(solution)/shard_map/ppermute | solution.py:74
  31.7 1.7 %collective-permute-start.9 = (bf16[352,256]{1,0:T(8,128)(2,1)S(1)}, bf16[352,256]{1,0:T(8,128)(2,1)S(1)}, u32[]{:S(2)}, u32[]{:S(2)}) collective-permute-start(bf16[352,256]{1,0:T(8,128)(2,1)S(1)} %get-tuple-element.62), channel_id=1, source_target_pairs={{0,1},{1,0},{2,3},{3,2},{4,5},{5,4},{6,7},{7,6},{8,9},{9,8},{10,11... | collective-permute-start | bytes 540680 | tf_op jit(solution)/shard_map/ppermute | solution.py:74
  32.2 1.4 %collective-permute-start.10 = (bf16[352,256]{1,0:T(8,128)(2,1)S(1)}, bf16[352,256]{1,0:T(8,128)(2,1)S(1)}, u32[]{:S(2)}, u32[]{:S(2)}) collective-permute-start(bf16[352,256]{1,0:T(8,128)(2,1)S(1)} %get-tuple-element.63), channel_id=1, source_target_pairs={{0,1},{1,0},{2,3},{3,2},{4,5},{5,4},{6,7},{7,6},{8,9},{9,8},{10,11... | collective-permute-start | bytes 540680 | tf_op jit(solution)/shard_map/ppermute | solution.py:74
  33.7 10.5 %collective-permute-start.11 = (bf16[528,256]{1,0:T(8,128)(2,1)S(1)}, bf16[528,256]{1,0:T(8,128)(2,1)S(1)}, u32[]{:S(2)}, u32[]{:S(2)}) collective-permute-start(bf16[528,256]{1,0:T(8,128)(2,1)S(1)} %get-tuple-element.65), channel_id=1, source_target_pairs={{0,2},{1,3},{2,0},{3,1},{4,6},{5,7},{6,4},{7,5},{8,10},{9,11},{10,... | collective-permute-start | bytes 811016 | tf_op jit(solution)/shard_map/ppermute | solution.py:74
  38.0 5.0 %collective-permute-start.15 = (bf16[2,128,256]{2,1,0:T(8,128)(2,1)S(1)}, bf16[2,128,256]{2,1,0:T(8,128)(2,1)S(1)}, u32[]{:S(2)}, u32[]{:S(2)}) collective-permute-start(bf16[2,128,256]{2,1,0:T(8,128)(2,1)S(1)} %get-tuple-element.73), channel_id=1, source_target_pairs={{0,8},{4,12},{8,0},{12,4},{16,24},{20,28},{24,16},{28,20},{1,9},{5... | collective-permute-start | bytes 393224 | tf_op jit(solution)/shard_map/ppermute | solution.py:74
  38.4 5.0 %collective-permute-start.16 = (bf16[2,128,256]{2,1,0:T(8,128)(2,1)S(1)}, bf16[2,128,256]{2,1,0:T(8,128)(2,1)S(1)}, u32[]{:S(2)}, u32[]{:S(2)}) collective-permute-start(bf16[2,128,256]{2,1,0:T(8,128)(2,1)S(1)} %get-tuple-element.75), channel_id=1, source_target_pairs={{0,4},{4,0},{8,12},{12,8},{16,20},{20,16},{24,28},{28,24},{1,5},{5... | collective-permute-start | bytes 393224 | tf_op jit(solution)/shard_map/ppermute | solution.py:74
  43.4 7.5 %collective-permute-start.17 = (bf16[1,128,512]{2,1,0:T(8,128)(2,1)S(1)}, bf16[1,128,512]{2,1,0:T(8,128)(2,1)S(1)}, u32[]{:S(2)}, u32[]{:S(2)}) collective-permute-start(bf16[1,128,512]{2,1,0:T(8,128)(2,1)S(1)} %get-tuple-element.77), channel_id=1, source_target_pairs={{0,16},{4,20},{8,24},{12,28},{16,0},{20,4},{24,8},{28,12},{1,17},{... | collective-permute-start | bytes 393224 | tf_op jit(solution)/shard_map/ppermute | solution.py:74
  44.2 5.6 %collective-permute-start.12 = (f32[16,256]{1,0:T(8,128)S(1)}, f32[16,256]{1,0:T(8,128)S(1)}, u32[]{:S(2)}, u32[]{:S(2)}) collective-permute-start(f32[16,256]{1,0:T(8,128)S(1)} %get-tuple-element.67), channel_id=1, source_target_pairs={{4,0},{8,4},{12,8},{16,12},{20,16},{24,20},{28,24},{5,1},{9,5},{13... | collective-permute-start | bytes 49160 | tf_op jit(solution)/shard_map/ppermute | solution.py:573

commit v3 on v1

--- a/solution.py
+++ b/solution.py
@@ -194,7 +194,10 @@
     states, decays = [a for a, _ in pairs], [b for _, b in pairs]
     places = [origin(digit, radix, hop) for hop in range(radix)]
     whole, whole_span = later_sum(-1, places, states, decays)
-    pack_state(next_ref, whole, whole_span)
+    if next_ref.shape[0] > whole.shape[0]:
+        pack_state(next_ref, whole, whole_span)
+    else:
+        next_ref[...] = whole.astype(BF16)
     later, span = later_sum(digit, places[1:], states[1:], decays[1:])
     if not first:
         held, reach = kept_state(refs[radix - 1])
@@ -262,26 +265,30 @@
 
 
 def turn_body(members, *refs):
-    pieces, turned, ends_ref = refs[:members], refs[members : 2 * members], refs[-1]
+    pieces, turned_ref, ends_ref = refs[:members], refs[members], refs[-1]
+    length, features = pieces[0].shape
     for hop in range(members):
-        ends_ref[hop] = pieces[hop][pieces[hop].shape[0] - PAD :, :]
-    for hop in range(members):
-        turned[hop][...] = pieces[hop][...].T
+        source = origin(lax.axis_index("tensor"), members, hop)
+        ends_ref[source] = pieces[hop][length - PAD :, :]
+        start = pl.multiple_of(source * features, features)
+        turned_ref[pl.ds(start, features), :] = pieces[hop][...].T
 
 
 def tail_body(radix, stride, first, members, chunk, *refs):
     received, refs = refs[: radix - 1], refs[radix - 1 :]
     if not first:
         held_ref, refs = refs[0], refs[1:]
-    states_ref, base_ref, coef_ref, input_ref, taps_ref, ends_ref = refs[:6]
-    layer_refs = refs[6 : 6 + members]
-    keep_near, send_near, keep_far, send_far, grads_ref, conv_ref = refs[6 + members :]
+    states_ref, base_ref, coef_ref, input_ref, taps_ref, ends_ref, layer_ref = refs[:7]
+    send_near, send_far, grads_ref, turned_ref, conv_ref = refs[7:]
     length, width = base_ref.shape
     place = lax.axis_index("context")
     digit = place // stride % radix
-    pairs = [unpack_state(ref) for ref in received]
-    places = [origin(digit, radix, hop) for hop in range(1, radix)]
-    carry, _ = later_sum(digit, places, [a for a, _ in pairs], [b for _, b in pairs])
+    if radix == 2:
+        carry = jnp.where(digit == 0, received[0][...].astype(F32), 0.0)
+    else:
+        pairs = [unpack_state(ref) for ref in received]
+        places = [origin(digit, radix, hop) for hop in range(1, radix)]
+        carry, _ = later_sum(digit, places, [a for a, _ in pairs], [b for _, b in pairs])
     if not first:
         held, reach = kept_state(held_ref)
         carry = held + jnp.exp(reach) * carry
@@ -301,28 +308,30 @@
         term = taps_ref[offset : offset + 1, :] * conv_ref[shift : shift + PAD + length, :]
         total = term if total is None else total + term
     grads_ref[...] = total.astype(BF16)
-    features = layer_refs[0].shape[0]
-    per_piece = features // chunk
-    me = lax.axis_index("tensor")
-    half = width // 2
-
-    def put(keep, send, same, index, value):
-        @pl.when(same)
-        def _():
-            keep[index] = value
-
-        @pl.when(jnp.logical_not(same))
-        def _():
-            send[index] = value.astype(BF16)
-
-    for hop in range(members):
-        source = origin(me, members, hop)
-        product = dot(layer_refs[hop][...], grads_ref[PAD:, :], (1, 0)) + dot(ends_ref[hop], grads_ref[:PAD, :], (0, 0))
-        for index in range(per_piece):
-            number = source * per_piece + index
-            rows = product[index * chunk : (index + 1) * chunk, :]
-            put(keep_near, send_near, (number & 1) == (place & 1), number >> 1, rows[:, :half])
-            put(keep_far, send_far, (number & 2) == (place & 2), (number & 1) + ((number >> 2) << 1), rows[:, half:])
+    features = ends_ref.shape[2]
+    for index in range(members):
+        turned_ref[index * features : (index + 1) * features, :] = ends_ref[index].T
+    products(chunk, 1, layer_ref, turned_ref, grads_ref, send_near, send_far)
+
+
+def products(chunk, flip, layer_ref, turned_ref, grads_ref, near_ref, far_ref):
+    place = lax.axis_index("context")
+    near_bit, far_bit = (place & 1) ^ flip, ((place >> 1) & 1) ^ flip
+    half = near_ref.shape[2]
+    for channels, out_ref, number in (
+        (slice(0, half), near_ref, lambda i: 2 * i + near_bit),
+        (slice(half, 2 * half), far_ref, lambda i: (i & 1) + ((i >> 1) << 2) + 2 * far_bit),
+    ):
+        starts = [pl.multiple_of(number(i) * chunk, chunk) for i in range(out_ref.shape[0])]
+        layers = jnp.concatenate([layer_ref[pl.ds(start, chunk), :] for start in starts], axis=0)
+        ends = jnp.concatenate([turned_ref[pl.ds(start, chunk), :] for start in starts], axis=0)
+        product = dot(layers, grads_ref[PAD:, channels], (1, 0)) + dot(ends, grads_ref[:PAD, channels], (1, 0))
+        for i in range(out_ref.shape[0]):
+            out_ref[i] = product[i * chunk : (i + 1) * chunk, :].astype(out_ref.dtype)
+
+
+def kept_body(chunk, layer_ref, turned_ref, grads_ref, keep_near, keep_far):
+    products(chunk, 0, layer_ref, turned_ref, grads_ref, keep_near, keep_far)
 
 
 def overlaps(index, high, sizes):
@@ -453,17 +462,19 @@
         last = stride * radix == spans_of
         received = [swap(payload, "context", stride, radix, hop, last) for hop in range(1, radix)]
         if not last:
+            following = stages[stages.index(radix) + 1] if len(stages) == 2 else 4
+            rows = state_width if following == 2 else state_width + PAD
             payload, *held = call(
                 functools.partial(merge_body, radix, stride, not held),
-                [(payload.shape, BF16), ((state_width + ROW, width), F32)],
+                [((rows, width), BF16), ((state_width + ROW, width), F32)],
                 [payload, *received, *held, base],
                 idle=1,
             )
             stride *= radix
 
-    *layers, ends = call(
+    turned, ends = call(
         functools.partial(turn_body, members),
-        [((features, length), BF16)] * members + [((members, PAD, features), BF16)],
+        [((members * features, length), BF16), ((members, PAD, features), BF16)],
         layers,
         moved=2 * members * features * length,
     )
@@ -473,14 +484,21 @@
     chunk = total_rows // spans_of
     scaling = 1.0 / math.sqrt(length * spans_of)
     split_shape = (spans_of // 2, chunk, width // 2)
-    keep_near, send_near, keep_far, send_far, grads = call(
+    send_near, send_far, grads, turned_ends = call(
         functools.partial(tail_body, stages[-1], stride, not held, members, chunk),
-        [(split_shape, F32), (split_shape, BF16), (split_shape, F32), (split_shape, BF16), ((PAD + length, width), BF16)],
-        [*received, *held, states, base, coef, input_here, taps_here, ends, *layers],
+        [(split_shape, BF16), (split_shape, BF16), ((PAD + length, width), BF16), ((total_rows, PAD), BF16)],
+        [*received, *held, states, base, coef, input_here, taps_here, ends, turned],
         scratch=[pltpu.VMEM((length + 2 * PAD, width), F32)],
         flops=2 * length * width * total_rows,
         moved=16 * length * width,
         vmem=16,
+    )
+    keep_near, keep_far = call(
+        functools.partial(kept_body, chunk),
+        [(split_shape, F32), (split_shape, F32)],
+        [turned, turned_ends, grads],
+        flops=length * width * total_rows,
+        moved=8 * length * width,
     )
 
     got_near = swap(send_near, "context", 1, 2, 1)

time: 53.2 us -> 50.1 us (0.942)
  waiting for transfers between devices: 25.7 us -> 19.7 us
  starting transfers between devices: 16.1 us -> 19.7 us
  Pallas kernels: 9.72 us -> 9.05 us
    ppermute x16, waiting for transfers between devices: 21.3 us -> 15.3 us  [swap(): return lax.ppermute(value, axis, pairs)]
    ppermute x16, starting transfers between devices: 11.5 us -> 15.1 us  [swap(): return lax.ppermute(value, axis, pairs)]
    pallas_call x11 -> x12, Pallas kernels: 9.72 us -> 9.05 us  [call(): pl.pallas_call(run, out_shape=[jax.ShapeDtypeStruct(shape, kind) for shap...]
  transfers between devices with their start and end apart: 18 -> 18, of which waited for: 12 -> 13; matrix products, arithmetic and copies ran while one was open for 0% -> 0% of each run, Pallas kernels for 12% -> 14%
where the time goes in v3:
time: 50.1 us; the launch traced here: 49.9 us
  starting transfers between devices  19.7 us (39%)
  waiting for transfers between devices  19.7 us (39%)
  Pallas kernels  9.05 us (18%)
  between operations  0.78 us (2%)
  local copies, waits for them, and re-layouts  0.66 us (1%)
    ppermute x16, waiting for transfers between devices, swap(): return lax.ppermute(value, axis, pairs)  15.3 us
    ppermute x16, starting transfers between devices, swap(): return lax.ppermute(value, axis, pairs)  15.1 us
    pallas_call x12, Pallas kernels, call(): pl.pallas_call(run, out_shape=[jax.ShapeDtypeStruct(shape, kind) for shap...  9.05 us
    ppermute x1, waiting for transfers between devices, local(): lax.ppermute(head, 'context', [(i + 1, i) for i in range(spans_of - 1)])  4.33 us
    ppermute x1, starting transfers between devices, local(): lax.ppermute(ends, 'context', [(i, i + 1) for i in range(spans_of - 1)])  3.31 us
    ppermute x1, starting transfers between devices, local(): lax.ppermute(head, 'context', [(i + 1, i) for i in range(spans_of - 1)])  1.29 us
  transfers between devices with their start and end apart: 18, of which 13 were waited for; matrix products, arithmetic and copies ran while one was open for 0% of the time, Pallas kernels for 14%

profile of v3, /device:TPU:0, one launch (start us, length us, event | category | flops | bytes accessed | tf_op | source)
XLA Modules:
  0.0 49.9 jit_solution(12783873771928128083)
XLA Ops:
  0.6 3.0 %collective-permute-start.1 = (bf16[512,256]{1,0:T(8,128)(2,1)}, bf16[512,256]{1,0:T(8,128)(2,1)S(1)}, u32[]{:S(2)}, u32[]{:S(2)}) collective-permute-start(bf16[512,256]{1,0:T(8,128)(2,1)} %refs_0_.3), channel_id=1, source_target_pairs={{0,2},{1,3},{2,0},{3,1},{4,6},{5,7},{6,4},{7,5},{8,10},{9,11},{10,... | collective-permute-start | bytes 786440 | tf_op jit(solution)/shard_map/ppermute | solution.py:74
  3.6 2.0 %shard_map.114 = (bf16[144,512]{1,0:T(8,128)(2,1)S(1)}, f32[2,136,512]{2,1,0:T(8,128)S(1)}, bf16[512,512]{1,0:T(8,128)(2,1)S(1)}, bf16[512,128]{1,0:T(8,128)(2,1...) custom-call(bf16[512,512]{1,0:T(8,128)(2,1)} %refs_0_.4, ...), custom_call_target="tpu_custom_call" | custom-call | flops 67108864 | bytes 524288 | tf_op jit(solution)/shard_map/pallas_call | solution.py:34
  5.6 1.6 %collective-permute-start.3 = (bf16[144,512]{1,0:T(8,128)(2,1)S(1)}, bf16[144,512]{1,0:T(8,128)(2,1)S(1)}, u32[]{:S(2)}, u32[]{:S(2)}) collective-permute-start(bf16[144,512]{1,0:T(8,128)(2,1)S(1)} %get-tuple-element.41.refs_0_), channel_id=1, source_target_pairs={{0,4},{4,0},{8,12},{12,8},{16,20},{20,16},{24,28},{28,24},{1,5},{5... | collective-permute-start | bytes 442376 | tf_op jit(solution)/shard_map/ppermute | solution.py:74
  7.2 1.6 %collective-permute-start.4 = (bf16[144,512]{1,0:T(8,128)(2,1)S(1)}, bf16[144,512]{1,0:T(8,128)(2,1)S(1)}, u32[]{:S(2)}, u32[]{:S(2)}) collective-permute-start(bf16[144,512]{1,0:T(8,128)(2,1)S(1)} %get-tuple-element.41.refs_0_), channel_id=1, source_target_pairs={{0,8},{4,12},{8,0},{12,4},{16,24},{20,28},{24,16},{28,20},{1,9},{5... | collective-permute-start | bytes 442376 | tf_op jit(solution)/shard_map/ppermute | solution.py:74
  9.2 1.0 %collective-permute-done.1.refs_2_ = bf16[512,256]{1,0:T(8,128)(2,1)S(1)} collective-permute-done((bf16[512,256]{1,0:T(8,128)(2,1)}, bf16[512,256]{1,0:T(8,128)(2,1)S(1)}, u32[]{:S(2)}, u32[]{:S(2)}) %collective-permute-start.1) | collective-permute-done | bytes 262176 | tf_op jit(solution)/shard_map/ppermute | solution.py:74
  10.8 2.7 %shard_map.115 = (f32[512,512]{1,0:T(8,128)S(1)}, f32[512,512]{1,0:T(8,128)S(1)}) custom-call(f32[8]{0:T(128)S(1)} %copy-done.2, bf16[512,128]{1,0:T(8,128)(2,1)S(1)} %get-tuple-element.42.refs_1_.refs_5_, bf16[512,128]{1,0:T(8,128)(2,1)S(1)} %get-tuple-element.43.refs_2_, bf16[512,512]{1,0:T(8,128)(2,1)S(1)} %get-tuple-element.44.refs_3_, ...), custom_call_target="tpu_custom_call" | custom-call | flops 34359738368 | bytes 3145728 | tf_op jit(solution)/shard_map/pallas_call | solution.py:34
  13.8 1.6 %collective-permute-done.5.refs_3_ = bf16[144,512]{1,0:T(8,128)(2,1)S(1)} collective-permute-done((bf16[144,512]{1,0:T(8,128)(2,1)S(1)}, bf16[144,512]{1,0:T(8,128)(2,1)S(1)}, u32[]{:S(2)}, u32[]{:S(2)}) %collective-permute-start.5) | collective-permute-done | bytes 147488 | tf_op jit(solution)/shard_map/ppermute | solution.py:74
  15.7 1.3 %collective-permute-start.6 = (bf16[128,512]{1,0:T(8,128)(2,1)S(1)}, bf16[128,512]{1,0:T(8,128)(2,1)S(1)}, u32[]{:S(2)}, u32[]{:S(2)}) collective-permute-start(bf16[128,512]{1,0:T(8,128)(2,1)S(1)} %get-tuple-element.49), channel_id=1, source_target_pairs={{16,0},{20,4},{24,8},{28,12},{17,1},{21,5},{25,9},{29,13},{18,2},{... | collective-permute-start | bytes 393224 | tf_op jit(solution)/shard_map/ppermute | solution.py:74
  17.4 3.3 %collective-permute-start.7 = (bf16[4,16,256]{2,1,0:T(8,128)(2,1)S(1)}, bf16[4,16,256]{2,1,0:T(8,128)(2,1)S(1)}, u32[]{:S(2)}, u32[]{:S(2)}) collective-permute-start(bf16[4,16,256]{2,1,0:T(8,128)(2,1)S(1)} %get-tuple-element.54), channel_id=1, source_target_pairs={{0,4},{4,8},{8,12},{12,16},{16,20},{20,24},{24,28},{1,5},{5,9},{9,... | collective-permute-start | bytes 98312 | tf_op jit(solution)/shard_map/ppermute | solution.py:481
  20.7 5.1 %collective-permute-done.6.refs_0_ = bf16[128,512]{1,0:T(8,128)(2,1)S(1)} collective-permute-done((bf16[128,512]{1,0:T(8,128)(2,1)S(1)}, bf16[128,512]{1,0:T(8,128)(2,1)S(1)}, u32[]{:S(2)}, u32[]{:S(2)}) %collective-permute-start.6) | collective-permute-done | bytes 131104 | tf_op jit(solution)/shard_map/ppermute | solution.py:74
  25.7 1.4 %shard_map.117 = (bf16[4,128,256]{2,1,0:T(8,128)(2,1)S(1)}, bf16[4,128,256]{2,1,0:T(8,128)(2,1)S(1)}, bf16[528,512]{1,0:T(8,128)(2,1)S(1)}, bf16[1024,16]{1,0:T(8,128)(2,1)S(1)}) custom-call(bf16[128,512]{1,0:T(8,128)(2,1)S(1)} %collective-permute-done.6.refs_0_, f32[136,512]{1,0:T(8,128)S(1)} %get-tuple-element.50.refs_1_, ...), custom_call_target="tpu_custom_call" | custom-call | flops 536870912 | bytes 4194304 | tf_op jit(solution)/shard_map/pallas_call | solution.py:34
  27.2 1.4 %collective-permute-start.8 = (bf16[4,128,256]{2,1,0:T(8,128)(2,1)S(1)}, bf16[4,128,256]{2,1,0:T(8,128)(2,1)S(1)}, u32[]{:S(2)}, u32[]{:S(2)}) collective-permute-start(bf16[4,128,256]{2,1,0:T(8,128)(2,1)S(1)} %get-tuple-element.58), channel_id=1, source_target_pairs={{0,4},{4,0},{8,12},{12,8},{16,20},{20,16},{24,28},{28,24},{1,5},{5... | collective-permute-start | bytes 786440 | tf_op jit(solution)/shard_map/ppermute | solution.py:74
  28.5 0.8 %shard_map.121 = (f32[528,256]{1,0:T(8,128)S(1)}, f32[528,256]{1,0:T(8,128)S(1)}, bf16[352,256]{1,0:T(8,128)(2,1)S(1)}, bf16[352,256]{1,0:T(8,128)(2,1)S(1)}, bf16[352,256]{1,0:T(8,128)(2,1)S(1)}) custom-call(bf16[528,512]{1,0:T(8,128)(2,1)S(1)} %get-tuple-element.56.refs_2_.refs_0_, bf16[1024,512]{1,0:T(8,128)(2,1)S(1)} %copy-done.1), custom_call_target="tpu_custom_call" | custom-call | flops 536870912 | bytes 2097152 | tf_op jit(solution)/shard_map/pallas_call | solution.py:34
  30.0 0.8 %collective-permute-done.13.refs_2_ = bf16[352,256]{1,0:T(8,128)(2,1)S(1)} collective-permute-done((bf16[352,256]{1,0:T(8,128)(2,1)S(1)}, bf16[352,256]{1,0:T(8,128)(2,1)S(1)}, u32[]{:S(2)}, u32[]{:S(2)}) %collective-permute-start.13) | collective-permute-done | bytes 180256 | tf_op jit(solution)/shard_map/ppermute | solution.py:74
  31.4 1.6 %collective-permute-start.16 = (bf16[528,256]{1,0:T(8,128)(2,1)S(1)}, bf16[528,256]{1,0:T(8,128)(2,1)S(1)}, u32[]{:S(2)}, u32[]{:S(2)}) collective-permute-start(bf16[528,256]{1,0:T(8,128)(2,1)S(1)} %get-tuple-element.73), channel_id=1, source_target_pairs={{0,2},{1,3},{2,0},{3,1},{4,6},{5,7},{6,4},{7,5},{8,10},{9,11},{10,... | collective-permute-start | bytes 811016 | tf_op jit(solution)/shard_map/ppermute | solution.py:74
  33.5 1.1 %collective-permute-done.8.refs_1_ = bf16[4,128,256]{2,1,0:T(8,128)(2,1)S(1)} collective-permute-done((bf16[4,128,256]{2,1,0:T(8,128)(2,1)S(1)}, bf16[4,128,256]{2,1,0:T(8,128)(2,1)S(1)}, u32[]{:S(2)}, u32[]{:S(2)}) %collective-permute-start.8) | collective-permute-done | bytes 262176 | tf_op jit(solution)/shard_map/ppermute | solution.py:74
  35.0 0.8 %collective-permute-start.10 = (bf16[2,128,256]{2,1,0:T(8,128)(2,1)S(1)}, bf16[2,128,256]{2,1,0:T(8,128)(2,1)S(1)}, u32[]{:S(2)}, u32[]{:S(2)}) collective-permute-start(bf16[2,128,256]{2,1,0:T(8,128)(2,1)S(1)} %get-tuple-element.62), channel_id=1, source_target_pairs={{0,8},{4,12},{8,0},{12,4},{16,24},{20,28},{24,16},{28,20},{1,9},{5... | collective-permute-start | bytes 393224 | tf_op jit(solution)/shard_map/ppermute | solution.py:74
  35.7 1.0 %collective-permute-start.11 = (bf16[2,128,256]{2,1,0:T(8,128)(2,1)S(1)}, bf16[2,128,256]{2,1,0:T(8,128)(2,1)S(1)}, u32[]{:S(2)}, u32[]{:S(2)}) collective-permute-start(bf16[2,128,256]{2,1,0:T(8,128)(2,1)S(1)} %get-tuple-element.64), channel_id=1, source_target_pairs={{0,4},{4,0},{8,12},{12,8},{16,20},{20,16},{24,28},{28,24},{1,5},{5... | collective-permute-start | bytes 393224 | tf_op jit(solution)/shard_map/ppermute | solution.py:74
  36.8 3.3 %collective-permute-done.10.refs_1_ = bf16[2,128,256]{2,1,0:T(8,128)(2,1)S(1)} collective-permute-done((bf16[2,128,256]{2,1,0:T(8,128)(2,1)S(1)}, bf16[2,128,256]{2,1,0:T(8,128)(2,1)S(1)}, u32[]{:S(2)}, u32[]{:S(2)}) %collective-permute-start.10) | collective-permute-done | bytes 131104 | tf_op jit(solution)/shard_map/ppermute | solution.py:74
  40.0 0.8 %collective-permute-done.11.refs_3_ = bf16[2,128,256]{2,1,0:T(8,128)(2,1)S(1)} collective-permute-done((bf16[2,128,256]{2,1,0:T(8,128)(2,1)S(1)}, bf16[2,128,256]{2,1,0:T(8,128)(2,1)S(1)}, u32[]{:S(2)}, u32[]{:S(2)}) %collective-permute-start.11) | collective-permute-done | bytes 131104 | tf_op jit(solution)/shard_map/ppermute | solution.py:74
  40.9 1.9 %collective-permute-start.12 = (bf16[1,128,512]{2,1,0:T(8,128)(2,1)S(1)}, bf16[1,128,512]{2,1,0:T(8,128)(2,1)S(1)}, u32[]{:S(2)}, u32[]{:S(2)}) collective-permute-start(bf16[1,128,512]{2,1,0:T(8,128)(2,1)S(1)} %get-tuple-element.66), channel_id=1, source_target_pairs={{0,16},{4,20},{8,24},{12,28},{16,0},{20,4},{24,8},{28,12},{1,17},{... | collective-permute-start | bytes 393224 | tf_op jit(solution)/shard_map/ppermute | solution.py:74
  42.8 1.3 %collective-permute-start.17 = (f32[16,256]{1,0:T(8,128)S(1)}, f32[16,256]{1,0:T(8,128)S(1)}, u32[]{:S(2)}, u32[]{:S(2)}) collective-permute-start(f32[16,256]{1,0:T(8,128)S(1)} %get-tuple-element.75), channel_id=1, source_target_pairs={{4,0},{8,4},{12,8},{16,12},{20,16},{24,20},{28,24},{5,1},{9,5},{13... | collective-permute-start | bytes 49160 | tf_op jit(solution)/shard_map/ppermute | solution.py:568
  44.1 4.3 %collective-permute-done.17.refs_3_ = f32[16,256]{1,0:T(8,128)S(1)} collective-permute-done((f32[16,256]{1,0:T(8,128)S(1)}, f32[16,256]{1,0:T(8,128)S(1)}, u32[]{:S(2)}, u32[]{:S(2)}) %collective-permute-start.17) | collective-permute-done | bytes 16416 | tf_op jit(solution)/shard_map/ppermute | solution.py:568
  49.0 0.8 %shard_map.124 = (f32[128,512]{1,0:T(8,128)}, bf16[512,256]{1,0:T(8,128)(2,1)}) custom-call(f32[1,128,512]{2,1,0:T(8,128)S(1)} %get-tuple-element.65.refs_0_, bf16[1,128,512]{2,1,0:T(8,128)(2,1)S(1)} %collective-permute-done.12.refs_1_, f32[512,256]{1,0:T(8,128)S(1)} %get-tuple-element.74.refs_2_, f32[16,256]{1,0:T(8,128)S(1)} %collective-permute-done.17.refs_3_), custom_call_target="tpu_custom_call" | custom-call | tf_op jit(solution)/shard_map/pallas_call | solution.py:34
  (30 shorter events, 4.8 us)
Async XLA Ops:
  0.6 8.6 %copy-start = (bf16[512,256]{1,0:T(8,128)(2,1)S(1)}, bf16[512,256]{1,0:T(8,128)(2,1)}, u32[]{:S(2)}) copy-start(bf16[512,256]{1,0:T(8,128)(2,1)} %refs_0_.3) | copy-start | bytes 786436
  0.6 9.5 %collective-permute-start.1 = (bf16[512,256]{1,0:T(8,128)(2,1)}, bf16[512,256]{1,0:T(8,128)(2,1)S(1)}, u32[]{:S(2)}, u32[]{:S(2)}) collective-permute-start(bf16[512,256]{1,0:T(8,128)(2,1)} %refs_0_.3), channel_id=1, source_target_pairs={{0,2},{1,3},{2,0},{3,1},{4,6},{5,7},{6,4},{7,5},{8,10},{9,11},{10,... | collective-permute-start | bytes 786440 | tf_op jit(solution)/shard_map/ppermute | solution.py:74
  5.6 7.8 %collective-permute-start.3 = (bf16[144,512]{1,0:T(8,128)(2,1)S(1)}, bf16[144,512]{1,0:T(8,128)(2,1)S(1)}, u32[]{:S(2)}, u32[]{:S(2)}) collective-permute-start(bf16[144,512]{1,0:T(8,128)(2,1)S(1)} %get-tuple-element.41.refs_0_), channel_id=1, source_target_pairs={{0,4},{4,0},{8,12},{12,8},{16,20},{20,16},{24,28},{28,24},{1,5},{5... | collective-permute-start | bytes 442376 | tf_op jit(solution)/shard_map/ppermute | solution.py:74
  7.2 6.6 %collective-permute-start.4 = (bf16[144,512]{1,0:T(8,128)(2,1)S(1)}, bf16[144,512]{1,0:T(8,128)(2,1)S(1)}, u32[]{:S(2)}, u32[]{:S(2)}) collective-permute-start(bf16[144,512]{1,0:T(8,128)(2,1)S(1)} %get-tuple-element.41.refs_0_), channel_id=1, source_target_pairs={{0,8},{4,12},{8,0},{12,4},{16,24},{20,28},{24,16},{28,20},{1,9},{5... | collective-permute-start | bytes 442376 | tf_op jit(solution)/shard_map/ppermute | solution.py:74
  8.8 6.7 %collective-permute-start.5 = (bf16[144,512]{1,0:T(8,128)(2,1)S(1)}, bf16[144,512]{1,0:T(8,128)(2,1)S(1)}, u32[]{:S(2)}, u32[]{:S(2)}) collective-permute-start(bf16[144,512]{1,0:T(8,128)(2,1)S(1)} %get-tuple-element.41.refs_0_), channel_id=1, source_target_pairs={{0,12},{4,8},{8,4},{12,0},{16,28},{20,24},{24,20},{28,16},{1,13},{... | collective-permute-start | bytes 442376 | tf_op jit(solution)/shard_map/ppermute | solution.py:74
  9.2 7.8 %collective-permute-start = (bf16[512,256]{1,0:T(8,128)(2,1)S(1)}, bf16[512,256]{1,0:T(8,128)(2,1)S(1)}, u32[]{:S(2)}, u32[]{:S(2)}) collective-permute-start(bf16[512,256]{1,0:T(8,128)(2,1)S(1)} %copy-done), channel_id=1, source_target_pairs={{0,1},{1,0},{2,3},{3,2},{4,5},{5,4},{6,7},{7,6},{8,9},{9,8},{10,11... | collective-permute-start | bytes 786440 | tf_op jit(solution)/shard_map/ppermute | solution.py:74
  10.2 6.9 %collective-permute-start.2 = (bf16[512,256]{1,0:T(8,128)(2,1)S(1)}, bf16[512,256]{1,0:T(8,128)(2,1)S(1)}, u32[]{:S(2)}, u32[]{:S(2)}) collective-permute-start(bf16[512,256]{1,0:T(8,128)(2,1)S(1)} %collective-permute-done.1.refs_2_), channel_id=1, source_target_pairs={{0,1},{1,0},{2,3},{3,2},{4,5},{5,4},{6,7},{7,6},{8,9},{9,8},{10,11... | collective-permute-start | bytes 786440 | tf_op jit(solution)/shard_map/ppermute | solution.py:74
  10.2 0.7 %copy-start.2 = (f32[8]{0:T(128)S(1)}, f32[8]{0:T(128)}, u32[]{:S(2)}) copy-start(f32[8]{0:T(128)} %refs_0_.5) | copy-start | bytes 100
  15.7 10.0 %collective-permute-start.6 = (bf16[128,512]{1,0:T(8,128)(2,1)S(1)}, bf16[128,512]{1,0:T(8,128)(2,1)S(1)}, u32[]{:S(2)}, u32[]{:S(2)}) collective-permute-start(bf16[128,512]{1,0:T(8,128)(2,1)S(1)} %get-tuple-element.49), channel_id=1, source_target_pairs={{16,0},{20,4},{24,8},{28,12},{17,1},{21,5},{25,9},{29,13},{18,2},{... | collective-permute-start | bytes 393224 | tf_op jit(solution)/shard_map/ppermute | solution.py:74
  17.4 8.4 %collective-permute-start.7 = (bf16[4,16,256]{2,1,0:T(8,128)(2,1)S(1)}, bf16[4,16,256]{2,1,0:T(8,128)(2,1)S(1)}, u32[]{:S(2)}, u32[]{:S(2)}) collective-permute-start(bf16[4,16,256]{2,1,0:T(8,128)(2,1)S(1)} %get-tuple-element.54), channel_id=1, source_target_pairs={{0,4},{4,8},{8,12},{12,16},{16,20},{20,24},{24,28},{1,5},{5,9},{9,... | collective-permute-start | bytes 98312 | tf_op jit(solution)/shard_map/ppermute | solution.py:481
  25.7 2.8 %copy-start.1 = (bf16[1024,512]{1,0:T(8,128)(2,1)S(1)}, bf16[1024,512]{1,0:T(8,128)(2,1)}, u32[]{:S(2)}) copy-start(bf16[1024,512]{1,0:T(8,128)(2,1)} %refs_1_.3) | copy-start | bytes 3145732
  27.2 7.4 %collective-permute-start.8 = (bf16[4,128,256]{2,1,0:T(8,128)(2,1)S(1)}, bf16[4,128,256]{2,1,0:T(8,128)(2,1)S(1)}, u32[]{:S(2)}, u32[]{:S(2)}) collective-permute-start(bf16[4,128,256]{2,1,0:T(8,128)(2,1)S(1)} %get-tuple-element.58), channel_id=1, source_target_pairs={{0,4},{4,0},{8,12},{12,8},{16,20},{20,16},{24,28},{28,24},{1,5},{5... | collective-permute-start | bytes 786440 | tf_op jit(solution)/shard_map/ppermute | solution.py:74
  28.5 6.4 %collective-permute-start.9 = (bf16[4,128,256]{2,1,0:T(8,128)(2,1)S(1)}, bf16[4,128,256]{2,1,0:T(8,128)(2,1)S(1)}, u32[]{:S(2)}, u32[]{:S(2)}) collective-permute-start(bf16[4,128,256]{2,1,0:T(8,128)(2,1)S(1)} %get-tuple-element.60), channel_id=1, source_target_pairs={{0,8},{4,12},{8,0},{12,4},{16,24},{20,28},{24,16},{28,20},{1,9},{5... | collective-permute-start | bytes 786440 | tf_op jit(solution)/shard_map/ppermute | solution.py:74
  29.3 1.5 %collective-permute-start.13 = (bf16[352,256]{1,0:T(8,128)(2,1)S(1)}, bf16[352,256]{1,0:T(8,128)(2,1)S(1)}, u32[]{:S(2)}, u32[]{:S(2)}) collective-permute-start(bf16[352,256]{1,0:T(8,128)(2,1)S(1)} %get-tuple-element.69), channel_id=1, source_target_pairs={{0,1},{1,0},{2,3},{3,2},{4,5},{5,4},{6,7},{7,6},{8,9},{9,8},{10,11... | collective-permute-start | bytes 540680 | tf_op jit(solution)/shard_map/ppermute | solution.py:74
  29.4 1.7 %collective-permute-start.14 = (bf16[352,256]{1,0:T(8,128)(2,1)S(1)}, bf16[352,256]{1,0:T(8,128)(2,1)S(1)}, u32[]{:S(2)}, u32[]{:S(2)}) collective-permute-start(bf16[352,256]{1,0:T(8,128)(2,1)S(1)} %get-tuple-element.70), channel_id=1, source_target_pairs={{0,1},{1,0},{2,3},{3,2},{4,5},{5,4},{6,7},{7,6},{8,9},{9,8},{10,11... | collective-permute-start | bytes 540680 | tf_op jit(solution)/shard_map/ppermute | solution.py:74
  29.9 1.4 %collective-permute-start.15 = (bf16[352,256]{1,0:T(8,128)(2,1)S(1)}, bf16[352,256]{1,0:T(8,128)(2,1)S(1)}, u32[]{:S(2)}, u32[]{:S(2)}) collective-permute-start(bf16[352,256]{1,0:T(8,128)(2,1)S(1)} %get-tuple-element.71), channel_id=1, source_target_pairs={{0,1},{1,0},{2,3},{3,2},{4,5},{5,4},{6,7},{7,6},{8,9},{9,8},{10,11... | collective-permute-start | bytes 540680 | tf_op jit(solution)/shard_map/ppermute | solution.py:74
  31.4 11.4 %collective-permute-start.16 = (bf16[528,256]{1,0:T(8,128)(2,1)S(1)}, bf16[528,256]{1,0:T(8,128)(2,1)S(1)}, u32[]{:S(2)}, u32[]{:S(2)}) collective-permute-start(bf16[528,256]{1,0:T(8,128)(2,1)S(1)} %get-tuple-element.73), channel_id=1, source_target_pairs={{0,2},{1,3},{2,0},{3,1},{4,6},{5,7},{6,4},{7,5},{8,10},{9,11},{10,... | collective-permute-start | bytes 811016 | tf_op jit(solution)/shard_map/ppermute | solution.py:74
  35.0 5.0 %collective-permute-start.10 = (bf16[2,128,256]{2,1,0:T(8,128)(2,1)S(1)}, bf16[2,128,256]{2,1,0:T(8,128)(2,1)S(1)}, u32[]{:S(2)}, u32[]{:S(2)}) collective-permute-start(bf16[2,128,256]{2,1,0:T(8,128)(2,1)S(1)} %get-tuple-element.62), channel_id=1, source_target_pairs={{0,8},{4,12},{8,0},{12,4},{16,24},{20,28},{24,16},{28,20},{1,9},{5... | collective-permute-start | bytes 393224 | tf_op jit(solution)/shard_map/ppermute | solution.py:74
  35.7 5.1 %collective-permute-start.11 = (bf16[2,128,256]{2,1,0:T(8,128)(2,1)S(1)}, bf16[2,128,256]{2,1,0:T(8,128)(2,1)S(1)}, u32[]{:S(2)}, u32[]{:S(2)}) collective-permute-start(bf16[2,128,256]{2,1,0:T(8,128)(2,1)S(1)} %get-tuple-element.64), channel_id=1, source_target_pairs={{0,4},{4,0},{8,12},{12,8},{16,20},{20,16},{24,28},{28,24},{1,5},{5... | collective-permute-start | bytes 393224 | tf_op jit(solution)/shard_map/ppermute | solution.py:74
  40.9 8.1 %collective-permute-start.12 = (bf16[1,128,512]{2,1,0:T(8,128)(2,1)S(1)}, bf16[1,128,512]{2,1,0:T(8,128)(2,1)S(1)}, u32[]{:S(2)}, u32[]{:S(2)}) collective-permute-start(bf16[1,128,512]{2,1,0:T(8,128)(2,1)S(1)} %get-tuple-element.66), channel_id=1, source_target_pairs={{0,16},{4,20},{8,24},{12,28},{16,0},{20,4},{24,8},{28,12},{1,17},{... | collective-permute-start | bytes 393224 | tf_op jit(solution)/shard_map/ppermute | solution.py:74
  42.8 5.6 %collective-permute-start.17 = (f32[16,256]{1,0:T(8,128)S(1)}, f32[16,256]{1,0:T(8,128)S(1)}, u32[]{:S(2)}, u32[]{:S(2)}) collective-permute-start(f32[16,256]{1,0:T(8,128)S(1)} %get-tuple-element.75), channel_id=1, source_target_pairs={{4,0},{8,4},{12,8},{16,12},{20,16},{24,20},{28,24},{5,1},{9,5},{13... | collective-permute-start | bytes 49160 | tf_op jit(solution)/shard_map/ppermute | solution.py:568

commit v4 on v3

--- a/solution.py
+++ b/solution.py
@@ -433,8 +433,8 @@
     bits = members.bit_length() - 1
     layers = [layers[int(format(hop, f"0{bits}b")[::-1], 2)] for hop in range(members)]
 
-    fetched = [grad_out, state_out, log_decay, state_in, step_size, conv_pre, conv_taps]
-    payload, states, grad_here, output_here, decay_here, input_here, step_here, pre_here, taps_here = call(
+    fetched = [grad_out, state_out, log_decay, state_in, step_size, conv_pre, conv_taps, layer_input]
+    payload, states, grad_here, output_here, decay_here, input_here, step_here, pre_here, taps_here, layer_here = call(
         functools.partial(state_body, heads, len(fetched) - 3),
         [((state_width + PAD, width), BF16), ((count, state_width + ROW, width), F32)]
         + [(a.shape, a.dtype) for a in fetched],
@@ -475,7 +475,7 @@
     turned, ends = call(
         functools.partial(turn_body, members),
         [((members * features, length), BF16), ((members, PAD, features), BF16)],
-        layers,
+        [layer_here, *layers[1:]],
         moved=2 * members * features * length,
     )
     ends = lax.ppermute(ends, "context", [(i, i + 1) for i in range(spans_of - 1)])

time: 50.1 us -> 50.1 us (level)
  no operation moved by 1% of the time
where the time goes in v4:
time: 50.1 us; the launch traced here: 49.9 us
  starting transfers between devices  19.7 us (39%)
  waiting for transfers between devices  19.6 us (39%)
  Pallas kernels  9.05 us (18%)
  between operations  0.78 us (2%)
  local copies, waits for them, and re-layouts  0.66 us (1%)
    ppermute x16, waiting for transfers between devices, swap(): return lax.ppermute(value, axis, pairs)  15.3 us
    ppermute x16, starting transfers between devices, swap(): return lax.ppermute(value, axis, pairs)  15.2 us
    pallas_call x12, Pallas kernels, call(): pl.pallas_call(run, out_shape=[jax.ShapeDtypeStruct(shape, kind) for shap...  9.05 us
    ppermute x1, waiting for transfers between devices, local(): lax.ppermute(head, 'context', [(i + 1, i) for i in range(spans_of - 1)])  4.33 us
    ppermute x1, starting transfers between devices, local(): lax.ppermute(ends, 'context', [(i, i + 1) for i in range(spans_of - 1)])  3.31 us
    ppermute x1, starting transfers between devices, local(): lax.ppermute(head, 'context', [(i + 1, i) for i in range(spans_of - 1)])  1.29 us
  transfers between devices with their start and end apart: 18, of which 13 were waited for; matrix products, arithmetic and copies ran while one was open for 0% of the time, Pallas kernels for 14%

profile of v4, /device:TPU:0, one launch (start us, length us, event | category | flops | bytes accessed | tf_op | source)
XLA Modules:
  0.0 49.9 jit_solution(13124414294009325811)
XLA Ops:
  0.6 3.0 %collective-permute-start.1 = (bf16[512,256]{1,0:T(8,128)(2,1)}, bf16[512,256]{1,0:T(8,128)(2,1)S(1)}, u32[]{:S(2)}, u32[]{:S(2)}) collective-permute-start(bf16[512,256]{1,0:T(8,128)(2,1)} %refs_7_.1), channel_id=1, source_target_pairs={{0,2},{1,3},{2,0},{3,1},{4,6},{5,7},{6,4},{7,5},{8,10},{9,11},{10,... | collective-permute-start | bytes 786440 | tf_op jit(solution)/shard_map/ppermute | solution.py:74
  3.6 2.0 %shard_map.113 = (bf16[144,512]{1,0:T(8,128)(2,1)S(1)}, f32[2,136,512]{2,1,0:T(8,128)S(1)}, bf16[512,512]{1,0:T(8,128)(2,1)S(1)}, bf16[512,128]{1,0:T(8,128)(2,1...) custom-call(bf16[512,512]{1,0:T(8,128)(2,1)} %refs_0_.2, ...), custom_call_target="tpu_custom_call" | custom-call | flops 67108864 | bytes 524288 | tf_op jit(solution)/shard_map/pallas_call | solution.py:34
  5.7 1.6 %collective-permute-start.3 = (bf16[144,512]{1,0:T(8,128)(2,1)S(1)}, bf16[144,512]{1,0:T(8,128)(2,1)S(1)}, u32[]{:S(2)}, u32[]{:S(2)}) collective-permute-start(bf16[144,512]{1,0:T(8,128)(2,1)S(1)} %get-tuple-element.43.refs_0_), channel_id=1, source_target_pairs={{0,4},{4,0},{8,12},{12,8},{16,20},{20,16},{24,28},{28,24},{1,5},{5... | collective-permute-start | bytes 442376 | tf_op jit(solution)/shard_map/ppermute | solution.py:74
  7.3 1.6 %collective-permute-start.4 = (bf16[144,512]{1,0:T(8,128)(2,1)S(1)}, bf16[144,512]{1,0:T(8,128)(2,1)S(1)}, u32[]{:S(2)}, u32[]{:S(2)}) collective-permute-start(bf16[144,512]{1,0:T(8,128)(2,1)S(1)} %get-tuple-element.43.refs_0_), channel_id=1, source_target_pairs={{0,8},{4,12},{8,0},{12,4},{16,24},{20,28},{24,16},{28,20},{1,9},{5... | collective-permute-start | bytes 442376 | tf_op jit(solution)/shard_map/ppermute | solution.py:74
  9.2 0.9 %collective-permute-done.1.refs_2_ = bf16[512,256]{1,0:T(8,128)(2,1)S(1)} collective-permute-done((bf16[512,256]{1,0:T(8,128)(2,1)}, bf16[512,256]{1,0:T(8,128)(2,1)S(1)}, u32[]{:S(2)}, u32[]{:S(2)}) %collective-permute-start.1) | collective-permute-done | bytes 262176 | tf_op jit(solution)/shard_map/ppermute | solution.py:74
  10.8 2.7 %shard_map.115 = (f32[512,512]{1,0:T(8,128)S(1)}, f32[512,512]{1,0:T(8,128)S(1)}) custom-call(f32[8]{0:T(128)S(1)} %copy-done.1, bf16[512,128]{1,0:T(8,128)(2,1)S(1)} %get-tuple-element.44.refs_1_.refs_5_, bf16[512,128]{1,0:T(8,128)(2,1)S(1)} %get-tuple-element.45.refs_2_, bf16[512,512]{1,0:T(8,128)(2,1)S(1)} %get-tuple-element.46.refs_3_, ...), custom_call_target="tpu_custom_call" | custom-call | flops 34359738368 | bytes 3145728 | tf_op jit(solution)/shard_map/pallas_call | solution.py:34
  13.9 1.6 %collective-permute-done.5.refs_3_ = bf16[144,512]{1,0:T(8,128)(2,1)S(1)} collective-permute-done((bf16[144,512]{1,0:T(8,128)(2,1)S(1)}, bf16[144,512]{1,0:T(8,128)(2,1)S(1)}, u32[]{:S(2)}, u32[]{:S(2)}) %collective-permute-start.5) | collective-permute-done | bytes 147488 | tf_op jit(solution)/shard_map/ppermute | solution.py:74
  15.7 1.3 %collective-permute-start.6 = (bf16[128,512]{1,0:T(8,128)(2,1)S(1)}, bf16[128,512]{1,0:T(8,128)(2,1)S(1)}, u32[]{:S(2)}, u32[]{:S(2)}) collective-permute-start(bf16[128,512]{1,0:T(8,128)(2,1)S(1)} %get-tuple-element.51), channel_id=1, source_target_pairs={{16,0},{20,4},{24,8},{28,12},{17,1},{21,5},{25,9},{29,13},{18,2},{... | collective-permute-start | bytes 393224 | tf_op jit(solution)/shard_map/ppermute | solution.py:74
  17.4 3.3 %collective-permute-start.7 = (bf16[4,16,256]{2,1,0:T(8,128)(2,1)S(1)}, bf16[4,16,256]{2,1,0:T(8,128)(2,1)S(1)}, u32[]{:S(2)}, u32[]{:S(2)}) collective-permute-start(bf16[4,16,256]{2,1,0:T(8,128)(2,1)S(1)} %get-tuple-element.56), channel_id=1, source_target_pairs={{0,4},{4,8},{8,12},{12,16},{16,20},{20,24},{24,28},{1,5},{5,9},{9,... | collective-permute-start | bytes 98312 | tf_op jit(solution)/shard_map/ppermute | solution.py:481
  20.7 5.1 %collective-permute-done.6.refs_0_ = bf16[128,512]{1,0:T(8,128)(2,1)S(1)} collective-permute-done((bf16[128,512]{1,0:T(8,128)(2,1)S(1)}, bf16[128,512]{1,0:T(8,128)(2,1)S(1)}, u32[]{:S(2)}, u32[]{:S(2)}) %collective-permute-start.6) | collective-permute-done | bytes 131104 | tf_op jit(solution)/shard_map/ppermute | solution.py:74
  25.8 1.4 %shard_map.117 = (bf16[4,128,256]{2,1,0:T(8,128)(2,1)S(1)}, bf16[4,128,256]{2,1,0:T(8,128)(2,1)S(1)}, bf16[528,512]{1,0:T(8,128)(2,1)S(1)}, bf16[1024,16]{1,0:T(8,128)(2,1)S(1)}) custom-call(bf16[128,512]{1,0:T(8,128)(2,1)S(1)} %collective-permute-done.6.refs_0_, f32[136,512]{1,0:T(8,128)S(1)} %get-tuple-element.52.refs_1_, ...), custom_call_target="tpu_custom_call" | custom-call | flops 536870912 | bytes 4194304 | tf_op jit(solution)/shard_map/pallas_call | solution.py:34
  27.2 1.4 %collective-permute-start.8 = (bf16[4,128,256]{2,1,0:T(8,128)(2,1)S(1)}, bf16[4,128,256]{2,1,0:T(8,128)(2,1)S(1)}, u32[]{:S(2)}, u32[]{:S(2)}) collective-permute-start(bf16[4,128,256]{2,1,0:T(8,128)(2,1)S(1)} %get-tuple-element.60), channel_id=1, source_target_pairs={{0,4},{4,0},{8,12},{12,8},{16,20},{20,16},{24,28},{28,24},{1,5},{5... | collective-permute-start | bytes 786440 | tf_op jit(solution)/shard_map/ppermute | solution.py:74
  28.5 0.8 %shard_map.121 = (f32[528,256]{1,0:T(8,128)S(1)}, f32[528,256]{1,0:T(8,128)S(1)}, bf16[352,256]{1,0:T(8,128)(2,1)S(1)}, bf16[352,256]{1,0:T(8,128)(2,1)S(1)}, bf16[352,256]{1,0:T(8,128)(2,1)S(1)}) custom-call(bf16[528,512]{1,0:T(8,128)(2,1)S(1)} %get-tuple-element.58.refs_2_.refs_0_, bf16[1024,512]{1,0:T(8,128)(2,1)S(1)} %copy-done), custom_call_target="tpu_custom_call" | custom-call | flops 536870912 | bytes 2097152 | tf_op jit(solution)/shard_map/pallas_call | solution.py:34
  29.9 0.8 %collective-permute-done.13.refs_2_ = bf16[352,256]{1,0:T(8,128)(2,1)S(1)} collective-permute-done((bf16[352,256]{1,0:T(8,128)(2,1)S(1)}, bf16[352,256]{1,0:T(8,128)(2,1)S(1)}, u32[]{:S(2)}, u32[]{:S(2)}) %collective-permute-start.13) | collective-permute-done | bytes 180256 | tf_op jit(solution)/shard_map/ppermute | solution.py:74
  31.4 1.6 %collective-permute-start.16 = (bf16[528,256]{1,0:T(8,128)(2,1)S(1)}, bf16[528,256]{1,0:T(8,128)(2,1)S(1)}, u32[]{:S(2)}, u32[]{:S(2)}) collective-permute-start(bf16[528,256]{1,0:T(8,128)(2,1)S(1)} %get-tuple-element.75), channel_id=1, source_target_pairs={{0,2},{1,3},{2,0},{3,1},{4,6},{5,7},{6,4},{7,5},{8,10},{9,11},{10,... | collective-permute-start | bytes 811016 | tf_op jit(solution)/shard_map/ppermute | solution.py:74
  33.5 1.1 %collective-permute-done.8.refs_1_ = bf16[4,128,256]{2,1,0:T(8,128)(2,1)S(1)} collective-permute-done((bf16[4,128,256]{2,1,0:T(8,128)(2,1)S(1)}, bf16[4,128,256]{2,1,0:T(8,128)(2,1)S(1)}, u32[]{:S(2)}, u32[]{:S(2)}) %collective-permute-start.8) | collective-permute-done | bytes 262176 | tf_op jit(solution)/shard_map/ppermute | solution.py:74
  35.0 0.7 %collective-permute-start.10 = (bf16[2,128,256]{2,1,0:T(8,128)(2,1)S(1)}, bf16[2,128,256]{2,1,0:T(8,128)(2,1)S(1)}, u32[]{:S(2)}, u32[]{:S(2)}) collective-permute-start(bf16[2,128,256]{2,1,0:T(8,128)(2,1)S(1)} %get-tuple-element.64), channel_id=1, source_target_pairs={{0,8},{4,12},{8,0},{12,4},{16,24},{20,28},{24,16},{28,20},{1,9},{5... | collective-permute-start | bytes 393224 | tf_op jit(solution)/shard_map/ppermute | solution.py:74
  35.7 1.1 %collective-permute-start.11 = (bf16[2,128,256]{2,1,0:T(8,128)(2,1)S(1)}, bf16[2,128,256]{2,1,0:T(8,128)(2,1)S(1)}, u32[]{:S(2)}, u32[]{:S(2)}) collective-permute-start(bf16[2,128,256]{2,1,0:T(8,128)(2,1)S(1)} %get-tuple-element.66), channel_id=1, source_target_pairs={{0,4},{4,0},{8,12},{12,8},{16,20},{20,16},{24,28},{28,24},{1,5},{5... | collective-permute-start | bytes 393224 | tf_op jit(solution)/shard_map/ppermute | solution.py:74
  36.8 3.2 %collective-permute-done.10.refs_1_ = bf16[2,128,256]{2,1,0:T(8,128)(2,1)S(1)} collective-permute-done((bf16[2,128,256]{2,1,0:T(8,128)(2,1)S(1)}, bf16[2,128,256]{2,1,0:T(8,128)(2,1)S(1)}, u32[]{:S(2)}, u32[]{:S(2)}) %collective-permute-start.10) | collective-permute-done | bytes 131104 | tf_op jit(solution)/shard_map/ppermute | solution.py:74
  40.0 0.8 %collective-permute-done.11.refs_3_ = bf16[2,128,256]{2,1,0:T(8,128)(2,1)S(1)} collective-permute-done((bf16[2,128,256]{2,1,0:T(8,128)(2,1)S(1)}, bf16[2,128,256]{2,1,0:T(8,128)(2,1)S(1)}, u32[]{:S(2)}, u32[]{:S(2)}) %collective-permute-start.11) | collective-permute-done | bytes 131104 | tf_op jit(solution)/shard_map/ppermute | solution.py:74
  40.9 1.9 %collective-permute-start.12 = (bf16[1,128,512]{2,1,0:T(8,128)(2,1)S(1)}, bf16[1,128,512]{2,1,0:T(8,128)(2,1)S(1)}, u32[]{:S(2)}, u32[]{:S(2)}) collective-permute-start(bf16[1,128,512]{2,1,0:T(8,128)(2,1)S(1)} %get-tuple-element.68), channel_id=1, source_target_pairs={{0,16},{4,20},{8,24},{12,28},{16,0},{20,4},{24,8},{28,12},{1,17},{... | collective-permute-start | bytes 393224 | tf_op jit(solution)/shard_map/ppermute | solution.py:74
  42.9 1.3 %collective-permute-start.17 = (f32[16,256]{1,0:T(8,128)S(1)}, f32[16,256]{1,0:T(8,128)S(1)}, u32[]{:S(2)}, u32[]{:S(2)}) collective-permute-start(f32[16,256]{1,0:T(8,128)S(1)} %get-tuple-element.77), channel_id=1, source_target_pairs={{4,0},{8,4},{12,8},{16,12},{20,16},{24,20},{28,24},{5,1},{9,5},{13... | collective-permute-start | bytes 49160 | tf_op jit(solution)/shard_map/ppermute | solution.py:568
  44.2 4.3 %collective-permute-done.17.refs_3_ = f32[16,256]{1,0:T(8,128)S(1)} collective-permute-done((f32[16,256]{1,0:T(8,128)S(1)}, f32[16,256]{1,0:T(8,128)S(1)}, u32[]{:S(2)}, u32[]{:S(2)}) %collective-permute-start.17) | collective-permute-done | bytes 16416 | tf_op jit(solution)/shard_map/ppermute | solution.py:568
  49.0 0.8 %shard_map.124 = (f32[128,512]{1,0:T(8,128)}, bf16[512,256]{1,0:T(8,128)(2,1)}) custom-call(f32[1,128,512]{2,1,0:T(8,128)S(1)} %get-tuple-element.67.refs_0_, bf16[1,128,512]{2,1,0:T(8,128)(2,1)S(1)} %collective-permute-done.12.refs_1_, f32[512,256]{1,0:T(8,128)S(1)} %get-tuple-element.76.refs_2_, f32[16,256]{1,0:T(8,128)S(1)} %collective-permute-done.17.refs_3_), custom_call_target="tpu_custom_call" | custom-call | tf_op jit(solution)/shard_map/pallas_call | solution.py:34
  (30 shorter events, 4.8 us)
Async XLA Ops:
  0.6 8.6 %copy-start.2 = (bf16[512,256]{1,0:T(8,128)(2,1)S(1)}, bf16[512,256]{1,0:T(8,128)(2,1)}, u32[]{:S(2)}) copy-start(bf16[512,256]{1,0:T(8,128)(2,1)} %refs_7_.1) | copy-start | bytes 786436
  0.6 9.5 %collective-permute-start.1 = (bf16[512,256]{1,0:T(8,128)(2,1)}, bf16[512,256]{1,0:T(8,128)(2,1)S(1)}, u32[]{:S(2)}, u32[]{:S(2)}) collective-permute-start(bf16[512,256]{1,0:T(8,128)(2,1)} %refs_7_.1), channel_id=1, source_target_pairs={{0,2},{1,3},{2,0},{3,1},{4,6},{5,7},{6,4},{7,5},{8,10},{9,11},{10,... | collective-permute-start | bytes 786440 | tf_op jit(solution)/shard_map/ppermute | solution.py:74
  5.7 7.8 %collective-permute-start.3 = (bf16[144,512]{1,0:T(8,128)(2,1)S(1)}, bf16[144,512]{1,0:T(8,128)(2,1)S(1)}, u32[]{:S(2)}, u32[]{:S(2)}) collective-permute-start(bf16[144,512]{1,0:T(8,128)(2,1)S(1)} %get-tuple-element.43.refs_0_), channel_id=1, source_target_pairs={{0,4},{4,0},{8,12},{12,8},{16,20},{20,16},{24,28},{28,24},{1,5},{5... | collective-permute-start | bytes 442376 | tf_op jit(solution)/shard_map/ppermute | solution.py:74
  7.3 6.6 %collective-permute-start.4 = (bf16[144,512]{1,0:T(8,128)(2,1)S(1)}, bf16[144,512]{1,0:T(8,128)(2,1)S(1)}, u32[]{:S(2)}, u32[]{:S(2)}) collective-permute-start(bf16[144,512]{1,0:T(8,128)(2,1)S(1)} %get-tuple-element.43.refs_0_), channel_id=1, source_target_pairs={{0,8},{4,12},{8,0},{12,4},{16,24},{20,28},{24,16},{28,20},{1,9},{5... | collective-permute-start | bytes 442376 | tf_op jit(solution)/shard_map/ppermute | solution.py:74
  8.8 6.7 %collective-permute-start.5 = (bf16[144,512]{1,0:T(8,128)(2,1)S(1)}, bf16[144,512]{1,0:T(8,128)(2,1)S(1)}, u32[]{:S(2)}, u32[]{:S(2)}) collective-permute-start(bf16[144,512]{1,0:T(8,128)(2,1)S(1)} %get-tuple-element.43.refs_0_), channel_id=1, source_target_pairs={{0,12},{4,8},{8,4},{12,0},{16,28},{20,24},{24,20},{28,16},{1,13},{... | collective-permute-start | bytes 442376 | tf_op jit(solution)/shard_map/ppermute | solution.py:74
  9.2 7.8 %collective-permute-start = (bf16[512,256]{1,0:T(8,128)(2,1)S(1)}, bf16[512,256]{1,0:T(8,128)(2,1)S(1)}, u32[]{:S(2)}, u32[]{:S(2)}) collective-permute-start(bf16[512,256]{1,0:T(8,128)(2,1)S(1)} %copy-done.2), channel_id=1, source_target_pairs={{0,1},{1,0},{2,3},{3,2},{4,5},{5,4},{6,7},{7,6},{8,9},{9,8},{10,11... | collective-permute-start | bytes 786440 | tf_op jit(solution)/shard_map/ppermute | solution.py:74
  10.2 6.9 %collective-permute-start.2 = (bf16[512,256]{1,0:T(8,128)(2,1)S(1)}, bf16[512,256]{1,0:T(8,128)(2,1)S(1)}, u32[]{:S(2)}, u32[]{:S(2)}) collective-permute-start(bf16[512,256]{1,0:T(8,128)(2,1)S(1)} %collective-permute-done.1.refs_2_), channel_id=1, source_target_pairs={{0,1},{1,0},{2,3},{3,2},{4,5},{5,4},{6,7},{7,6},{8,9},{9,8},{10,11... | collective-permute-start | bytes 786440 | tf_op jit(solution)/shard_map/ppermute | solution.py:74
  10.2 0.7 %copy-start.1 = (f32[8]{0:T(128)S(1)}, f32[8]{0:T(128)}, u32[]{:S(2)}) copy-start(f32[8]{0:T(128)} %refs_0_.3) | copy-start | bytes 100
  15.7 10.0 %collective-permute-start.6 = (bf16[128,512]{1,0:T(8,128)(2,1)S(1)}, bf16[128,512]{1,0:T(8,128)(2,1)S(1)}, u32[]{:S(2)}, u32[]{:S(2)}) collective-permute-start(bf16[128,512]{1,0:T(8,128)(2,1)S(1)} %get-tuple-element.51), channel_id=1, source_target_pairs={{16,0},{20,4},{24,8},{28,12},{17,1},{21,5},{25,9},{29,13},{18,2},{... | collective-permute-start | bytes 393224 | tf_op jit(solution)/shard_map/ppermute | solution.py:74
  17.4 8.4 %collective-permute-start.7 = (bf16[4,16,256]{2,1,0:T(8,128)(2,1)S(1)}, bf16[4,16,256]{2,1,0:T(8,128)(2,1)S(1)}, u32[]{:S(2)}, u32[]{:S(2)}) collective-permute-start(bf16[4,16,256]{2,1,0:T(8,128)(2,1)S(1)} %get-tuple-element.56), channel_id=1, source_target_pairs={{0,4},{4,8},{8,12},{12,16},{16,20},{20,24},{24,28},{1,5},{5,9},{9,... | collective-permute-start | bytes 98312 | tf_op jit(solution)/shard_map/ppermute | solution.py:481
  25.7 2.8 %copy-start = (bf16[1024,512]{1,0:T(8,128)(2,1)S(1)}, bf16[1024,512]{1,0:T(8,128)(2,1)}, u32[]{:S(2)}) copy-start(bf16[1024,512]{1,0:T(8,128)(2,1)} %refs_1_.3) | copy-start | bytes 3145732
  27.2 7.4 %collective-permute-start.8 = (bf16[4,128,256]{2,1,0:T(8,128)(2,1)S(1)}, bf16[4,128,256]{2,1,0:T(8,128)(2,1)S(1)}, u32[]{:S(2)}, u32[]{:S(2)}) collective-permute-start(bf16[4,128,256]{2,1,0:T(8,128)(2,1)S(1)} %get-tuple-element.60), channel_id=1, source_target_pairs={{0,4},{4,0},{8,12},{12,8},{16,20},{20,16},{24,28},{28,24},{1,5},{5... | collective-permute-start | bytes 786440 | tf_op jit(solution)/shard_map/ppermute | solution.py:74
  28.5 6.4 %collective-permute-start.9 = (bf16[4,128,256]{2,1,0:T(8,128)(2,1)S(1)}, bf16[4,128,256]{2,1,0:T(8,128)(2,1)S(1)}, u32[]{:S(2)}, u32[]{:S(2)}) collective-permute-start(bf16[4,128,256]{2,1,0:T(8,128)(2,1)S(1)} %get-tuple-element.62), channel_id=1, source_target_pairs={{0,8},{4,12},{8,0},{12,4},{16,24},{20,28},{24,16},{28,20},{1,9},{5... | collective-permute-start | bytes 786440 | tf_op jit(solution)/shard_map/ppermute | solution.py:74
  29.3 1.5 %collective-permute-start.13 = (bf16[352,256]{1,0:T(8,128)(2,1)S(1)}, bf16[352,256]{1,0:T(8,128)(2,1)S(1)}, u32[]{:S(2)}, u32[]{:S(2)}) collective-permute-start(bf16[352,256]{1,0:T(8,128)(2,1)S(1)} %get-tuple-element.71), channel_id=1, source_target_pairs={{0,1},{1,0},{2,3},{3,2},{4,5},{5,4},{6,7},{7,6},{8,9},{9,8},{10,11... | collective-permute-start | bytes 540680 | tf_op jit(solution)/shard_map/ppermute | solution.py:74
  29.4 1.7 %collective-permute-start.14 = (bf16[352,256]{1,0:T(8,128)(2,1)S(1)}, bf16[352,256]{1,0:T(8,128)(2,1)S(1)}, u32[]{:S(2)}, u32[]{:S(2)}) collective-permute-start(bf16[352,256]{1,0:T(8,128)(2,1)S(1)} %get-tuple-element.72), channel_id=1, source_target_pairs={{0,1},{1,0},{2,3},{3,2},{4,5},{5,4},{6,7},{7,6},{8,9},{9,8},{10,11... | collective-permute-start | bytes 540680 | tf_op jit(solution)/shard_map/ppermute | solution.py:74
  29.9 1.4 %collective-permute-start.15 = (bf16[352,256]{1,0:T(8,128)(2,1)S(1)}, bf16[352,256]{1,0:T(8,128)(2,1)S(1)}, u32[]{:S(2)}, u32[]{:S(2)}) collective-permute-start(bf16[352,256]{1,0:T(8,128)(2,1)S(1)} %get-tuple-element.73), channel_id=1, source_target_pairs={{0,1},{1,0},{2,3},{3,2},{4,5},{5,4},{6,7},{7,6},{8,9},{9,8},{10,11... | collective-permute-start | bytes 540680 | tf_op jit(solution)/shard_map/ppermute | solution.py:74
  31.4 11.4 %collective-permute-start.16 = (bf16[528,256]{1,0:T(8,128)(2,1)S(1)}, bf16[528,256]{1,0:T(8,128)(2,1)S(1)}, u32[]{:S(2)}, u32[]{:S(2)}) collective-permute-start(bf16[528,256]{1,0:T(8,128)(2,1)S(1)} %get-tuple-element.75), channel_id=1, source_target_pairs={{0,2},{1,3},{2,0},{3,1},{4,6},{5,7},{6,4},{7,5},{8,10},{9,11},{10,... | collective-permute-start | bytes 811016 | tf_op jit(solution)/shard_map/ppermute | solution.py:74
  35.0 5.0 %collective-permute-start.10 = (bf16[2,128,256]{2,1,0:T(8,128)(2,1)S(1)}, bf16[2,128,256]{2,1,0:T(8,128)(2,1)S(1)}, u32[]{:S(2)}, u32[]{:S(2)}) collective-permute-start(bf16[2,128,256]{2,1,0:T(8,128)(2,1)S(1)} %get-tuple-element.64), channel_id=1, source_target_pairs={{0,8},{4,12},{8,0},{12,4},{16,24},{20,28},{24,16},{28,20},{1,9},{5... | collective-permute-start | bytes 393224 | tf_op jit(solution)/shard_map/ppermute | solution.py:74
  35.7 5.1 %collective-permute-start.11 = (bf16[2,128,256]{2,1,0:T(8,128)(2,1)S(1)}, bf16[2,128,256]{2,1,0:T(8,128)(2,1)S(1)}, u32[]{:S(2)}, u32[]{:S(2)}) collective-permute-start(bf16[2,128,256]{2,1,0:T(8,128)(2,1)S(1)} %get-tuple-element.66), channel_id=1, source_target_pairs={{0,4},{4,0},{8,12},{12,8},{16,20},{20,16},{24,28},{28,24},{1,5},{5... | collective-permute-start | bytes 393224 | tf_op jit(solution)/shard_map/ppermute | solution.py:74
  40.9 8.2 %collective-permute-start.12 = (bf16[1,128,512]{2,1,0:T(8,128)(2,1)S(1)}, bf16[1,128,512]{2,1,0:T(8,128)(2,1)S(1)}, u32[]{:S(2)}, u32[]{:S(2)}) collective-permute-start(bf16[1,128,512]{2,1,0:T(8,128)(2,1)S(1)} %get-tuple-element.68), channel_id=1, source_target_pairs={{0,16},{4,20},{8,24},{12,28},{16,0},{20,4},{24,8},{28,12},{1,17},{... | collective-permute-start | bytes 393224 | tf_op jit(solution)/shard_map/ppermute | solution.py:74
  42.9 5.6 %collective-permute-start.17 = (f32[16,256]{1,0:T(8,128)S(1)}, f32[16,256]{1,0:T(8,128)S(1)}, u32[]{:S(2)}, u32[]{:S(2)}) collective-permute-start(f32[16,256]{1,0:T(8,128)S(1)} %get-tuple-element.77), channel_id=1, source_target_pairs={{4,0},{8,4},{12,8},{16,12},{20,16},{24,20},{28,24},{5,1},{9,5},{13... | collective-permute-start | bytes 49160 | tf_op jit(solution)/shard_map/ppermute | solution.py:568

commit v5 on v3

--- a/solution.py
+++ b/solution.py
@@ -147,22 +147,25 @@
     rest, refs = refs[:others], refs[others:]
     payload_ref, states_ref, grad_ref, output_ref, decay_ref = refs[:5]
     rest_out, sems = refs[5:-1], refs[-1]
-    pairs = [(grad_hbm, grad_ref), (output_hbm, output_ref), (decay_hbm, decay_ref), *zip(rest, rest_out)]
+    blocks = [slice(k * BLOCK, (k + 1) * BLOCK) for k in range(grad_ref.shape[0] // BLOCK)]
+    pairs = [(decay_hbm, decay_ref), (output_hbm, output_ref)]
+    pairs += [(grad_hbm.at[rows, :], grad_ref.at[rows, :]) for rows in blocks]
+    pairs += list(zip(rest, rest_out))
     copies = [pltpu.make_async_copy(a, b, sems.at[index]) for index, (a, b) in enumerate(pairs)]
-    firsts, later = copies[:3], copies[3:]
-    for copy in firsts + later:
+    for copy in copies:
         copy.start()
-    for copy in firsts:
-        copy.wait()
+    copies[0].wait()
     width = grad_ref.shape[1]
     count = grad_ref.shape[0] // BLOCK
     spreader = spread_heads(heads, width)
-    states, spans = [], []
-    for k in range(count):
-        rows = slice(k * BLOCK, (k + 1) * BLOCK)
-        cumulative = running(decay_ref[:, rows])
-        spans.append(jnp.sum(spreader * cumulative[:, BLOCK - 1 :], axis=0, keepdims=True))
-        weighted = (grad_ref[rows, :].astype(F32) * widen(jnp.exp(cumulative), spreader)).astype(BF16)
+    sums = [running(decay_ref[:, rows]) for rows in blocks]
+    factors = [widen(jnp.exp(cumulative), spreader) for cumulative in sums]
+    spans = [jnp.sum(spreader * cumulative[:, BLOCK - 1 :], axis=0, keepdims=True) for cumulative in sums]
+    copies[1].wait()
+    states = []
+    for k, rows in enumerate(blocks):
+        copies[2 + k].wait()
+        weighted = (grad_ref[rows, :].astype(F32) * factors[k]).astype(BF16)
         states.append(dot(output_ref[rows, :], weighted, (0, 0)))
     total, span = states[-1], spans[-1]
     for k in reversed(range(count - 1)):
@@ -171,7 +174,7 @@
     pack_state(payload_ref, total, span)
     for k in range(count):
         keep_state(states_ref.at[k], states[k], spans[k])
-    for copy in later:
+    for copy in copies[2 + count :]:
         copy.wait()
 
 
@@ -440,7 +443,7 @@
         + [(a.shape, a.dtype) for a in fetched],
         fetched,
         hbm=len(fetched),
-        scratch=[pltpu.SemaphoreType.DMA((len(fetched),))],
+        scratch=[pltpu.SemaphoreType.DMA((len(fetched) - 1 + count,))],
         flops=2 * length * width * state_width,
         moved=2 * length * width,
         vmem=12,

time: 50.1 us -> 50 us (level)
  waiting for transfers between devices: 19.7 us -> 20.9 us
  starting transfers between devices: 19.7 us -> 18.7 us
    ppermute x16, waiting for transfers between devices: 15.3 us -> 16.6 us  [swap(): return lax.ppermute(value, axis, pairs)]
    ppermute x16, starting transfers between devices: 15.1 us -> 14.1 us  [swap(): return lax.ppermute(value, axis, pairs)]
  transfers between devices with their start and end apart: 18 -> 18, of which waited for: 13 -> 13; matrix products, arithmetic and copies ran while one was open for 0% -> 0% of each run, Pallas kernels for 14% -> 13%
where the time goes in v5:
time: 50 us; the launch traced here: 49.8 us
  waiting for transfers between devices  20.9 us (42%)
  starting transfers between devices  18.7 us (37%)
  Pallas kernels  8.78 us (18%)
  between operations  0.78 us (2%)
  local copies, waits for them, and re-layouts  0.66 us (1%)
    ppermute x16, waiting for transfers between devices, swap(): return lax.ppermute(value, axis, pairs)  16.6 us
    ppermute x16, starting transfers between devices, swap(): return lax.ppermute(value, axis, pairs)  14.1 us
    pallas_call x12, Pallas kernels, call(): pl.pallas_call(run, out_shape=[jax.ShapeDtypeStruct(shape, kind) for shap...  8.78 us
    ppermute x1, waiting for transfers between devices, local(): lax.ppermute(head, 'context', [(i + 1, i) for i in range(spans_of - 1)])  4.33 us
    ppermute x1, starting transfers between devices, local(): lax.ppermute(ends, 'context', [(i, i + 1) for i in range(spans_of - 1)])  3.31 us
    ppermute x1, starting transfers between devices, local(): lax.ppermute(head, 'context', [(i + 1, i) for i in range(spans_of - 1)])  1.29 us
  transfers between devices with their start and end apart: 18, of which 13 were waited for; matrix products, arithmetic and copies ran while one was open for 0% of the time, Pallas kernels for 13%

profile of v5, /device:TPU:0, one launch (start us, length us, event | category | flops | bytes accessed | tf_op | source)
XLA Modules:
  0.0 49.8 jit_solution(9394534558401894811)
XLA Ops:
  0.6 3.0 %collective-permute-start.1 = (bf16[512,256]{1,0:T(8,128)(2,1)}, bf16[512,256]{1,0:T(8,128)(2,1)S(1)}, u32[]{:S(2)}, u32[]{:S(2)}) collective-permute-start(bf16[512,256]{1,0:T(8,128)(2,1)} %refs_0_.3), channel_id=1, source_target_pairs={{0,2},{1,3},{2,0},{3,1},{4,6},{5,7},{6,4},{7,5},{8,10},{9,11},{10,... | collective-permute-start | bytes 786440 | tf_op jit(solution)/shard_map/ppermute | solution.py:74
  3.6 1.7 %shard_map.114 = (bf16[144,512]{1,0:T(8,128)(2,1)S(1)}, f32[2,136,512]{2,1,0:T(8,128)S(1)}, bf16[512,512]{1,0:T(8,128)(2,1)S(1)}, bf16[512,128]{1,0:T(8,128)(2,1...) custom-call(bf16[512,512]{1,0:T(8,128)(2,1)} %refs_0_.4, ...), custom_call_target="tpu_custom_call" | custom-call | flops 67108864 | bytes 524288 | tf_op jit(solution)/shard_map/pallas_call | solution.py:34
  5.4 1.6 %collective-permute-start.3 = (bf16[144,512]{1,0:T(8,128)(2,1)S(1)}, bf16[144,512]{1,0:T(8,128)(2,1)S(1)}, u32[]{:S(2)}, u32[]{:S(2)}) collective-permute-start(bf16[144,512]{1,0:T(8,128)(2,1)S(1)} %get-tuple-element.41.refs_0_), channel_id=1, source_target_pairs={{0,4},{4,0},{8,12},{12,8},{16,20},{20,16},{24,28},{28,24},{1,5},{5... | collective-permute-start | bytes 442376 | tf_op jit(solution)/shard_map/ppermute | solution.py:74
  7.0 1.6 %collective-permute-start.4 = (bf16[144,512]{1,0:T(8,128)(2,1)S(1)}, bf16[144,512]{1,0:T(8,128)(2,1)S(1)}, u32[]{:S(2)}, u32[]{:S(2)}) collective-permute-start(bf16[144,512]{1,0:T(8,128)(2,1)S(1)} %get-tuple-element.41.refs_0_), channel_id=1, source_target_pairs={{0,8},{4,12},{8,0},{12,4},{16,24},{20,28},{24,16},{28,20},{1,9},{5... | collective-permute-start | bytes 442376 | tf_op jit(solution)/shard_map/ppermute | solution.py:74
  8.9 1.2 %collective-permute-done.1.refs_2_ = bf16[512,256]{1,0:T(8,128)(2,1)S(1)} collective-permute-done((bf16[512,256]{1,0:T(8,128)(2,1)}, bf16[512,256]{1,0:T(8,128)(2,1)S(1)}, u32[]{:S(2)}, u32[]{:S(2)}) %collective-permute-start.1) | collective-permute-done | bytes 262176 | tf_op jit(solution)/shard_map/ppermute | solution.py:74
  10.2 0.7 %copy-done.2 = f32[8]{0:T(128)S(1)} copy-done((f32[8]{0:T(128)S(1)}, f32[8]{0:T(128)}, u32[]{:S(2)}) %copy-start.2) | copy-done | bytes 56
  10.8 2.7 %shard_map.115 = (f32[512,512]{1,0:T(8,128)S(1)}, f32[512,512]{1,0:T(8,128)S(1)}) custom-call(f32[8]{0:T(128)S(1)} %copy-done.2, bf16[512,128]{1,0:T(8,128)(2,1)S(1)} %get-tuple-element.42.refs_1_.refs_5_, bf16[512,128]{1,0:T(8,128)(2,1)S(1)} %get-tuple-element.43.refs_2_, bf16[512,512]{1,0:T(8,128)(2,1)S(1)} %get-tuple-element.44.refs_3_, ...), custom_call_target="tpu_custom_call" | custom-call | flops 34359738368 | bytes 3145728 | tf_op jit(solution)/shard_map/pallas_call | solution.py:34
  13.6 1.6 %collective-permute-done.5.refs_3_ = bf16[144,512]{1,0:T(8,128)(2,1)S(1)} collective-permute-done((bf16[144,512]{1,0:T(8,128)(2,1)S(1)}, bf16[144,512]{1,0:T(8,128)(2,1)S(1)}, u32[]{:S(2)}, u32[]{:S(2)}) %collective-permute-start.5) | collective-permute-done | bytes 147488 | tf_op jit(solution)/shard_map/ppermute | solution.py:74
  15.4 1.3 %collective-permute-start.6 = (bf16[128,512]{1,0:T(8,128)(2,1)S(1)}, bf16[128,512]{1,0:T(8,128)(2,1)S(1)}, u32[]{:S(2)}, u32[]{:S(2)}) collective-permute-start(bf16[128,512]{1,0:T(8,128)(2,1)S(1)} %get-tuple-element.49), channel_id=1, source_target_pairs={{16,0},{20,4},{24,8},{28,12},{17,1},{21,5},{25,9},{29,13},{18,2},{... | collective-permute-start | bytes 393224 | tf_op jit(solution)/shard_map/ppermute | solution.py:74
  17.1 3.3 %collective-permute-start.7 = (bf16[4,16,256]{2,1,0:T(8,128)(2,1)S(1)}, bf16[4,16,256]{2,1,0:T(8,128)(2,1)S(1)}, u32[]{:S(2)}, u32[]{:S(2)}) collective-permute-start(bf16[4,16,256]{2,1,0:T(8,128)(2,1)S(1)} %get-tuple-element.54), channel_id=1, source_target_pairs={{0,4},{4,8},{8,12},{12,16},{16,20},{20,24},{24,28},{1,5},{5,9},{9,... | collective-permute-start | bytes 98312 | tf_op jit(solution)/shard_map/ppermute | solution.py:484
  20.4 5.1 %collective-permute-done.6.refs_0_ = bf16[128,512]{1,0:T(8,128)(2,1)S(1)} collective-permute-done((bf16[128,512]{1,0:T(8,128)(2,1)S(1)}, bf16[128,512]{1,0:T(8,128)(2,1)S(1)}, u32[]{:S(2)}, u32[]{:S(2)}) %collective-permute-start.6) | collective-permute-done | bytes 131104 | tf_op jit(solution)/shard_map/ppermute | solution.py:74
  25.5 1.4 %shard_map.117 = (bf16[4,128,256]{2,1,0:T(8,128)(2,1)S(1)}, bf16[4,128,256]{2,1,0:T(8,128)(2,1)S(1)}, bf16[528,512]{1,0:T(8,128)(2,1)S(1)}, bf16[1024,16]{1,0:T(8,128)(2,1)S(1)}) custom-call(bf16[128,512]{1,0:T(8,128)(2,1)S(1)} %collective-permute-done.6.refs_0_, f32[136,512]{1,0:T(8,128)S(1)} %get-tuple-element.50.refs_1_, ...), custom_call_target="tpu_custom_call" | custom-call | flops 536870912 | bytes 4194304 | tf_op jit(solution)/shard_map/pallas_call | solution.py:34
  26.9 1.7 %collective-permute-start.8 = (bf16[4,128,256]{2,1,0:T(8,128)(2,1)S(1)}, bf16[4,128,256]{2,1,0:T(8,128)(2,1)S(1)}, u32[]{:S(2)}, u32[]{:S(2)}) collective-permute-start(bf16[4,128,256]{2,1,0:T(8,128)(2,1)S(1)} %get-tuple-element.58), channel_id=1, source_target_pairs={{0,4},{4,0},{8,12},{12,8},{16,20},{20,16},{24,28},{28,24},{1,5},{5... | collective-permute-start | bytes 786440 | tf_op jit(solution)/shard_map/ppermute | solution.py:74
  28.5 0.8 %shard_map.121 = (f32[528,256]{1,0:T(8,128)S(1)}, f32[528,256]{1,0:T(8,128)S(1)}, bf16[352,256]{1,0:T(8,128)(2,1)S(1)}, bf16[352,256]{1,0:T(8,128)(2,1)S(1)}, bf16[352,256]{1,0:T(8,128)(2,1)S(1)}) custom-call(bf16[528,512]{1,0:T(8,128)(2,1)S(1)} %get-tuple-element.56.refs_2_.refs_0_, bf16[1024,512]{1,0:T(8,128)(2,1)S(1)} %copy-done.1), custom_call_target="tpu_custom_call" | custom-call | flops 536870912 | bytes 2097152 | tf_op jit(solution)/shard_map/pallas_call | solution.py:34
  30.0 0.8 %collective-permute-done.13.refs_2_ = bf16[352,256]{1,0:T(8,128)(2,1)S(1)} collective-permute-done((bf16[352,256]{1,0:T(8,128)(2,1)S(1)}, bf16[352,256]{1,0:T(8,128)(2,1)S(1)}, u32[]{:S(2)}, u32[]{:S(2)}) %collective-permute-start.13) | collective-permute-done | bytes 180256 | tf_op jit(solution)/shard_map/ppermute | solution.py:74
  31.4 1.6 %collective-permute-start.16 = (bf16[528,256]{1,0:T(8,128)(2,1)S(1)}, bf16[528,256]{1,0:T(8,128)(2,1)S(1)}, u32[]{:S(2)}, u32[]{:S(2)}) collective-permute-start(bf16[528,256]{1,0:T(8,128)(2,1)S(1)} %get-tuple-element.73), channel_id=1, source_target_pairs={{0,2},{1,3},{2,0},{3,1},{4,6},{5,7},{6,4},{7,5},{8,10},{9,11},{10,... | collective-permute-start | bytes 811016 | tf_op jit(solution)/shard_map/ppermute | solution.py:74
  33.0 0.6 %shard_map.118 = (f32[4,128,256]{2,1,0:T(8,128)S(1)}, f32[4,128,256]{2,1,0:T(8,128)S(1)}) custom-call(bf16[1024,512]{1,0:T(8,128)(2,1)S(1)} %get-tuple-element.40.refs_8_.refs_0_, bf16[1024,16]{1,0:T(8,128)(2,1)S(1)} %get-tuple-element.55.refs_1_, bf16[528,512]{1,0:T(8,128)(2,1)S(1)} %get-tuple-element.56.refs_2_.refs_0_), custom_call_target="tpu_custom_call" | custom-call | flops 268435456 | bytes 2097152 | tf_op jit(solution)/shard_map/pallas_call | solution.py:34
  34.0 1.4 %collective-permute-done.9.refs_3_ = bf16[4,128,256]{2,1,0:T(8,128)(2,1)S(1)} collective-permute-done((bf16[4,128,256]{2,1,0:T(8,128)(2,1)S(1)}, bf16[4,128,256]{2,1,0:T(8,128)(2,1)S(1)}, u32[]{:S(2)}, u32[]{:S(2)}) %collective-permute-start.9) | collective-permute-done | bytes 262176 | tf_op jit(solution)/shard_map/ppermute | solution.py:74
  36.2 4.3 %collective-permute-done.10.refs_1_ = bf16[2,128,256]{2,1,0:T(8,128)(2,1)S(1)} collective-permute-done((bf16[2,128,256]{2,1,0:T(8,128)(2,1)S(1)}, bf16[2,128,256]{2,1,0:T(8,128)(2,1)S(1)}, u32[]{:S(2)}, u32[]{:S(2)}) %collective-permute-start.10) | collective-permute-done | bytes 131104 | tf_op jit(solution)/shard_map/ppermute | solution.py:74
  40.9 1.6 %collective-permute-start.12 = (bf16[1,128,512]{2,1,0:T(8,128)(2,1)S(1)}, bf16[1,128,512]{2,1,0:T(8,128)(2,1)S(1)}, u32[]{:S(2)}, u32[]{:S(2)}) collective-permute-start(bf16[1,128,512]{2,1,0:T(8,128)(2,1)S(1)} %get-tuple-element.66), channel_id=1, source_target_pairs={{0,16},{4,20},{8,24},{12,28},{16,0},{20,4},{24,8},{28,12},{1,17},{... | collective-permute-start | bytes 393224 | tf_op jit(solution)/shard_map/ppermute | solution.py:74
  42.6 1.3 %collective-permute-start.17 = (f32[16,256]{1,0:T(8,128)S(1)}, f32[16,256]{1,0:T(8,128)S(1)}, u32[]{:S(2)}, u32[]{:S(2)}) collective-permute-start(f32[16,256]{1,0:T(8,128)S(1)} %get-tuple-element.75), channel_id=1, source_target_pairs={{4,0},{8,4},{12,8},{16,12},{20,16},{24,20},{28,24},{5,1},{9,5},{13... | collective-permute-start | bytes 49160 | tf_op jit(solution)/shard_map/ppermute | solution.py:571
  43.9 4.3 %collective-permute-done.17.refs_3_ = f32[16,256]{1,0:T(8,128)S(1)} collective-permute-done((f32[16,256]{1,0:T(8,128)S(1)}, f32[16,256]{1,0:T(8,128)S(1)}, u32[]{:S(2)}, u32[]{:S(2)}) %collective-permute-start.17) | collective-permute-done | bytes 16416 | tf_op jit(solution)/shard_map/ppermute | solution.py:571
  48.2 0.8 %collective-permute-done.12.refs_1_ = bf16[1,128,512]{2,1,0:T(8,128)(2,1)S(1)} collective-permute-done((bf16[1,128,512]{2,1,0:T(8,128)(2,1)S(1)}, bf16[1,128,512]{2,1,0:T(8,128)(2,1)S(1)}, u32[]{:S(2)}, u32[]{:S(2)}) %collective-permute-start.12) | collective-permute-done | bytes 131104 | tf_op jit(solution)/shard_map/ppermute | solution.py:74
  49.0 0.8 %shard_map.124 = (f32[128,512]{1,0:T(8,128)}, bf16[512,256]{1,0:T(8,128)(2,1)}) custom-call(f32[1,128,512]{2,1,0:T(8,128)S(1)} %get-tuple-element.65.refs_0_, bf16[1,128,512]{2,1,0:T(8,128)(2,1)S(1)} %collective-permute-done.12.refs_1_, f32[512,256]{1,0:T(8,128)S(1)} %get-tuple-element.74.refs_2_, f32[16,256]{1,0:T(8,128)S(1)} %collective-permute-done.17.refs_3_), custom_call_target="tpu_custom_call" | custom-call | tf_op jit(solution)/shard_map/pallas_call | solution.py:34
  (30 shorter events, 4.1 us)
Async XLA Ops:
  0.6 8.3 %copy-start = (bf16[512,256]{1,0:T(8,128)(2,1)S(1)}, bf16[512,256]{1,0:T(8,128)(2,1)}, u32[]{:S(2)}) copy-start(bf16[512,256]{1,0:T(8,128)(2,1)} %refs_0_.3) | copy-start | bytes 786436
  0.6 9.5 %collective-permute-start.1 = (bf16[512,256]{1,0:T(8,128)(2,1)}, bf16[512,256]{1,0:T(8,128)(2,1)S(1)}, u32[]{:S(2)}, u32[]{:S(2)}) collective-permute-start(bf16[512,256]{1,0:T(8,128)(2,1)} %refs_0_.3), channel_id=1, source_target_pairs={{0,2},{1,3},{2,0},{3,1},{4,6},{5,7},{6,4},{7,5},{8,10},{9,11},{10,... | collective-permute-start | bytes 786440 | tf_op jit(solution)/shard_map/ppermute | solution.py:74
  5.4 8.1 %collective-permute-start.3 = (bf16[144,512]{1,0:T(8,128)(2,1)S(1)}, bf16[144,512]{1,0:T(8,128)(2,1)S(1)}, u32[]{:S(2)}, u32[]{:S(2)}) collective-permute-start(bf16[144,512]{1,0:T(8,128)(2,1)S(1)} %get-tuple-element.41.refs_0_), channel_id=1, source_target_pairs={{0,4},{4,0},{8,12},{12,8},{16,20},{20,16},{24,28},{28,24},{1,5},{5... | collective-permute-start | bytes 442376 | tf_op jit(solution)/shard_map/ppermute | solution.py:74
  7.0 6.6 %collective-permute-start.4 = (bf16[144,512]{1,0:T(8,128)(2,1)S(1)}, bf16[144,512]{1,0:T(8,128)(2,1)S(1)}, u32[]{:S(2)}, u32[]{:S(2)}) collective-permute-start(bf16[144,512]{1,0:T(8,128)(2,1)S(1)} %get-tuple-element.41.refs_0_), channel_id=1, source_target_pairs={{0,8},{4,12},{8,0},{12,4},{16,24},{20,28},{24,16},{28,20},{1,9},{5... | collective-permute-start | bytes 442376 | tf_op jit(solution)/shard_map/ppermute | solution.py:74
  8.5 6.7 %collective-permute-start.5 = (bf16[144,512]{1,0:T(8,128)(2,1)S(1)}, bf16[144,512]{1,0:T(8,128)(2,1)S(1)}, u32[]{:S(2)}, u32[]{:S(2)}) collective-permute-start(bf16[144,512]{1,0:T(8,128)(2,1)S(1)} %get-tuple-element.41.refs_0_), channel_id=1, source_target_pairs={{0,12},{4,8},{8,4},{12,0},{16,28},{20,24},{24,20},{28,16},{1,13},{... | collective-permute-start | bytes 442376 | tf_op jit(solution)/shard_map/ppermute | solution.py:74
  8.9 7.8 %collective-permute-start = (bf16[512,256]{1,0:T(8,128)(2,1)S(1)}, bf16[512,256]{1,0:T(8,128)(2,1)S(1)}, u32[]{:S(2)}, u32[]{:S(2)}) collective-permute-start(bf16[512,256]{1,0:T(8,128)(2,1)S(1)} %copy-done), channel_id=1, source_target_pairs={{0,1},{1,0},{2,3},{3,2},{4,5},{5,4},{6,7},{7,6},{8,9},{9,8},{10,11... | collective-permute-start | bytes 786440 | tf_op jit(solution)/shard_map/ppermute | solution.py:74
  10.2 6.6 %collective-permute-start.2 = (bf16[512,256]{1,0:T(8,128)(2,1)S(1)}, bf16[512,256]{1,0:T(8,128)(2,1)S(1)}, u32[]{:S(2)}, u32[]{:S(2)}) collective-permute-start(bf16[512,256]{1,0:T(8,128)(2,1)S(1)} %collective-permute-done.1.refs_2_), channel_id=1, source_target_pairs={{0,1},{1,0},{2,3},{3,2},{4,5},{5,4},{6,7},{7,6},{8,9},{9,8},{10,11... | collective-permute-start | bytes 786440 | tf_op jit(solution)/shard_map/ppermute | solution.py:74
  10.2 0.7 %copy-start.2 = (f32[8]{0:T(128)S(1)}, f32[8]{0:T(128)}, u32[]{:S(2)}) copy-start(f32[8]{0:T(128)} %refs_0_.5) | copy-start | bytes 100
  15.4 10.0 %collective-permute-start.6 = (bf16[128,512]{1,0:T(8,128)(2,1)S(1)}, bf16[128,512]{1,0:T(8,128)(2,1)S(1)}, u32[]{:S(2)}, u32[]{:S(2)}) collective-permute-start(bf16[128,512]{1,0:T(8,128)(2,1)S(1)} %get-tuple-element.49), channel_id=1, source_target_pairs={{16,0},{20,4},{24,8},{28,12},{17,1},{21,5},{25,9},{29,13},{18,2},{... | collective-permute-start | bytes 393224 | tf_op jit(solution)/shard_map/ppermute | solution.py:74
  17.1 8.4 %collective-permute-start.7 = (bf16[4,16,256]{2,1,0:T(8,128)(2,1)S(1)}, bf16[4,16,256]{2,1,0:T(8,128)(2,1)S(1)}, u32[]{:S(2)}, u32[]{:S(2)}) collective-permute-start(bf16[4,16,256]{2,1,0:T(8,128)(2,1)S(1)} %get-tuple-element.54), channel_id=1, source_target_pairs={{0,4},{4,8},{8,12},{12,16},{16,20},{20,24},{24,28},{1,5},{5,9},{9,... | collective-permute-start | bytes 98312 | tf_op jit(solution)/shard_map/ppermute | solution.py:484
  25.5 3.1 %copy-start.1 = (bf16[1024,512]{1,0:T(8,128)(2,1)S(1)}, bf16[1024,512]{1,0:T(8,128)(2,1)}, u32[]{:S(2)}) copy-start(bf16[1024,512]{1,0:T(8,128)(2,1)} %refs_1_.3) | copy-start | bytes 3145732
  26.9 7.2 %collective-permute-start.8 = (bf16[4,128,256]{2,1,0:T(8,128)(2,1)S(1)}, bf16[4,128,256]{2,1,0:T(8,128)(2,1)S(1)}, u32[]{:S(2)}, u32[]{:S(2)}) collective-permute-start(bf16[4,128,256]{2,1,0:T(8,128)(2,1)S(1)} %get-tuple-element.58), channel_id=1, source_target_pairs={{0,4},{4,0},{8,12},{12,8},{16,20},{20,16},{24,28},{28,24},{1,5},{5... | collective-permute-start | bytes 786440 | tf_op jit(solution)/shard_map/ppermute | solution.py:74
  28.5 6.9 %collective-permute-start.9 = (bf16[4,128,256]{2,1,0:T(8,128)(2,1)S(1)}, bf16[4,128,256]{2,1,0:T(8,128)(2,1)S(1)}, u32[]{:S(2)}, u32[]{:S(2)}) collective-permute-start(bf16[4,128,256]{2,1,0:T(8,128)(2,1)S(1)} %get-tuple-element.60), channel_id=1, source_target_pairs={{0,8},{4,12},{8,0},{12,4},{16,24},{20,28},{24,16},{28,20},{1,9},{5... | collective-permute-start | bytes 786440 | tf_op jit(solution)/shard_map/ppermute | solution.py:74
  29.3 1.5 %collective-permute-start.13 = (bf16[352,256]{1,0:T(8,128)(2,1)S(1)}, bf16[352,256]{1,0:T(8,128)(2,1)S(1)}, u32[]{:S(2)}, u32[]{:S(2)}) collective-permute-start(bf16[352,256]{1,0:T(8,128)(2,1)S(1)} %get-tuple-element.69), channel_id=1, source_target_pairs={{0,1},{1,0},{2,3},{3,2},{4,5},{5,4},{6,7},{7,6},{8,9},{9,8},{10,11... | collective-permute-start | bytes 540680 | tf_op jit(solution)/shard_map/ppermute | solution.py:74
  29.4 1.7 %collective-permute-start.14 = (bf16[352,256]{1,0:T(8,128)(2,1)S(1)}, bf16[352,256]{1,0:T(8,128)(2,1)S(1)}, u32[]{:S(2)}, u32[]{:S(2)}) collective-permute-start(bf16[352,256]{1,0:T(8,128)(2,1)S(1)} %get-tuple-element.70), channel_id=1, source_target_pairs={{0,1},{1,0},{2,3},{3,2},{4,5},{5,4},{6,7},{7,6},{8,9},{9,8},{10,11... | collective-permute-start | bytes 540680 | tf_op jit(solution)/shard_map/ppermute | solution.py:74
  29.9 1.4 %collective-permute-start.15 = (bf16[352,256]{1,0:T(8,128)(2,1)S(1)}, bf16[352,256]{1,0:T(8,128)(2,1)S(1)}, u32[]{:S(2)}, u32[]{:S(2)}) collective-permute-start(bf16[352,256]{1,0:T(8,128)(2,1)S(1)} %get-tuple-element.71), channel_id=1, source_target_pairs={{0,1},{1,0},{2,3},{3,2},{4,5},{5,4},{6,7},{7,6},{8,9},{9,8},{10,11... | collective-permute-start | bytes 540680 | tf_op jit(solution)/shard_map/ppermute | solution.py:74
  31.4 11.1 %collective-permute-start.16 = (bf16[528,256]{1,0:T(8,128)(2,1)S(1)}, bf16[528,256]{1,0:T(8,128)(2,1)S(1)}, u32[]{:S(2)}, u32[]{:S(2)}) collective-permute-start(bf16[528,256]{1,0:T(8,128)(2,1)S(1)} %get-tuple-element.73), channel_id=1, source_target_pairs={{0,2},{1,3},{2,0},{3,1},{4,6},{5,7},{6,4},{7,5},{8,10},{9,11},{10,... | collective-permute-start | bytes 811016 | tf_op jit(solution)/shard_map/ppermute | solution.py:74
  35.5 5.0 %collective-permute-start.10 = (bf16[2,128,256]{2,1,0:T(8,128)(2,1)S(1)}, bf16[2,128,256]{2,1,0:T(8,128)(2,1)S(1)}, u32[]{:S(2)}, u32[]{:S(2)}) collective-permute-start(bf16[2,128,256]{2,1,0:T(8,128)(2,1)S(1)} %get-tuple-element.62), channel_id=1, source_target_pairs={{0,8},{4,12},{8,0},{12,4},{16,24},{20,28},{24,16},{28,20},{1,9},{5... | collective-permute-start | bytes 393224 | tf_op jit(solution)/shard_map/ppermute | solution.py:74
  35.8 5.0 %collective-permute-start.11 = (bf16[2,128,256]{2,1,0:T(8,128)(2,1)S(1)}, bf16[2,128,256]{2,1,0:T(8,128)(2,1)S(1)}, u32[]{:S(2)}, u32[]{:S(2)}) collective-permute-start(bf16[2,128,256]{2,1,0:T(8,128)(2,1)S(1)} %get-tuple-element.64), channel_id=1, source_target_pairs={{0,4},{4,0},{8,12},{12,8},{16,20},{20,16},{24,28},{28,24},{1,5},{5... | collective-permute-start | bytes 393224 | tf_op jit(solution)/shard_map/ppermute | solution.py:74
  40.9 8.1 %collective-permute-start.12 = (bf16[1,128,512]{2,1,0:T(8,128)(2,1)S(1)}, bf16[1,128,512]{2,1,0:T(8,128)(2,1)S(1)}, u32[]{:S(2)}, u32[]{:S(2)}) collective-permute-start(bf16[1,128,512]{2,1,0:T(8,128)(2,1)S(1)} %get-tuple-element.66), channel_id=1, source_target_pairs={{0,16},{4,20},{8,24},{12,28},{16,0},{20,4},{24,8},{28,12},{1,17},{... | collective-permute-start | bytes 393224 | tf_op jit(solution)/shard_map/ppermute | solution.py:74
  42.6 5.6 %collective-permute-start.17 = (f32[16,256]{1,0:T(8,128)S(1)}, f32[16,256]{1,0:T(8,128)S(1)}, u32[]{:S(2)}, u32[]{:S(2)}) collective-permute-start(f32[16,256]{1,0:T(8,128)S(1)} %get-tuple-element.75), channel_id=1, source_target_pairs={{4,0},{8,4},{12,8},{16,12},{20,16},{24,20},{28,24},{5,1},{9,5},{13... | collective-permute-start | bytes 49160 | tf_op jit(solution)/shard_map/ppermute | solution.py:571
